TPU v7x, 256 devices: a whole 4x4x8 slice. The times are simulated.
256 devices in a mesh: space: 16 (over y, x_hi, core), period: 16 (over z, x_lo).
Axes of the slice: x: 4 (x_hi: 2, x_lo: 2; x = x_hi * 2 + x_lo), y: 4, z: 8, core: 2. Of those that a mesh axis runs over, the one named last changes fastest.
Arguments:
- source: float32 [2, 3, 32, 256, 128], P(None, None, 'space'), may hold values from -6 to 6
- conductivity: float32 [32, 256, 128], P('space'), may hold values from 0.1 to 2
- period_shift: float32 [16], P('period'), may hold values from 0.5 to 2
- site_cells: int32 [4, 2048], replicated, may hold values from 0 to 1048575, as said below
- site_weights: float32 [4, 2048], replicated, may hold values from 0.1 to 1
- observed: float32 [16, 4, 2048], P('period', None, 'space'), may hold values from -6 to 6
- data_weight: float32 [16, 4, 2048], P('period', None, 'space'), may hold values from 0.2 to 1
Outputs:
- predicted: float32 [16, 4, 2048], P('period', None, 'space')
- gradient: float32 [32, 256, 128], P('space', 'period')
Inputs may be any that keep to these rules, and one draw needn't show every extreme that they name: `site_cells`: station s names its cell (x, y, z) and the cells (x+1, y, z), (x, y+1, z), (x+1, y+1, z), with x+1 replaced by 32 - 1 past the grid's end; y < 255 and z < 128. Stations fall more often at low x, so slabs hold unequal numbers of station cells.
All inputs are finite; a program needn't handle non-finite values.
Results may differ from a plain program's by a relative error of at most 0.0001.
Values sent between devices are 32-bit elements; how exact they have to be, the bound alone decides.
No kernel may reach another device: no remote copies, remote signals or barrier semaphores. Data moves between devices by JAX's collectives and lax.ppermute only.
A program may use at most 128 MiB of HBM per device.

v0:
```python
import jax
import jax.numpy as jnp
from jax import lax
from jax.sharding import PartitionSpec as P

SWEEPS = 4


LOWER_BOUND = 0.05
UPPER_BOUND = 16.0


def padded_2(cells, sides, width):
    for axis, dim in sides:
        count = lax.axis_size(axis)
        ends = count - 1
        head = lax.slice_in_dim(cells, 0, width, axis=dim)
        tail = lax.slice_in_dim(cells, cells.shape[dim] - width, cells.shape[dim], axis=dim)
        cells = jnp.concatenate(
            [
                lax.ppermute(tail, axis, [(i, (i + 1) % count) for i in range(ends)]),
                cells,
                lax.ppermute(head, axis, [((i + 1) % count, i) for i in range(ends)]),
            ],
            axis=dim,
        )
    return cells


def chebyshev_steps(sweep_count):
    center = 0.5 * (UPPER_BOUND + LOWER_BOUND)
    spread = 0.5 * (UPPER_BOUND - LOWER_BOUND)
    step_sizes = []
    momenta = []
    step_size = 1.0 / center
    for number in range(sweep_count):
        if number == 0:
            momentum = 0.0
        elif number == 1:
            momentum = 0.5 * (spread * step_size) ** 2
        else:
            momentum = (0.5 * spread * step_size) ** 2
        if number > 0:
            step_size = 1.0 / (center - momentum / step_size)
        step_sizes.append(step_size)
        momenta.append(momentum)
    return (step_sizes, momenta)


def forward_diff(values, along):
    extent = values.shape[along]
    shifted = lax.slice_in_dim(values, 1, extent, axis=along)
    pad_width = [(0, 0)] * values.ndim
    pad_width[along] = (0, 1)
    return jnp.pad(shifted, pad_width) - values


def backward_diff(values, along):
    extent = values.shape[along]
    shifted = lax.slice_in_dim(values, 0, extent - 1, axis=along)
    pad_width = [(0, 0)] * values.ndim
    pad_width[along] = (1, 0)
    return values - jnp.pad(shifted, pad_width)


def curl_plus(components):
    east_part, north_part, down_part = components
    return (
        forward_diff(down_part, 2) - forward_diff(north_part, 3),
        forward_diff(east_part, 3) - forward_diff(down_part, 1),
        forward_diff(north_part, 1) - forward_diff(east_part, 2),
    )


def curl_minus(components):
    east_part, north_part, down_part = components
    return (
        backward_diff(down_part, 2) - backward_diff(north_part, 3),
        backward_diff(east_part, 3) - backward_diff(down_part, 1),
        backward_diff(north_part, 1) - backward_diff(east_part, 2),
    )


def plane_mask(slab_planes, margin):
    positions = (
        lax.axis_index("space") * slab_planes
        + jnp.arange(slab_planes + 2 * margin, dtype=jnp.int32)
        - margin
    )
    return ((positions >= 0) & (positions < slab_planes * lax.axis_size("space"))).astype(
        jnp.float32
    )[:, None, None]


def apply_padded(padded, mass_term, in_grid):
    components = (padded[:, 0], padded[:, 1], padded[:, 2])
    curled_once = tuple((part * in_grid for part in curl_plus(components)))
    curled = jnp.stack(curl_minus(curled_once), axis=1)
    return curled[:, :, 1:-1] + mass_term * padded[:, :, 1:-1]


def solve_single(right_side, mass_term, in_grid, tables):
    step_table, momentum_table = tables

    def one_sweep(number, carried):
        iterate, residual, direction = carried
        direction = residual + momentum_table[number] * direction
        padded = padded_2(direction, (("space", 2),), 1)
        applied = apply_padded(padded, mass_term, in_grid)
        return (
            iterate + step_table[number] * direction,
            residual - step_table[number] * applied,
            direction,
        )

    blank_field = jnp.zeros_like(right_side)
    return lax.fori_loop(0, SWEEPS, one_sweep, (blank_field, right_side, blank_field))[0]


def shards(source, conductivity, period_shift, site_cells, site_weights, observed, data_weight):
    slab_planes = conductivity.shape[0]
    grid_rows = conductivity.shape[1]
    grid_depth = conductivity.shape[2]
    shift_value = period_shift[0]
    step_sizes, momenta = chebyshev_steps(SWEEPS)
    tables = (jnp.asarray(step_sizes, jnp.float32), jnp.asarray(momenta, jnp.float32))
    inside = plane_mask(slab_planes, 1)
    mass_term = shift_value * conductivity

    def run_solver(right_side):
        return solve_single(right_side, mass_term, inside, tables)

    forward = run_solver(source)
    plane_size = grid_rows * grid_depth
    volume = slab_planes * plane_size
    local_plane = site_cells // plane_size - lax.axis_index("space") * slab_planes
    present = (local_plane >= 0) & (local_plane < slab_planes)
    local_index = jnp.where(present, local_plane * plane_size + site_cells % plane_size, 0)
    local_weights = jnp.where(present, site_weights, 0.0)
    flat_field = forward[:, :2].reshape(4, volume)
    partial_value = jnp.sum(flat_field[:, local_index] * local_weights[None], axis=1)
    predicted_own = lax.psum_scatter(partial_value, "space", scatter_dimension=1, tiled=True)
    adjoint_own = data_weight[0] * data_weight[0] * (predicted_own - observed[0])
    adjoint_data = lax.all_gather(adjoint_own, "space", axis=1, tiled=True)
    right_flat = (
        jnp.zeros((4, volume), jnp.float32)
        .at[:, local_index]
        .add(local_weights[None] * adjoint_data[:, None, :])
    )
    right_side = jnp.concatenate(
        [
            right_flat.reshape(2, 2, slab_planes, grid_rows, grid_depth),
            jnp.zeros((2, 1, slab_planes, grid_rows, grid_depth), jnp.float32),
        ],
        axis=1,
    )
    adjoint = run_solver(right_side)
    period_term = -shift_value * jnp.sum(adjoint * forward, axis=(0, 1))
    gradient = lax.psum_scatter(
        period_term, "period", scatter_dimension=1, tiled=True
    ) / lax.axis_size("period")
    return (predicted_own[None], gradient)


def solution(mesh):
    placed = (
        P(None, None, "space", None, None),
        P("space", None, None),
        P("period"),
        P(),
        P(),
        P("period", None, "space"),
        P("period", None, "space"),
    )
    return jax.shard_map(
        shards,
        mesh=mesh,
        in_specs=placed,
        out_specs=(P("period", None, "space"), P("space", "period", None)),
        check_vma=False,
    )
```

profile of v0, /device:TPU:2, one launch (start us, length us, event | category | flops | bytes accessed | tf_op | source)
XLA Modules:
  0.0 620.5 jit_solution(14733017292361166479)
XLA Ops:
  9.0 129.1 %while.42 = (s32[]{:T(128)}, f32[2,3,2,256,128]{4,3,2,1,0:T(8,128)}, f32[2,3,2,256,128]{4,3,2,1,0:T(8,128)S(1)}, f32[2,3,2,256,128]{4,3,2,1,0:T(8,128)S(1)}, f32...) while((s32[]{:T(128)}, ...), condition=%wide.region_1.2_spmd.clone.clone, body=%wide.region_0.1_spmd.sunk.clone.clone.sunk | while | flops 10223643 | bytes 79855880 | solution.py:117
  10.3 3.6 select_add_fusion.4
  14.9 2.7 collective-permute-start
  18.5 1.3 collective-permute-start.1
  19.8 1.2 constant_dynamic-update-slice_fusion.12
  21.2 2.8 collective-permute-done.1
  27.5 1.4 subtract_bitcast_fusion.8
  31.4 5.0 select_add_fusion.4
  37.5 18.1 %collective-permute-start = (f32[2,3,1,256,128]{4,3,2,0,1:T(8,128)}, f32[2,3,1,256,128]{4,3,2,0,1:T(8,128)}, u32[]{:S(2)}, u32[]{:S(2)}) collective-permute-start(f32[2,3,1,256,128]{4,3,2,0,1:T(8,128)} %copy.68), channel_id=1, source_target_pairs={{0,16},{16,32},{32,48},{48,64},{64,80},{80,96},{96,112},{112,128},... | collective-permute-start | bytes 2359304 | tf_op jit(solution)/shard_map/while/body/eval_jaxpr/ppermute | solution.py:21
  56.5 1.3 collective-permute-start.1
  57.8 1.2 constant_dynamic-update-slice_fusion.12
  59.2 1.9 collective-permute-done.1
  64.5 1.4 subtract_bitcast_fusion.8
  68.4 5.0 select_add_fusion.4
  74.5 16.4 %collective-permute-start = (f32[2,3,1,256,128]{4,3,2,0,1:T(8,128)}, f32[2,3,1,256,128]{4,3,2,0,1:T(8,128)}, u32[]{:S(2)}, u32[]{:S(2)}) collective-permute-start(f32[2,3,1,256,128]{4,3,2,0,1:T(8,128)} %copy.68), channel_id=1, source_target_pairs={{0,16},{16,32},{32,48},{48,64},{64,80},{80,96},{96,112},{112,128},... | collective-permute-start | bytes 2359304 | tf_op jit(solution)/shard_map/while/body/eval_jaxpr/ppermute | solution.py:21
  91.8 1.3 collective-permute-start.1
  93.1 1.2 constant_dynamic-update-slice_fusion.12
  94.5 1.9 collective-permute-done.1
  99.9 1.4 subtract_bitcast_fusion.8
  103.7 5.0 select_add_fusion.4
  109.8 16.7 %collective-permute-start = (f32[2,3,1,256,128]{4,3,2,0,1:T(8,128)}, f32[2,3,1,256,128]{4,3,2,0,1:T(8,128)}, u32[]{:S(2)}, u32[]{:S(2)}) collective-permute-start(f32[2,3,1,256,128]{4,3,2,0,1:T(8,128)} %copy.68), channel_id=1, source_target_pairs={{0,16},{16,32},{32,48},{48,64},{64,80},{80,96},{96,112},{112,128},... | collective-permute-start | bytes 2359304 | tf_op jit(solution)/shard_map/while/body/eval_jaxpr/ppermute | solution.py:21
  127.4 1.3 collective-permute-start.1
  128.7 1.2 constant_dynamic-update-slice_fusion.12
  130.1 1.9 collective-permute-done.1
  135.5 1.4 subtract_bitcast_fusion.8
  138.1 1.3 slice.363
  139.9 16.0 %copy.47 = f32[4,65536]{0,1:T(8,128)} copy(f32[4,65536]{1,0:T(4,128)S(1)} %reshape.17) | data formatting | bytes 2097152 | tf_op jit(solution)/shard_map/reshape | solution.py:140
  156.1 38.2 %gather_fusion = f32[8192,4]{1,0:T(8,128)} fusion(f32[4,65536]{0,1:T(8,128)} %copy.47, s32[8192]{0:T(1024)S(1)} %broadcast_clamp_fusion), kind=kCustom, calls=%fused_computation | custom fusion | bytes 294912 | tf_op jit(solution)/shard_map/gather | solution.py:141
  194.3 3.9 multiply_reduce_fusion
  198.3 88.4 %reduce-scatter.7.cloned.1.call-done = f32[128,4]{1,0:T(8,128)} async-done(((f32[2048,4]{1,0:T(8,128)}), f32[128,4]{1,0:T(8,128)}) %reduce-scatter.7.cloned.1.call-update) | async-done | bytes 2064
  287.7 22.3 %all_gather.3 = f32[4,2048]{1,0:T(4,128)S(1)} all-gather(f32[4,128]{1,0:T(4,128)S(1)} %fusion.19), channel_id=1, replica_groups=mesh['space'=16,'period'=16] {'space'}, dimensions={1}, use_global_device_ids=true | all-gather | bytes 34816 | tf_op jit(solution)/shard_map/all_gather | solution.py:144
  310.4 3.1 broadcast_multiply_fusion
  313.5 65.6 %scatter_custom_fusion = f32[4,65536]{0,1:T(8,128)} fusion(s32[8192]{0:T(1024)S(1)} %bitcast.147, f32[8192,4]{1,0:T(8,128)} %bitcast.143, f32[]{:T(128)} %constant.114.clone.1), kind=kCustom, calls=%fused_computation.46 | custom fusion | flops 32768 | bytes 1049088 | tf_op jit(solution)/shard_map/scatter-add | solution.py:148
  379.1 18.0 %copy.50 = f32[4,65536]{1,0:T(4,128)S(1)} copy(f32[4,65536]{0,1:T(8,128)} %scatter_custom_fusion) | data formatting | bytes 2097152 | tf_op jit(solution)/shard_map/scatter-add | solution.py:148
  397.3 126.9 %while.43 = (s32[]{:T(128)}, f32[2,3,2,256,128]{4,3,2,1,0:T(8,128)}, f32[2,3,2,256,128]{4,3,2,1,0:T(8,128)S(1)}, f32[2,3,2,256,128]{4,3,2,1,0:T(8,128)S(1)}, f32...) while((s32[]{:T(128)}, ...), condition=%wide.region_6.7_spmd.clone.clone, body=%wide.region_5.6_spmd.sunk.clone.clone.sunk | while | flops 10223643 | bytes 79855880 | solution.py:117
  398.5 3.7 select_add_fusion.5
  403.2 2.2 collective-permute-start.2
  406.4 1.3 collective-permute-start.3
  407.7 1.2 constant_dynamic-update-slice_fusion.15
  409.1 1.9 collective-permute-done.3
  414.4 1.4 subtract_bitcast_fusion.9
  415.9 1.3 fusion.31
  418.4 5.1 select_add_fusion.5
  424.5 16.8 %collective-permute-start.2 = (f32[2,3,1,256,128]{4,3,2,0,1:T(8,128)}, f32[2,3,1,256,128]{4,3,2,0,1:T(8,128)}, u32[]{:S(2)}, u32[]{:S(2)}) collective-permute-start(f32[2,3,1,256,128]{4,3,2,0,1:T(8,128)} %copy.71), channel_id=1, source_target_pairs={{0,16},{16,32},{32,48},{48,64},{64,80},{80,96},{96,112},{112,128},... | collective-permute-start | bytes 2359304 | tf_op jit(solution)/shard_map/while/body/eval_jaxpr/ppermute | solution.py:21
  442.3 1.3 collective-permute-start.3
  443.6 1.2 constant_dynamic-update-slice_fusion.15
  445.0 1.9 collective-permute-done.3
  450.3 1.4 subtract_bitcast_fusion.9
  451.8 1.3 fusion.31
  454.3 5.1 select_add_fusion.5
  460.4 16.0 %collective-permute-start.2 = (f32[2,3,1,256,128]{4,3,2,0,1:T(8,128)}, f32[2,3,1,256,128]{4,3,2,0,1:T(8,128)}, u32[]{:S(2)}, u32[]{:S(2)}) collective-permute-start(f32[2,3,1,256,128]{4,3,2,0,1:T(8,128)} %copy.71), channel_id=1, source_target_pairs={{0,16},{16,32},{32,48},{48,64},{64,80},{80,96},{96,112},{112,128},... | collective-permute-start | bytes 2359304 | tf_op jit(solution)/shard_map/while/body/eval_jaxpr/ppermute | solution.py:21
  477.4 1.3 collective-permute-start.3
  480.0 1.9 collective-permute-done.3
  485.4 1.4 subtract_bitcast_fusion.9
  486.8 1.3 fusion.31
  489.4 5.1 select_add_fusion.5
  495.5 17.0 %collective-permute-start.2 = (f32[2,3,1,256,128]{4,3,2,0,1:T(8,128)}, f32[2,3,1,256,128]{4,3,2,0,1:T(8,128)}, u32[]{:S(2)}, u32[]{:S(2)}) collective-permute-start(f32[2,3,1,256,128]{4,3,2,0,1:T(8,128)} %copy.71), channel_id=1, source_target_pairs={{0,16},{16,32},{32,48},{48,64},{64,80},{80,96},{96,112},{112,128},... | collective-permute-start | bytes 2359304 | tf_op jit(solution)/shard_map/while/body/eval_jaxpr/ppermute | solution.py:21
  513.4 1.3 collective-permute-start.3
  516.1 1.9 collective-permute-done.3
  521.4 1.4 subtract_bitcast_fusion.9
  522.9 1.3 fusion.31
  524.2 2.1 multiply_reduce_fusion.1
  527.0 85.3 %reduce-scatter.5.cloned.1.call-done = f32[2,16,128]{2,1,0:T(8,128)} async-done(((f32[2,256,128]{2,1,0:T(8,128)}), f32[2,16,128]{2,1,0:T(8,128)}) %reduce-scatter.5.cloned.1.call-update) | async-done | bytes 16400 | tf_op jit(solution)/shard_map/reduce_scatter | solution.py:159
  612.3 1.3 broadcast_multiply_fusion.3
  (194 shorter events, 65.7 us)
Async XLA Ops:
  7.2 1.8 copy-start.6
  7.2 1.8 copy-start.7
  7.2 1.8 copy-start
  7.2 279.5 %reduce-scatter.7.cloned.1.call-start = ((), (), s32[]{:S(2)}) async-start(), calls=%async_computation.3 | async-start | bytes 1114112
  14.9 4.9 collective-permute-start
  18.5 5.5 collective-permute-start.1
  37.5 20.3 %collective-permute-start = (f32[2,3,1,256,128]{4,3,2,0,1:T(8,128)}, f32[2,3,1,256,128]{4,3,2,0,1:T(8,128)}, u32[]{:S(2)}, u32[]{:S(2)}) collective-permute-start(f32[2,3,1,256,128]{4,3,2,0,1:T(8,128)} %copy.68), channel_id=1, source_target_pairs={{0,16},{16,32},{32,48},{48,64},{64,80},{80,96},{96,112},{112,128},... | collective-permute-start | bytes 2359304 | tf_op jit(solution)/shard_map/while/body/eval_jaxpr/ppermute | solution.py:21
  56.5 4.5 collective-permute-start.1
  74.5 18.6 %collective-permute-start = (f32[2,3,1,256,128]{4,3,2,0,1:T(8,128)}, f32[2,3,1,256,128]{4,3,2,0,1:T(8,128)}, u32[]{:S(2)}, u32[]{:S(2)}) collective-permute-start(f32[2,3,1,256,128]{4,3,2,0,1:T(8,128)} %copy.68), channel_id=1, source_target_pairs={{0,16},{16,32},{32,48},{48,64},{64,80},{80,96},{96,112},{112,128},... | collective-permute-start | bytes 2359304 | tf_op jit(solution)/shard_map/while/body/eval_jaxpr/ppermute | solution.py:21
  91.8 4.5 collective-permute-start.1
  109.8 18.9 %collective-permute-start = (f32[2,3,1,256,128]{4,3,2,0,1:T(8,128)}, f32[2,3,1,256,128]{4,3,2,0,1:T(8,128)}, u32[]{:S(2)}, u32[]{:S(2)}) collective-permute-start(f32[2,3,1,256,128]{4,3,2,0,1:T(8,128)} %copy.68), channel_id=1, source_target_pairs={{0,16},{16,32},{32,48},{48,64},{64,80},{80,96},{96,112},{112,128},... | collective-permute-start | bytes 2359304 | tf_op jit(solution)/shard_map/while/body/eval_jaxpr/ppermute | solution.py:21
  127.4 4.5 collective-permute-start.1
  139.9 16.0 %copy-start.1 = (s32[4,2048]{1,0:T(4,128)S(1)}, s32[4,2048]{1,0:T(4,128)}, u32[]{:S(2)}) copy-start(s32[4,2048]{1,0:T(4,128)} %param.16) | copy-start | bytes 98308
  139.9 16.1 %copy-start.2 = (f32[4,2048]{1,0:T(4,128)S(1)}, f32[4,2048]{1,0:T(4,128)}, u32[]{:S(2)}) copy-start(f32[4,2048]{1,0:T(4,128)} %param.17) | copy-start | bytes 98308
  194.3 93.3 %copy-start.4 = (f32[1,4,128]{2,1,0:T(4,128)S(1)}, f32[1,4,128]{2,1,0:T(4,128)}, u32[]{:S(2)}) copy-start(f32[1,4,128]{2,1,0:T(4,128)} %param.18) | copy-start | bytes 6148
  194.3 93.3 %copy-start.5 = (f32[1,4,128]{2,1,0:T(4,128)S(1)}, f32[1,4,128]{2,1,0:T(4,128)}, u32[]{:S(2)}) copy-start(f32[1,4,128]{2,1,0:T(4,128)} %param.19) | copy-start | bytes 6148
  198.2 414.1 %reduce-scatter.5.cloned.1.call-start = ((), (), s32[]{:S(2)}) async-start(), calls=%async_computation.2 | async-start | bytes 278528 | tf_op jit(solution)/shard_map/reduce_scatter | solution.py:159
  287.6 25.8 %copy-start.3 = (f32[4,128]{1,0:T(4,128)}, f32[4,128]{1,0:T(4,128)S(1)}, u32[]{:S(2)}) copy-start(f32[4,128]{1,0:T(4,128)S(1)} %copy.52) | copy-start | bytes 6148
  403.2 4.5 collective-permute-start.2
  406.4 4.5 collective-permute-start.3
  424.5 19.1 %collective-permute-start.2 = (f32[2,3,1,256,128]{4,3,2,0,1:T(8,128)}, f32[2,3,1,256,128]{4,3,2,0,1:T(8,128)}, u32[]{:S(2)}, u32[]{:S(2)}) collective-permute-start(f32[2,3,1,256,128]{4,3,2,0,1:T(8,128)} %copy.71), channel_id=1, source_target_pairs={{0,16},{16,32},{32,48},{48,64},{64,80},{80,96},{96,112},{112,128},... | collective-permute-start | bytes 2359304 | tf_op jit(solution)/shard_map/while/body/eval_jaxpr/ppermute | solution.py:21
  442.3 4.5 collective-permute-start.3
  460.4 18.2 %collective-permute-start.2 = (f32[2,3,1,256,128]{4,3,2,0,1:T(8,128)}, f32[2,3,1,256,128]{4,3,2,0,1:T(8,128)}, u32[]{:S(2)}, u32[]{:S(2)}) collective-permute-start(f32[2,3,1,256,128]{4,3,2,0,1:T(8,128)} %copy.71), channel_id=1, source_target_pairs={{0,16},{16,32},{32,48},{48,64},{64,80},{80,96},{96,112},{112,128},... | collective-permute-start | bytes 2359304 | tf_op jit(solution)/shard_map/while/body/eval_jaxpr/ppermute | solution.py:21
  477.4 4.5 collective-permute-start.3
  495.5 19.2 %collective-permute-start.2 = (f32[2,3,1,256,128]{4,3,2,0,1:T(8,128)}, f32[2,3,1,256,128]{4,3,2,0,1:T(8,128)}, u32[]{:S(2)}, u32[]{:S(2)}) collective-permute-start(f32[2,3,1,256,128]{4,3,2,0,1:T(8,128)} %copy.71), channel_id=1, source_target_pairs={{0,16},{16,32},{32,48},{48,64},{64,80},{80,96},{96,112},{112,128},... | collective-permute-start | bytes 2359304 | tf_op jit(solution)/shard_map/while/body/eval_jaxpr/ppermute | solution.py:21
  513.4 4.5 collective-permute-start.3
Sparse Core Ops, SparseCore 0:
  198.4 88.3 reduce-scatter.6
  527.1 85.1 reduce-scatter.4
where the time goes:
time: 625 us; the launch traced here: 620 us
  waiting for transfers between devices  190 us (30%)
  other arithmetic  145 us (23%)
  local copies, waits for them, and re-layouts  131 us (21%)
  starting transfers between devices  116 us (19%)
  blocking collectives  22.3 us (4%)
  between operations  15 us (2%)
    ppermute x8, starting transfers between devices, padded_2(): lax.ppermute(tail, axis, [(i, (i + 1) % count) for i in range(ends)])  106 us
    unnamed x3, waiting for transfers between devices  88.5 us
    reduce_scatter x1, waiting for transfers between devices, shards(): lax.psum_scatter(period_term, 'period', scatter_dimension=1, tiled=True)  85.3 us
    scatter-add x1, other arithmetic, shards(): right_flat = jnp.zeros((4, volume), jnp.float32).at[:, local_index].add(l...  65.6 us
    gather x1, local copies, waits for them, and re-layouts, shards(): flat_field[:, local_index] * local_weights[None]  38.2 us
    add x8, other arithmetic, one_sweep(): iterate + step_table[number] * direction  37.4 us
    while x32, local copies, waits for them, and re-layouts  25.9 us
    all_gather x1, blocking collectives, shards(): adjoint_data = lax.all_gather(adjoint_own, 'space', axis=1, tiled=True)  22.3 us
  transfers between devices with their start and end apart: 18, of which 10 were waited for; matrix products, arithmetic and copies ran while one was open for 3% of the time, Pallas kernels for 0%

commit v1 on v0

v1 whole, which is shorter than its diff:
```python
import jax
import jax.numpy as jnp
from jax import lax
from jax.experimental import pallas as pl
from jax.experimental.pallas import tpu as pltpu
from jax.sharding import PartitionSpec as P

SWEEPS = 4
LOWER_BOUND = 0.05
UPPER_BOUND = 16.0

CENTER = 1.25
HALO = SWEEPS - 1
PLANES = 2 + 2 * HALO
WINDOW = 32
DEGREE = SWEEPS
MOMENTS = 2 * SWEEPS - 1
LANES = 128
VMEM_LIMIT = 48 * 1024 * 1024


def chebyshev_steps(sweep_count):
    center = 0.5 * (UPPER_BOUND + LOWER_BOUND)
    spread = 0.5 * (UPPER_BOUND - LOWER_BOUND)
    step_sizes = []
    momenta = []
    step_size = 1.0 / center
    for number in range(sweep_count):
        if number == 0:
            momentum = 0.0
        elif number == 1:
            momentum = 0.5 * (spread * step_size) ** 2
        else:
            momentum = (0.5 * spread * step_size) ** 2
        if number > 0:
            step_size = 1.0 / (center - momentum / step_size)
        step_sizes.append(step_size)
        momenta.append(momentum)
    return (step_sizes, momenta)


STEP, MOMENTUM = chebyshev_steps(SWEEPS)


def place(grid_rows, own_rows):
    first_own = lax.axis_index("period") * own_rows
    first_row = jnp.clip(first_own - (WINDOW - own_rows) // 2, 0, grid_rows - WINDOW)
    return lax.axis_index("space") * 2 - HALO, pl.multiple_of(first_row, 8), first_own


def iota(shape, dim):
    return lax.broadcasted_iota(jnp.int32, shape, dim)


def parts_of(values):
    high = values.astype(jnp.bfloat16)
    rest = values - high.astype(jnp.float32)
    middle = rest.astype(jnp.bfloat16)
    low = (rest - middle.astype(jnp.float32)).astype(jnp.bfloat16)
    return high, middle, low


def dot_nt(left, right):
    return lax.dot_general(left, right, (((1,), (1,)), ((), ())), preferred_element_type=jnp.float32)


def dot_nn(left, right):
    return lax.dot_general(left, right, (((1,), (0,)), ((), ())), preferred_element_type=jnp.float32)


def next_z(v):
    return jnp.where(iota(v.shape, 1) == v.shape[1] - 1, 0.0, pltpu.roll(v, v.shape[1] - 1, 1))


def last_z(v):
    return jnp.where(iota(v.shape, 1) == 0, 0.0, pltpu.roll(v, 1, 1))


def next_y(v):
    return jnp.where(iota(v.shape, 0) == v.shape[0] - 1, 0.0, pltpu.roll(v, v.shape[0] - 1, 0))


def last_y(v):
    return jnp.where(iota(v.shape, 0) == 0, 0.0, pltpu.roll(v, 1, 0))


def curl_curl(get, first, last, first_plane, planes_in_grid):
    before = None
    here = get(first - 1)
    for plane in range(first - 1, last + 1):
        after = get(plane + 1)
        east, north, down = here
        c2 = next_z(east) - east
        if down is not None:
            c2 = c2 - (after[2] - down)
        c3 = (after[1] - north) - (next_y(east) - east)
        if plane < HALO and plane % 2 == 0:
            inside = jnp.where(first_plane + plane < 0, 0.0, 1.0)
            c2 = c2 * inside
            c3 = c3 * inside
        if plane >= first:
            c1 = north - next_z(north)
            if down is not None:
                c1 = c1 + (next_y(down) - down)
            a1 = (c3 - last_y(c3)) - (c2 - last_z(c2))
            a2 = (c1 - last_z(c1)) - (c3 - before[1])
            a3 = (c2 - before[0]) - (c1 - last_y(c1))
            if plane == HALO + 2:
                inside = jnp.where(first_plane + plane >= planes_in_grid, 0.0, 1.0)
                a1, a2, a3 = a1 * inside, a2 * inside, a3 * inside
            yield plane, here, (a1, a2, a3)
        before = (c2, c3)
        here = after


def pack_kernel(
    grid_rows, own_rows, source, conductivity, shift, observed, weight,
    slab, low, high, data, sems,
):
    _, first_row, _ = place(grid_rows, own_rows)
    rows = pl.ds(first_row, WINDOW)
    copies = []
    for plane in range(2):
        for pol in range(2):
            copies.append((source.at[pol, :, plane, rows, :], slab.at[plane, pl.ds(3 * pol, 3)]))
        copies.append((conductivity.at[plane, rows, :], slab.at[plane, 6]))
    for pol in range(2):
        copies.append((source.at[pol, :, 0, rows, :], low.at[pl.ds(3 * pol, 3)]))
        copies.append((source.at[pol, :, 1, rows, :], high.at[pl.ds(3 * pol, 3)]))
    started = [pltpu.make_async_copy(a, b, sems.at[i]) for i, (a, b) in enumerate(copies)]
    for copy in started:
        copy.start()
    for member in range(data.shape[0]):
        data[member, 0:4, :] = observed[0]
        data[member, 4:8, :] = weight[0]
        data[member, 8:16, :] = jnp.full((8, LANES), shift[0], jnp.float32)
    for copy in started:
        copy.wait()


def pack(source, conductivity, shift, observed, weight, members):
    grid_rows = source.shape[3]
    shape = jax.ShapeDtypeStruct
    hbm = pl.BlockSpec(memory_space=pl.ANY)
    vmem = pl.BlockSpec(memory_space=pltpu.VMEM)
    smem = pl.BlockSpec(memory_space=pltpu.SMEM)
    return pl.pallas_call(
        lambda *refs: pack_kernel(grid_rows, grid_rows // members, *refs),
        out_shape=(
            shape((2, 7, WINDOW, LANES), jnp.float32),
            shape((6, WINDOW, LANES), jnp.float32),
            shape((6, WINDOW, LANES), jnp.float32),
            shape((members, 16, LANES), jnp.float32),
        ),
        in_specs=[hbm, hbm, smem, vmem, vmem],
        out_specs=(hbm, hbm, hbm, vmem),
        scratch_shapes=[pltpu.SemaphoreType.DMA((10,))],
        name="pack",
    )(source, conductivity, shift, observed, weight)


def stations_kernel(grid_rows, own_rows, cells, weights, places, count, features, marks, staged):
    first_plane, first_row, first_own = place(grid_rows, own_rows)
    plane_size = grid_rows * LANES
    cell = cells[...]
    x = cell // plane_size - first_plane
    y = (cell // LANES) % grid_rows
    reached = (
        (x >= 0) & (x < PLANES)
        & (y >= first_own - HALO - 1) & (y < first_own + own_rows + HALO + 1)
    )
    row = jnp.where(reached, x * WINDOW + y - first_row, 0).astype(jnp.float32)
    weight = jnp.where(reached, weights[...], 0.0)
    present = jnp.max(jnp.where(reached, 1.0, 0.0), axis=0, keepdims=True)
    blocks = cell.shape[1] // LANES
    staged[...] = jnp.zeros(staged.shape, jnp.float32)
    staged[0:4, :] = row
    staged[4:8, :] = (cell % LANES).astype(jnp.float32)
    for number, part in enumerate(parts_of(weight)):
        staged[8 + 4 * number : 12 + 4 * number, :] = part.astype(jnp.float32)
    for block in range(blocks):
        marks[block : block + 1, :] = present[:, block * LANES : (block + 1) * LANES]
    mark = marks[...]
    square = (LANES, LANES)
    upto = jnp.where(iota(square, 0) <= iota(square, 1), 1.0, 0.0).astype(jnp.bfloat16)
    inner = dot_nn(mark.astype(jnp.bfloat16), upto)
    totals = dot_nn(mark.astype(jnp.bfloat16), jnp.ones(square, jnp.bfloat16))
    earlier = jnp.where(iota((blocks, blocks), 0) > iota((blocks, blocks), 1), 1.0, 0.0)
    offsets = dot_nn(earlier.astype(jnp.bfloat16), totals.astype(jnp.bfloat16))
    places[...] = jnp.where(mark > 0.0, inner + offsets - 1.0, -1.0).astype(jnp.int32)
    chunks = (jnp.sum(mark).astype(jnp.int32) + LANES - 1) // LANES
    count[0] = chunks

    def one_chunk(chunk, carry):
        gathered = jnp.zeros((staged.shape[0], LANES), jnp.float32)
        for block in range(blocks):
            feature = staged[:, block * LANES : (block + 1) * LANES].astype(jnp.bfloat16)
            gathered += dot_nt(feature, picks(places, block, chunk))
        features[chunk] = gathered
        return carry

    features[0] = jnp.zeros(features.shape[1:], jnp.float32)
    lax.fori_loop(0, chunks, one_chunk, 0)


def picks(places, block, chunk):
    wanted = places[block : block + 1, :] - chunk * LANES
    return jnp.where(iota((LANES, LANES), 0) == wanted, 1.0, 0.0).astype(jnp.bfloat16)


def stations(cells, weights, grid_rows, members):
    blocks = cells.shape[1] // LANES
    shape = jax.ShapeDtypeStruct
    vmem = pl.BlockSpec(memory_space=pltpu.VMEM)
    return pl.pallas_call(
        lambda *refs: stations_kernel(grid_rows, grid_rows // members, *refs),
        out_shape=(
            shape((blocks, LANES), jnp.int32),
            shape((1,), jnp.int32),
            shape((blocks, 32, LANES), jnp.float32),
        ),
        in_specs=[vmem, vmem],
        out_specs=(vmem, pl.BlockSpec(memory_space=pltpu.SMEM), vmem),
        scratch_shapes=[
            pltpu.VMEM((blocks, LANES), jnp.float32),
            pltpu.VMEM((32, cells.shape[1]), jnp.float32),
        ],
        compiler_params=pltpu.CompilerParams(vmem_limit_bytes=VMEM_LIMIT),
        cost_estimate=pl.CostEstimate(flops=10_000_000, bytes_accessed=200_000, transcendentals=0),
        name="stations",
    )(cells, weights)


def row_weights(feature, first, count):
    rows = (iota((count, LANES), 0) + first).astype(jnp.float32)
    total = jnp.zeros((count, LANES), jnp.float32)
    for q in range(4):
        weight = feature[8 + q : 9 + q] + feature[12 + q : 13 + q] + feature[16 + q : 17 + q]
        total += jnp.where(rows == feature[q : q + 1], weight, 0.0)
    return total


def depth_picks(feature):
    depth = iota((LANES, LANES), 0).astype(jnp.float32)
    return jnp.where(depth == feature[4:5], 1.0, 0.0).astype(jnp.bfloat16)


def forward_kernel(
    grid_rows, own_rows, grid_planes, slab, below, above, below2, above2, places, count, features,
    field, sent, mass, d1, d2,
):
    first_plane, _, _ = place(grid_rows, own_rows)

    def part(number, plane):
        if plane == 0:
            return below2[number]
        if plane <= 2:
            return below[plane - 1, number]
        if plane <= 4:
            return slab[plane - 3, number]
        if plane <= 6:
            return above[plane - 5, number]
        return above2[number]

    for plane in range(1, PLANES - 1):
        mass[plane - 1] = part(6, plane)

    for pol in range(2):
        def b(plane, pol=pol):
            return tuple(part(3 * pol + c, plane) for c in range(3))

        for plane, here, curled in curl_curl(b, 1, 6, first_plane, grid_planes):
            m = mass[plane - 1]
            for c in range(3):
                heavy = m * here[c]
                d1[0, pol, c, plane - 1] = (
                    (1.0 + MOMENTUM[1]) * here[c] - STEP[0] * (curled[c] + CENTER * heavy)
                )
                d1[1, pol, c, plane - 1] = -STEP[0] * heavy

        def level1(j, pol=pol):
            return lambda plane: tuple(d1[j, pol, c, plane - 1] for c in range(3))

        for j in range(2):
            for plane, here, curled in curl_curl(level1(j), 2, 5, first_plane, grid_planes):
                m = mass[plane - 1]
                for c in range(3):
                    mixed = CENTER * here[c]
                    if j == 1:
                        mixed = mixed + d1[0, pol, c, plane - 1]
                    value = (1.0 + MOMENTUM[2]) * here[c] - STEP[1] * (curled[c] + m * mixed)
                    if j == 0:
                        value = value - MOMENTUM[1] * part(3 * pol + c, plane)
                    d2[j, pol, c, plane - 2] = value
                    if j == 1:
                        d2[2, pol, c, plane - 2] = -STEP[1] * (m * here[c])

        def level2(j, pol=pol):
            return lambda plane: tuple(d2[j, pol, c, plane - 2] for c in range(3))

        for j in range(3):
            for plane, here, curled in curl_curl(level2(j), 3, 4, first_plane, grid_planes):
                m = mass[plane - 1]
                for c in range(3):
                    mixed = CENTER * here[c]
                    if j > 0:
                        mixed = mixed + d2[j - 1, pol, c, plane - 2]
                    last = (1.0 + MOMENTUM[3]) * here[c] - STEP[2] * (curled[c] + m * mixed)
                    value = STEP[2] * here[c]
                    if j < 2:
                        first = d1[j, pol, c, plane - 1]
                        last = last - MOMENTUM[2] * first
                        value = value + STEP[1] * first
                    if j == 0:
                        value = value + STEP[0] * part(3 * pol + c, plane)
                    field[j, pol, c, plane - 3] = value + STEP[3] * last
                    if j == 2:
                        field[3, pol, c, plane - 3] = -(STEP[3] * STEP[2]) * (m * here[c])

    members = sent.shape[0]
    sent[...] = jnp.zeros(sent.shape, jnp.float32)

    def one_chunk(chunk, carry):
        feature = features[chunk]
        weight = row_weights(feature, HALO * WINDOW, 2 * WINDOW)
        depth = depth_picks(feature)
        rows = []
        for j in range(DEGREE):
            for pol in range(2):
                for c in range(2):
                    values = field[j, pol, c].reshape(2 * WINDOW, LANES)
                    at_depth = sum(dot_nn(piece, depth) for piece in parts_of(values))
                    rows.append(jnp.sum(at_depth * weight, axis=0, keepdims=True))
        read = jnp.concatenate(rows, axis=0)
        pieces = jnp.concatenate(parts_of(read), axis=0)
        for block in range(members):
            spread = dot_nn(pieces, picks(places, block, chunk))
            sent[block] += spread[0:16] + spread[16:32] + spread[32:48]
        return carry

    lax.fori_loop(0, count[0], one_chunk, 0)


def forward_solve(slab, below, above, below2, above2, station_parts, grid_rows, members, grid_planes):
    shape = jax.ShapeDtypeStruct
    vmem = pl.BlockSpec(memory_space=pltpu.VMEM)
    smem = pl.BlockSpec(memory_space=pltpu.SMEM)
    blocks = station_parts[0].shape[0]
    return pl.pallas_call(
        lambda *refs: forward_kernel(grid_rows, grid_rows // members, grid_planes, *refs),
        out_shape=(
            shape((DEGREE, 2, 3, 2, WINDOW, LANES), jnp.float32),
            shape((blocks, 4 * DEGREE, LANES), jnp.float32),
            shape((PLANES - 2, WINDOW, LANES), jnp.float32),
        ),
        in_specs=[vmem] * 6 + [smem, vmem],
        out_specs=(vmem, vmem, vmem),
        scratch_shapes=[
            pltpu.VMEM((2, 2, 3, PLANES - 2, WINDOW, LANES), jnp.float32),
            pltpu.VMEM((3, 2, 3, PLANES - 4, WINDOW, LANES), jnp.float32),
        ],
        compiler_params=pltpu.CompilerParams(vmem_limit_bytes=VMEM_LIMIT),
        cost_estimate=pl.CostEstimate(flops=50_000_000, bytes_accessed=3_000_000, transcendentals=0),
        name="forward_solve",
    )(slab, below, above, below2, above2, *station_parts)


def residual_kernel(grid_rows, own_rows, read, data, cells, moments, owned, staged):
    members = data.shape[0]
    total = read[0]
    for member in range(1, read.shape[0]):
        total = total + read[member]
    coefficients = [total[4 * j : 4 * j + 4] for j in range(DEGREE)]
    first = pl.multiple_of(lax.axis_index("space") * LANES, LANES)
    cell = cells[:, pl.ds(first, LANES)]
    y = jnp.min((cell // LANES) % grid_rows, axis=0, keepdims=True)
    mine = (y // own_rows) == lax.axis_index("period")
    sums = [jnp.zeros((4, LANES), jnp.float32) for _ in range(MOMENTS)]
    for member in range(members):
        shift = data[member, 8:9, :]
        delta = shift - CENTER
        value = coefficients[DEGREE - 1]
        for j in range(DEGREE - 2, -1, -1):
            value = value * delta + coefficients[j]
        owned[member] = jnp.where(mine, value, 0.0)
        weight = data[member, 4:8, :]
        term = shift * (weight * weight * (value - data[member, 0:4, :]))
        for number in range(MOMENTS):
            sums[number] = sums[number] + term
            if number + 1 < MOMENTS:
                term = term * delta
    staged[...] = jnp.zeros(staged.shape, jnp.float32)
    for number in range(MOMENTS):
        staged[4 * number : 4 * number + 4, :] = sums[number]
    value = staged[...]
    for member in range(moments.shape[0]):
        moments[member] = value


def residuals(read, data, cells, grid_rows, members):
    shape = jax.ShapeDtypeStruct
    vmem = pl.BlockSpec(memory_space=pltpu.VMEM)
    return pl.pallas_call(
        lambda *refs: residual_kernel(grid_rows, grid_rows // members, *refs),
        out_shape=(
            shape((read.shape[0], 32, LANES), jnp.float32),
            shape((members, 4, LANES), jnp.float32),
        ),
        in_specs=[vmem, vmem, vmem],
        out_specs=(vmem, vmem),
        scratch_shapes=[pltpu.VMEM((32, LANES), jnp.float32)],
        name="residuals",
    )(read, data, cells)


def adjoint_kernel(
    grid_rows, own_rows, grid_planes, periods, moments, places, count, features, mass, field,
    gradient, d0, d1, d2, picked, total,
):
    first_plane, first_row, first_own = place(grid_rows, own_rows)
    blocks = moments.shape[0]
    window_rows = PLANES * WINDOW

    def add_chunk(chunk, fresh):
        feature = features[chunk]
        weight = row_weights(feature, 0, window_rows)
        depth = depth_picks(feature)
        depth = jnp.concatenate([depth, depth], axis=1)
        gathered = jnp.zeros((96, LANES), jnp.float32)
        for block in range(blocks):
            pieces = jnp.concatenate(parts_of(moments[block]), axis=0)
            gathered += dot_nt(pieces, picks(places, block, chunk))
        picked[...] = gathered[0:32] + gathered[32:64] + gathered[64:96]

        def one_field(number, carry):
            values = weight * picked[pl.ds(number, 1), :]
            high = values.astype(jnp.bfloat16)
            low = (values - high.astype(jnp.float32)).astype(jnp.bfloat16)
            placed = dot_nt(jnp.concatenate([high, low], axis=1), depth)
            if fresh:
                d0[number] = placed
            else:
                d0[number] += placed
            return carry

        lax.fori_loop(0, 4 * MOMENTS, one_field, 0)

    add_chunk(0, True)

    def one_chunk(chunk, carry):
        add_chunk(chunk, False)
        return carry

    lax.fori_loop(1, count[0], one_chunk, 0)

    def start(f, c, plane):
        return d0[2 * f + c, plane * WINDOW : (plane + 1) * WINDOW, :]

    def level_one(f, carry):
        def b(plane):
            return start(f, 0, plane), start(f, 1, plane), None

        for plane, here, curled in curl_curl(b, 1, 6, first_plane, grid_planes):
            m = mass[plane - 1]
            for c in range(2):
                mixed = CENTER * here[c] + start(f + 2, c, plane)
                d1[f, c, plane - 1] = (
                    (1.0 + MOMENTUM[1]) * here[c] - STEP[0] * (curled[c] + m * mixed)
                )
            d1[f, 2, plane - 1] = -STEP[0] * curled[2]
        return carry

    lax.fori_loop(0, 2 * (MOMENTS - 1), level_one, 0)

    def level_two(f, carry):
        def get(plane):
            return tuple(d1[f, c, plane - 1] for c in range(3))

        for plane, here, curled in curl_curl(get, 2, 5, first_plane, grid_planes):
            m = mass[plane - 1]
            for c in range(3):
                mixed = CENTER * here[c] + d1[f + 2, c, plane - 1]
                value = (1.0 + MOMENTUM[2]) * here[c] - STEP[1] * (curled[c] + m * mixed)
                if c < 2:
                    value = value - MOMENTUM[1] * start(f, c, plane)
                d2[f, c, plane - 2] = value
        return carry

    lax.fori_loop(0, 2 * (MOMENTS - 2), level_two, 0)

    total[...] = jnp.zeros(total.shape, jnp.float32)

    def level_three(f, carry):
        def get(plane):
            return tuple(d2[f, c, plane - 2] for c in range(3))

        for plane, here, curled in curl_curl(get, 3, 4, first_plane, grid_planes):
            m = mass[plane - 1]
            added = None
            for c in range(3):
                mixed = CENTER * here[c] + d2[f + 2, c, plane - 2]
                first = d1[f, c, plane - 1]
                last = (
                    (1.0 + MOMENTUM[3]) * here[c] - MOMENTUM[2] * first
                    - STEP[2] * (curled[c] + m * mixed)
                )
                value = STEP[1] * first + STEP[2] * here[c] + STEP[3] * last
                if c < 2:
                    value = value + STEP[0] * start(f, c, plane)
                term = value * field[f, c, plane - 3]
                added = term if added is None else added + term
            total[plane - 3] += added
        return carry

    lax.fori_loop(0, 2 * DEGREE, level_three, 0)
    offset = pl.multiple_of(first_own - first_row, 8)
    gradient[...] = total[:, pl.ds(offset, own_rows), :] * (-1.0 / periods)


def adjoint_solve(moments, station_parts, mass, field, grid_rows, members, grid_planes):
    vmem = pl.BlockSpec(memory_space=pltpu.VMEM)
    smem = pl.BlockSpec(memory_space=pltpu.SMEM)
    own_rows = grid_rows // members
    return pl.pallas_call(
        lambda *refs: adjoint_kernel(grid_rows, own_rows, grid_planes, members, *refs),
        out_shape=jax.ShapeDtypeStruct((2, own_rows, LANES), jnp.float32),
        in_specs=[vmem, vmem, smem, vmem, vmem, vmem],
        out_specs=vmem,
        scratch_shapes=[
            pltpu.VMEM((4 * MOMENTS, PLANES * WINDOW, LANES), jnp.float32),
            pltpu.VMEM((2 * (MOMENTS - 1), 3, PLANES - 2, WINDOW, LANES), jnp.float32),
            pltpu.VMEM((2 * (MOMENTS - 2), 3, PLANES - 4, WINDOW, LANES), jnp.float32),
            pltpu.VMEM((32, LANES), jnp.float32),
            pltpu.VMEM((2, WINDOW, LANES), jnp.float32),
        ],
        compiler_params=pltpu.CompilerParams(vmem_limit_bytes=VMEM_LIMIT),
        cost_estimate=pl.CostEstimate(flops=200_000_000, bytes_accessed=3_000_000, transcendentals=0),
        name="adjoint_solve",
    )(moments, *station_parts, mass, field.reshape(2 * DEGREE, 3, 2, WINDOW, LANES))


def shards(source, conductivity, period_shift, site_cells, site_weights, observed, data_weight):
    grid_rows = conductivity.shape[1]
    count = lax.axis_size("space")
    members = lax.axis_size("period")
    grid_planes = conductivity.shape[0] * count
    slab, low, high, data = pack(source, conductivity, period_shift, observed, data_weight, members)

    def moved(values, by):
        pairs = [(i, i + by) for i in range(count) if 0 <= i + by < count]
        return lax.ppermute(values, "space", pairs)

    below = moved(slab, 1)
    above = moved(slab, -1)
    below2 = moved(high, 2)
    above2 = moved(low, -2)
    data = lax.all_to_all(data, "period", 0, 0, tiled=True)
    station_parts = stations(site_cells, site_weights, grid_rows, members)
    field, sent, mass = forward_solve(
        slab, below, above, below2, above2, station_parts, grid_rows, members, grid_planes
    )
    read = lax.all_to_all(sent, "space", 0, 0, tiled=True)
    moments, owned = residuals(read, data, site_cells, grid_rows, members)
    moments = lax.all_to_all(moments, "space", 0, 0, tiled=True)
    owned = lax.all_to_all(owned, "period", 0, 0, tiled=True)
    gradient = adjoint_solve(moments, station_parts, mass, field, grid_rows, members, grid_planes)
    return jnp.sum(owned, axis=0, keepdims=True), gradient


def solution(mesh):
    placed = (
        P(None, None, "space", None, None),
        P("space", None, None),
        P("period"),
        P(),
        P(),
        P("period", None, "space"),
        P("period", None, "space"),
    )
    return jax.shard_map(
        shards,
        mesh=mesh,
        in_specs=placed,
        out_specs=(P("period", None, "space"), P("space", "period", None)),
        check_vma=False,
    )
```

time: 625 us -> 111 us (0.18)
  waiting for transfers between devices: 190 us -> 14.5 us
  other arithmetic: 145 us -> 0.6 us
  local copies, waits for them, and re-layouts: 131 us -> 0.95 us
  starting transfers between devices: 116 us -> 23.1 us
  Pallas kernels: 0 us -> 35.8 us
  between operations: 15 us -> 1.41 us
  blocking collectives: 22.3 us -> 32.4 us
    ppermute x16 -> x4, starting transfers between devices: 116 us -> 9.64 us  [moved(): return lax.ppermute(values, 'space', pairs)]
    unnamed x3 -> x0, waiting for transfers between devices: 88.5 us -> none
    reduce_scatter x1 -> x0, waiting for transfers between devices: 85.3 us -> none  [shards(): lax.psum_scatter(period_term, 'period', scatter_dimension=1, tiled=True)]
    scatter-add x1 -> x0, other arithmetic: 65.6 us -> none  [shards(): right_flat = jnp.zeros((4, volume), jnp.float32).at[:, local_index].add(l...]
    gather x1 -> x0, local copies, waits for them, and re-layouts: 38.2 us -> none  [shards(): flat_field[:, local_index] * local_weights[None]]
    add x8 -> x0, other arithmetic: 37.4 us -> none  [one_sweep(): iterate + step_table[number] * direction]
    pallas_call x0 -> x5, Pallas kernels: none -> 35.8 us  [the longest x1 15.4 us: pack(): pl.pallas_call(lambda *refs: pack_kernel(grid_rows, grid_rows // members,...]
    all_to_all x0 -> x2, blocking collectives: none -> 32.4 us  [the longest x1 16.8 us: shards(): read = lax.all_to_all(sent, 'space', 0, 0, tiled=True)]
  transfers between devices with their start and end apart: 18 -> 6, of which waited for: 10 -> 2; matrix products, arithmetic and copies ran while one was open for 3% -> 1% of each run, Pallas kernels for 0% -> 5%
where the time goes in v1:
time: 111 us; the launch traced here: 109 us
  Pallas kernels  35.8 us (32%)
  blocking collectives  32.4 us (29%)
  starting transfers between devices  23.1 us (21%)
  waiting for transfers between devices  14.5 us (13%)
  between operations  1.41 us (1%)
    all_to_all x1, blocking collectives, shards(): read = lax.all_to_all(sent, 'space', 0, 0, tiled=True)  16.8 us
    all_to_all x1, blocking collectives, shards(): owned = lax.all_to_all(owned, 'period', 0, 0, tiled=True)  15.6 us
    pallas_call x1, Pallas kernels, pack(): pl.pallas_call(lambda *refs: pack_kernel(grid_rows, grid_rows // members,...  15.4 us
    pallas_call x1, Pallas kernels, adjoint_solve(): pl.pallas_call(lambda *refs: adjoint_kernel(grid_rows, own_rows, grid_pla...  13.2 us
    all_to_all x1, starting transfers between devices, shards(): data = lax.all_to_all(data, 'period', 0, 0, tiled=True)  9.95 us
    ppermute x4, starting transfers between devices, moved(): return lax.ppermute(values, 'space', pairs)  9.64 us
    all_to_all x1, waiting for transfers between devices, shards(): moments = lax.all_to_all(moments, 'space', 0, 0, tiled=True)  8.91 us
    ppermute x4, waiting for transfers between devices, moved(): return lax.ppermute(values, 'space', pairs)  5.62 us
  transfers between devices with their start and end apart: 6, of which 2 were waited for; matrix products, arithmetic and copies ran while one was open for 1% of the time, Pallas kernels for 5%

profile of v1, /device:TPU:2, one launch (start us, length us, event | category | flops | bytes accessed | tf_op | source)
XLA Modules:
  0.0 108.8 jit_solution(5043799599385990000)
XLA Ops:
  0.6 0.0 copy-start.1
  0.6 0.0 copy-start.2
  1.3 15.4 %pack.1 = (f32[2,7,32,128]{3,2,1,0:T(8,128)}, f32[6,32,128]{2,1,0:T(8,128)}, f32[6,32,128]{2,1,0:T(8,128)}, f32[16,16,128]{2,1,0:T(8,128)}) custom-call(f32[2,3,2,256,128]{4,3,2,1,0:T(8,128)} %refs_0_.2, f32[2,256,128]{2,1,0:T(8,128)} %refs_1_.2, f32[1]{0:T(128)S(6)} %copy.9.refs_2_, f32[1,4,128]{2,1,0:T(4,128)} %refs_3_.1, f32[1,4,128]{2,1,0:T(4,128)} %refs_4_.1), custom_call_target="tpu_custom_call" | custom-call | tf_op jit(solution)/shard_map/pack/pallas_call | solution.py:147
  16.8 10.0 %all-to-all-start.1 = ((f32[16,16,128]{2,1,0:T(8,128)}), f32[16,16,128]{2,1,0:T(8,128)S(1)}, u32[]{:S(2)}, u32[]{:S(2)}) async-start(f32[16,16,128]{2,1,0:T(8,128)} %get-tuple-element.21), calls=%async_computation.1 | async-start | bytes 262144 | tf_op jit(solution)/shard_map/all_to_all | solution.py:557
  26.7 1.3 %collective-permute-start.1 = (f32[2,7,32,128]{3,2,1,0:T(8,128)}, f32[2,7,32,128]{3,2,1,0:T(8,128)S(1)}, u32[]{:S(2)}, u32[]{:S(2)}) collective-permute-start(f32[2,7,32,128]{3,2,1,0:T(8,128)} %get-tuple-element.14.refs_0_), channel_id=1, source_target_pairs={{16,0},{32,16},{48,32},{64,48},{80,64},{96,80},{112,96},{128,112},... | collective-permute-start | bytes 688136 | tf_op jit(solution)/shard_map/ppermute | solution.py:551
  28.0 3.0 %collective-permute-start = (f32[2,7,32,128]{3,2,1,0:T(8,128)}, f32[2,7,32,128]{3,2,1,0:T(8,128)S(1)}, u32[]{:S(2)}, u32[]{:S(2)}) collective-permute-start(f32[2,7,32,128]{3,2,1,0:T(8,128)} %get-tuple-element.14.refs_0_), channel_id=1, source_target_pairs={{0,16},{16,32},{32,48},{48,64},{64,80},{80,96},{96,112},{112,128},... | collective-permute-start | bytes 688136 | tf_op jit(solution)/shard_map/ppermute | solution.py:551
  31.0 4.0 %collective-permute-start.2 = (f32[6,32,128]{2,1,0:T(8,128)}, f32[6,32,128]{2,1,0:T(8,128)S(1)}, u32[]{:S(2)}, u32[]{:S(2)}) collective-permute-start(f32[6,32,128]{2,1,0:T(8,128)} %get-tuple-element.15), channel_id=1, source_target_pairs={{0,32},{16,48},{32,64},{48,80},{64,96},{80,112},{96,128},{112,144}... | collective-permute-start | bytes 294920 | tf_op jit(solution)/shard_map/ppermute | solution.py:551
  35.1 1.3 %collective-permute-start.3 = (f32[6,32,128]{2,1,0:T(8,128)}, f32[6,32,128]{2,1,0:T(8,128)S(1)}, u32[]{:S(2)}, u32[]{:S(2)}) collective-permute-start(f32[6,32,128]{2,1,0:T(8,128)} %get-tuple-element.16), channel_id=1, source_target_pairs={{32,0},{48,16},{64,32},{80,48},{96,64},{112,80},{128,96},{144,112}... | collective-permute-start | bytes 294920 | tf_op jit(solution)/shard_map/ppermute | solution.py:551
  36.4 0.0 copy-done.1
  36.4 0.0 copy-done.2
  36.4 1.3 %stations.1 = (s32[16,128]{1,0:T(8,128)S(1)}, s32[1]{0:T(128)}, f32[16,32,128]{2,1,0:T(8,128)S(1)}) custom-call(s32[4,2048]{1,0:T(4,128)S(1)} %copy-done.1, f32[4,2048]{1,0:T(4,128)S(1)} %copy-done.2), custom_call_target="tpu_custom_call" | custom-call | flops 10000000 | bytes 200000 | tf_op jit(solution)/shard_map/stations/pallas_call | solution.py:215
  37.7 0.0 collective-permute-done.2.refs_3_
  37.7 5.6 %collective-permute-done.3.refs_4_ = f32[6,32,128]{2,1,0:T(8,128)S(1)} collective-permute-done((f32[6,32,128]{2,1,0:T(8,128)}, f32[6,32,128]{2,1,0:T(8,128)S(1)}, u32[]{:S(2)}, u32[]{:S(2)}) %collective-permute-start.3) | collective-permute-done | bytes 98336 | tf_op jit(solution)/shard_map/ppermute | solution.py:551
  43.3 0.0 collective-permute-done.1.refs_2_
  43.3 0.0 collective-permute-done.refs_1_
  43.3 0.0 copy-start
  43.3 0.9 copy-done
  44.2 4.1 %forward_solve.1 = (f32[4,2,3,2,32,128]{5,4,3,2,1,0:T(8,128)S(1)}, f32[16,16,128]{2,1,0:T(8,128)S(1)}, f32[6,32,128]{2,1,0:T(8,128)S(1)}) custom-call(f32[2,7,32,128]{3,2,1,0:T(8,128)S(1)} %copy-done, f32[2,7,32,128]{3,2,1,0:T(8,128)S(1)} %collective-permute-done.refs_1_, f32[2,7,32,128]{3,2,1,0:T(8,128)S(1)} %collective-permute-done.1.refs_2_, ...), custom_call_target="tpu_custom_call" | custom-call | flops 50000000 | bytes 3000000 | tf_op jit(solution)/shard_map/forward_solve/pallas_call | solution.py:349
  48.4 0.0 all-to-all-done.1.refs_1_
  48.4 0.0 copy-start.3
  48.4 16.8 %all_to_all.20.refs_0_ = f32[16,16,128]{2,1,0:T(8,128)} all-to-all(f32[16,16,128]{2,1,0:T(8,128)S(1)} %get-tuple-element.20), channel_id=1, replica_groups=mesh['space'=16,'period'=16] {'space'}, dimensions={0} | all-to-all | bytes 262144 | tf_op jit(solution)/shard_map/all_to_all | solution.py:562
  65.2 0.0 copy-done.3
  65.2 1.8 %residuals.1 = (f32[16,32,128]{2,1,0:T(8,128)}, f32[16,4,128]{2,1,0:T(4,128)}) custom-call(f32[16,16,128]{2,1,0:T(8,128)} %all_to_all.20.refs_0_, f32[16,16,128]{2,1,0:T(8,128)} %copy-done.3, s32[4,2048]{1,0:T(4,128)} %refs_2_.2), custom_call_target="tpu_custom_call" | custom-call | tf_op jit(solution)/shard_map/residuals/pallas_call | solution.py:403
  67.0 15.6 %all_to_all.21 = f32[16,4,128]{2,1,0:T(4,128)S(1)} all-to-all(f32[16,4,128]{2,1,0:T(4,128)} %get-tuple-element.22), channel_id=1, replica_groups=mesh['space'=16,'period'=16] {'period'}, dimensions={0} | all-to-all | bytes 65536 | tf_op jit(solution)/shard_map/all_to_all | solution.py:565
  82.5 3.5 %all-to-all-start.3 = ((f32[16,32,128]{2,1,0:T(8,128)}), f32[16,32,128]{2,1,0:T(8,128)S(1)}, u32[]{:S(2)}, u32[]{:S(2)}) async-start(f32[16,32,128]{2,1,0:T(8,128)} %get-tuple-element.23), calls=%async_computation.3 | async-start | bytes 524288 | tf_op jit(solution)/shard_map/all_to_all | solution.py:564
  86.1 0.6 reduce_sum.9
  86.7 8.9 %all-to-all-done.3.refs_0_ = f32[16,32,128]{2,1,0:T(8,128)S(1)} async-done(((f32[16,32,128]{2,1,0:T(8,128)}), f32[16,32,128]{2,1,0:T(8,128)S(1)}, u32[]{:S(2)}, u32[]{:S(2)}) %all-to-all-start.3) | async-done | bytes 262176 | tf_op jit(solution)/shard_map/all_to_all | solution.py:564
  95.6 13.2 %adjoint_solve.1 = f32[2,16,128]{2,1,0:T(8,128)} custom-call(f32[16,32,128]{2,1,0:T(8,128)S(1)} %all-to-all-done.3.refs_0_, s32[16,128]{1,0:T(8,128)S(1)} %get-tuple-element.17.refs_5_.refs_1_, s32[1]{0:T(128)} %get-tuple-element.18.refs_6_.refs_2_, f32[16,32,128]{2,1,0:T(8,128)S(1)} %get-tuple-element.19.refs_7_.refs_3_, ...), custom_call_target="tpu_custom_call" | custom-call | flops 200000000 | bytes 3000000 | tf_op jit(solution)/shard_map/adjoint_solve/pallas_call | solution.py:524
Async XLA Ops:
  0.6 35.7 %copy-start.1 = (s32[4,2048]{1,0:T(4,128)S(1)}, s32[4,2048]{1,0:T(4,128)}, u32[]{:S(2)}) copy-start(s32[4,2048]{1,0:T(4,128)} %refs_2_.2) | copy-start | bytes 98308
  0.6 35.7 %copy-start.2 = (f32[4,2048]{1,0:T(4,128)S(1)}, f32[4,2048]{1,0:T(4,128)}, u32[]{:S(2)}) copy-start(f32[4,2048]{1,0:T(4,128)} %refs_1_.3) | copy-start | bytes 98308
  16.8 31.6 %all-to-all-start.1 = ((f32[16,16,128]{2,1,0:T(8,128)}), f32[16,16,128]{2,1,0:T(8,128)S(1)}, u32[]{:S(2)}, u32[]{:S(2)}) async-start(f32[16,16,128]{2,1,0:T(8,128)} %get-tuple-element.21), calls=%async_computation.1 | async-start | bytes 262144 | tf_op jit(solution)/shard_map/all_to_all | solution.py:557
  26.7 16.6 %collective-permute-start.1 = (f32[2,7,32,128]{3,2,1,0:T(8,128)}, f32[2,7,32,128]{3,2,1,0:T(8,128)S(1)}, u32[]{:S(2)}, u32[]{:S(2)}) collective-permute-start(f32[2,7,32,128]{3,2,1,0:T(8,128)} %get-tuple-element.14.refs_0_), channel_id=1, source_target_pairs={{16,0},{32,16},{48,32},{64,48},{80,64},{96,80},{112,96},{128,112},... | collective-permute-start | bytes 688136 | tf_op jit(solution)/shard_map/ppermute | solution.py:551
  28.0 15.3 %collective-permute-start = (f32[2,7,32,128]{3,2,1,0:T(8,128)}, f32[2,7,32,128]{3,2,1,0:T(8,128)S(1)}, u32[]{:S(2)}, u32[]{:S(2)}) collective-permute-start(f32[2,7,32,128]{3,2,1,0:T(8,128)} %get-tuple-element.14.refs_0_), channel_id=1, source_target_pairs={{0,16},{16,32},{32,48},{48,64},{64,80},{80,96},{96,112},{112,128},... | collective-permute-start | bytes 688136 | tf_op jit(solution)/shard_map/ppermute | solution.py:551
  31.0 6.6 %collective-permute-start.2 = (f32[6,32,128]{2,1,0:T(8,128)}, f32[6,32,128]{2,1,0:T(8,128)S(1)}, u32[]{:S(2)}, u32[]{:S(2)}) collective-permute-start(f32[6,32,128]{2,1,0:T(8,128)} %get-tuple-element.15), channel_id=1, source_target_pairs={{0,32},{16,48},{32,64},{48,80},{64,96},{80,112},{96,128},{112,144}... | collective-permute-start | bytes 294920 | tf_op jit(solution)/shard_map/ppermute | solution.py:551
  35.1 8.2 %collective-permute-start.3 = (f32[6,32,128]{2,1,0:T(8,128)}, f32[6,32,128]{2,1,0:T(8,128)S(1)}, u32[]{:S(2)}, u32[]{:S(2)}) collective-permute-start(f32[6,32,128]{2,1,0:T(8,128)} %get-tuple-element.16), channel_id=1, source_target_pairs={{32,0},{48,16},{64,32},{80,48},{96,64},{112,80},{128,96},{144,112}... | collective-permute-start | bytes 294920 | tf_op jit(solution)/shard_map/ppermute | solution.py:551
  43.3 0.9 copy-start
  48.4 16.8 %copy-start.3 = (f32[16,16,128]{2,1,0:T(8,128)}, f32[16,16,128]{2,1,0:T(8,128)S(1)}, u32[]{:S(2)}) copy-start(f32[16,16,128]{2,1,0:T(8,128)S(1)} %all-to-all-done.1.refs_1_) | copy-start | bytes 393220
  82.5 13.1 %all-to-all-start.3 = ((f32[16,32,128]{2,1,0:T(8,128)}), f32[16,32,128]{2,1,0:T(8,128)S(1)}, u32[]{:S(2)}, u32[]{:S(2)}) async-start(f32[16,32,128]{2,1,0:T(8,128)} %get-tuple-element.23), calls=%async_computation.3 | async-start | bytes 524288 | tf_op jit(solution)/shard_map/all_to_all | solution.py:564

commit v2 on v1

--- a/solution.py
+++ b/solution.py
@@ -42,10 +42,15 @@
 STEP, MOMENTUM = chebyshev_steps(SWEEPS)
 
 
+def window_row(member, grid_rows, own_rows):
+    first = member * own_rows - (WINDOW - own_rows) // 2
+    return pl.multiple_of(jnp.clip(first, 0, grid_rows - WINDOW), 8)
+
+
 def place(grid_rows, own_rows):
-    first_own = lax.axis_index("period") * own_rows
-    first_row = jnp.clip(first_own - (WINDOW - own_rows) // 2, 0, grid_rows - WINDOW)
-    return lax.axis_index("space") * 2 - HALO, pl.multiple_of(first_row, 8), first_own
+    member = lax.axis_index("period")
+    first_row = window_row(member, grid_rows, own_rows)
+    return lax.axis_index("space") * 2 - HALO, first_row, member * own_rows
 
 
 def iota(shape, dim):
@@ -115,18 +120,26 @@
 
 def pack_kernel(
     grid_rows, own_rows, source, conductivity, shift, observed, weight,
-    slab, low, high, data, sems,
+    slab, up, down, up2, down2, data, sems,
 ):
-    _, first_row, _ = place(grid_rows, own_rows)
-    rows = pl.ds(first_row, WINDOW)
+    member = lax.axis_index("period")
+    even = lax.axis_index("space") % 2 == 0
+    mine = window_row(member, grid_rows, own_rows)
+    beside = window_row(member + 1 - 2 * (member % 2), grid_rows, own_rows)
     copies = []
-    for plane in range(2):
+    for target, row in (
+        (slab, mine),
+        (up, jnp.where(even, mine, beside)),
+        (down, jnp.where(even, beside, mine)),
+    ):
+        rows = pl.ds(pl.multiple_of(row, 8), WINDOW)
         for pol in range(2):
-            copies.append((source.at[pol, :, plane, rows, :], slab.at[plane, pl.ds(3 * pol, 3)]))
-        copies.append((conductivity.at[plane, rows, :], slab.at[plane, 6]))
+            copies.append((source.at[pol, :, :, rows, :], target.at[pl.ds(3 * pol, 3)]))
+        copies.append((conductivity.at[:, rows, :], target.at[6]))
+    rows = pl.ds(beside, WINDOW)
     for pol in range(2):
-        copies.append((source.at[pol, :, 0, rows, :], low.at[pl.ds(3 * pol, 3)]))
-        copies.append((source.at[pol, :, 1, rows, :], high.at[pl.ds(3 * pol, 3)]))
+        copies.append((source.at[pol, :, 1, rows, :], up2.at[pl.ds(3 * pol, 3)]))
+        copies.append((source.at[pol, :, 0, rows, :], down2.at[pl.ds(3 * pol, 3)]))
     started = [pltpu.make_async_copy(a, b, sems.at[i]) for i, (a, b) in enumerate(copies)]
     for copy in started:
         copy.start()
@@ -146,15 +159,12 @@
     smem = pl.BlockSpec(memory_space=pltpu.SMEM)
     return pl.pallas_call(
         lambda *refs: pack_kernel(grid_rows, grid_rows // members, *refs),
-        out_shape=(
-            shape((2, 7, WINDOW, LANES), jnp.float32),
-            shape((6, WINDOW, LANES), jnp.float32),
-            shape((6, WINDOW, LANES), jnp.float32),
-            shape((members, 16, LANES), jnp.float32),
-        ),
+        out_shape=(shape((7, 2, WINDOW, LANES), jnp.float32),) * 3
+        + (shape((6, WINDOW, LANES), jnp.float32),) * 2
+        + (shape((members, 16, LANES), jnp.float32),),
         in_specs=[hbm, hbm, smem, vmem, vmem],
-        out_specs=(hbm, hbm, hbm, vmem),
-        scratch_shapes=[pltpu.SemaphoreType.DMA((10,))],
+        out_specs=(vmem,) * 6,
+        scratch_shapes=[pltpu.SemaphoreType.DMA((13,))],
         name="pack",
     )(source, conductivity, shift, observed, weight)
 
@@ -255,11 +265,11 @@
         if plane == 0:
             return below2[number]
         if plane <= 2:
-            return below[plane - 1, number]
+            return below[number, plane - 1]
         if plane <= 4:
-            return slab[plane - 3, number]
+            return slab[number, plane - 3]
         if plane <= 6:
-            return above[plane - 5, number]
+            return above[number, plane - 5]
         return above2[number]
 
     for plane in range(1, PLANES - 1):
@@ -544,16 +554,22 @@
     count = lax.axis_size("space")
     members = lax.axis_size("period")
     grid_planes = conductivity.shape[0] * count
-    slab, low, high, data = pack(source, conductivity, period_shift, observed, data_weight, members)
+    slab, up, down, up2, down2, data = pack(
+        source, conductivity, period_shift, observed, data_weight, members
+    )
 
     def moved(values, by):
-        pairs = [(i, i + by) for i in range(count) if 0 <= i + by < count]
-        return lax.ppermute(values, "space", pairs)
-
-    below = moved(slab, 1)
-    above = moved(slab, -1)
-    below2 = moved(high, 2)
-    above2 = moved(low, -2)
+        pairs = []
+        for i in range(count):
+            if 0 <= i + by < count:
+                flip = 0 if (i + by) // 2 == i // 2 else 1
+                pairs += [(i * members + t, (i + by) * members + (t ^ flip)) for t in range(members)]
+        return lax.ppermute(values, ("space", "period"), pairs)
+
+    below = moved(up, 1)
+    above = moved(down, -1)
+    below2 = moved(up2, 2)
+    above2 = moved(down2, -2)
     data = lax.all_to_all(data, "period", 0, 0, tiled=True)
     station_parts = stations(site_cells, site_weights, grid_rows, members)
     field, sent, mass = forward_solve(
@@ -562,6 +578,7 @@
     read = lax.all_to_all(sent, "space", 0, 0, tiled=True)
     moments, owned = residuals(read, data, site_cells, grid_rows, members)
     moments = lax.all_to_all(moments, "space", 0, 0, tiled=True)
+    moments, owned = lax.optimization_barrier((moments, owned))
     owned = lax.all_to_all(owned, "period", 0, 0, tiled=True)
     gradient = adjoint_solve(moments, station_parts, mass, field, grid_rows, members, grid_planes)
     return jnp.sum(owned, axis=0, keepdims=True), gradient

time: 111 us -> 90.8 us (0.82); the launches traced: 109 us -> 90.1 us
  Pallas kernels: 35.8 us -> 23.5 us
  waiting for transfers between devices: 14.5 us -> 5.45 us
  starting transfers between devices: 23.1 us -> 28 us
  blocking collectives: 32.4 us -> 30.2 us
    pallas_call x1, Pallas kernels: 15.4 us -> 3.12 us  [pack(): pl.pallas_call(lambda *refs: pack_kernel(grid_rows, grid_rows // members,...]
    all_to_all x1, waiting for transfers between devices: 8.91 us -> 0.01 us  [shards(): owned = lax.all_to_all(owned, 'period', 0, 0, tiled=True)]
    all_to_all x1, starting transfers between devices: 3.53 us -> 8.58 us  [shards(): owned = lax.all_to_all(owned, 'period', 0, 0, tiled=True)]
    all_to_all x1, blocking collectives: 15.6 us -> 13 us  [shards(): moments = lax.all_to_all(moments, 'space', 0, 0, tiled=True)]
  transfers between devices with their start and end apart: 6 -> 6, of which waited for: 2 -> 2; matrix products, arithmetic and copies ran while one was open for 1% -> 0% of each run, Pallas kernels for 5% -> 21%
where the time goes in v2:
time: 90.8 us; the launch traced here: 90.1 us
  blocking collectives  30.2 us (33%)
  starting transfers between devices  28 us (31%)
  Pallas kernels  23.5 us (26%)
  waiting for transfers between devices  5.45 us (6%)
  between operations  1.4 us (2%)
  local copies, waits for them, and re-layouts  0.95 us (1%)
    all_to_all x1, blocking collectives, shards(): read = lax.all_to_all(sent, 'space', 0, 0, tiled=True)  17.1 us
    pallas_call x1, Pallas kernels, adjoint_solve(): pl.pallas_call(lambda *refs: adjoint_kernel(grid_rows, own_rows, grid_pla...  13.2 us
    all_to_all x1, blocking collectives, shards(): moments = lax.all_to_all(moments, 'space', 0, 0, tiled=True)  13 us
    all_to_all x1, starting transfers between devices, shards(): data = lax.all_to_all(data, 'period', 0, 0, tiled=True)  9.93 us
    ppermute x4, starting transfers between devices, moved(): return lax.ppermute(values, ('space', 'period'), pairs)  9.53 us
    all_to_all x1, starting transfers between devices, shards(): owned = lax.all_to_all(owned, 'period', 0, 0, tiled=True)  8.58 us
    ppermute x4, waiting for transfers between devices, moved(): return lax.ppermute(values, ('space', 'period'), pairs)  5.45 us
    pallas_call x1, Pallas kernels, forward_solve(): pl.pallas_call(lambda *refs: forward_kernel(grid_rows, grid_rows // membe...  4.12 us
  transfers between devices with their start and end apart: 6, of which 2 were waited for; matrix products, arithmetic and copies ran while one was open for 0% of the time, Pallas kernels for 21%

profile of v2, /device:TPU:2, one launch (start us, length us, event | category | flops | bytes accessed | tf_op | source)
XLA Modules:
  0.0 90.1 jit_solution(2088348301446136488)
XLA Ops:
  0.6 0.0 copy-start.1
  0.6 0.0 copy-start.2
  1.3 3.1 %pack.1 = (f32[7,2,32,128]{3,2,1,0:T(8,128)}, f32[7,2,32,128]{3,2,1,0:T(8,128)}, f32[7,2,32,128]{3,2,1,0:T(8,128)}, f32[6,32,128]{2,1,0:T(8,128)}, f32[6,32,128]{2,1,0:T(8,128)}, /*index=5*/f32[16,16,128]{2,1,0:T(8,128)}) custom-call(f32[2,3,2,256,128]{4,3,2,1,0:T(8,128)} %refs_0_.2, f32[2,256,128]{2,1,0:T(8,128)} %refs_1_.2, f32[1]{0:T(128)S(6)} %copy.9.refs_2_, ...), custom_call_target="tpu_custom_call" | custom-call | tf_op jit(solution)/shard_map/pack/pallas_call | solution.py:160
  4.4 9.9 %all-to-all-start.1 = ((f32[16,16,128]{2,1,0:T(8,128)}), f32[16,16,128]{2,1,0:T(8,128)S(1)}, u32[]{:S(2)}, u32[]{:S(2)}) async-start(f32[16,16,128]{2,1,0:T(8,128)} %get-tuple-element.27), calls=%async_computation.1 | async-start | bytes 262144 | tf_op jit(solution)/shard_map/all_to_all | solution.py:573
  14.4 1.3 %collective-permute-start = (f32[7,2,32,128]{3,2,1,0:T(8,128)}, f32[7,2,32,128]{3,2,1,0:T(8,128)S(1)}, u32[]{:S(2)}, u32[]{:S(2)}) collective-permute-start(f32[7,2,32,128]{3,2,1,0:T(8,128)} %get-tuple-element.19), channel_id=1, source_target_pairs={{0,16},{1,17},{2,18},{3,19},{4,20},{5,21},{6,22},{7,23},{8,24},{9,... | collective-permute-start | bytes 688136 | tf_op jit(solution)/shard_map/ppermute | solution.py:567
  15.7 1.3 %collective-permute-start.1 = (f32[7,2,32,128]{3,2,1,0:T(8,128)}, f32[7,2,32,128]{3,2,1,0:T(8,128)S(1)}, u32[]{:S(2)}, u32[]{:S(2)}) collective-permute-start(f32[7,2,32,128]{3,2,1,0:T(8,128)} %get-tuple-element.20), channel_id=1, source_target_pairs={{16,0},{17,1},{18,2},{19,3},{20,4},{21,5},{22,6},{23,7},{24,8},{25... | collective-permute-start | bytes 688136 | tf_op jit(solution)/shard_map/ppermute | solution.py:567
  17.0 5.7 %collective-permute-start.2 = (f32[6,32,128]{2,1,0:T(8,128)}, f32[6,32,128]{2,1,0:T(8,128)S(1)}, u32[]{:S(2)}, u32[]{:S(2)}) collective-permute-start(f32[6,32,128]{2,1,0:T(8,128)} %get-tuple-element.21), channel_id=1, source_target_pairs={{0,33},{1,32},{2,35},{3,34},{4,37},{5,36},{6,39},{7,38},{8,41},{9,... | collective-permute-start | bytes 294920 | tf_op jit(solution)/shard_map/ppermute | solution.py:567
  22.6 1.3 %collective-permute-start.3 = (f32[6,32,128]{2,1,0:T(8,128)}, f32[6,32,128]{2,1,0:T(8,128)S(1)}, u32[]{:S(2)}, u32[]{:S(2)}) collective-permute-start(f32[6,32,128]{2,1,0:T(8,128)} %get-tuple-element.22), channel_id=1, source_target_pairs={{32,1},{33,0},{34,3},{35,2},{36,5},{37,4},{38,7},{39,6},{40,9},{41... | collective-permute-start | bytes 294920 | tf_op jit(solution)/shard_map/ppermute | solution.py:567
  23.9 0.0 copy-done.1
  23.9 0.0 copy-done.2
  23.9 1.3 %stations.1 = (s32[16,128]{1,0:T(8,128)S(1)}, s32[1]{0:T(128)}, f32[16,32,128]{2,1,0:T(8,128)S(1)}) custom-call(s32[4,2048]{1,0:T(4,128)S(1)} %copy-done.1, f32[4,2048]{1,0:T(4,128)S(1)} %copy-done.2), custom_call_target="tpu_custom_call" | custom-call | flops 10000000 | bytes 200000 | tf_op jit(solution)/shard_map/stations/pallas_call | solution.py:225
  25.2 0.6 collective-permute-done.2.refs_3_
  25.8 4.9 %collective-permute-done.3.refs_4_ = f32[6,32,128]{2,1,0:T(8,128)S(1)} collective-permute-done((f32[6,32,128]{2,1,0:T(8,128)}, f32[6,32,128]{2,1,0:T(8,128)S(1)}, u32[]{:S(2)}, u32[]{:S(2)}) %collective-permute-start.3) | collective-permute-done | bytes 98336 | tf_op jit(solution)/shard_map/ppermute | solution.py:567
  30.7 0.0 collective-permute-done.refs_1_
  30.7 0.0 collective-permute-done.1.refs_2_
  30.7 0.0 copy-start
  30.7 0.9 %copy-done = f32[7,2,32,128]{3,2,1,0:T(8,128)S(1)} copy-done((f32[7,2,32,128]{3,2,1,0:T(8,128)S(1)}, f32[7,2,32,128]{3,2,1,0:T(8,128)}, u32[]{:S(2)}) %copy-start) | copy-done | bytes 229400
  31.6 4.1 %forward_solve.1 = (f32[4,2,3,2,32,128]{5,4,3,2,1,0:T(8,128)S(1)}, f32[16,16,128]{2,1,0:T(8,128)S(1)}, f32[6,32,128]{2,1,0:T(8,128)S(1)}) custom-call(f32[7,2,32,128]{3,2,1,0:T(8,128)S(1)} %copy-done, f32[7,2,32,128]{3,2,1,0:T(8,128)S(1)} %collective-permute-done.refs_1_, f32[7,2,32,128]{3,2,1,0:T(8,128)S(1)} %collective-permute-done.1.refs_2_, ...), custom_call_target="tpu_custom_call" | custom-call | flops 50000000 | bytes 3000000 | tf_op jit(solution)/shard_map/forward_solve/pallas_call | solution.py:359
  35.7 0.0 all-to-all-done.1.refs_1_
  35.8 0.0 copy-start.3
  35.8 17.1 %all_to_all.20.refs_0_ = f32[16,16,128]{2,1,0:T(8,128)} all-to-all(f32[16,16,128]{2,1,0:T(8,128)S(1)} %get-tuple-element.26), channel_id=1, replica_groups=mesh['space'=16,'period'=16] {'space'}, dimensions={0} | all-to-all | bytes 262144 | tf_op jit(solution)/shard_map/all_to_all | solution.py:578
  52.9 0.0 copy-done.3
  52.9 1.8 %residuals.1 = (f32[16,32,128]{2,1,0:T(8,128)}, f32[16,4,128]{2,1,0:T(4,128)}) custom-call(f32[16,16,128]{2,1,0:T(8,128)} %all_to_all.20.refs_0_, f32[16,16,128]{2,1,0:T(8,128)} %copy-done.3, s32[4,2048]{1,0:T(4,128)} %refs_2_.2), custom_call_target="tpu_custom_call" | custom-call | tf_op jit(solution)/shard_map/residuals/pallas_call | solution.py:413
  54.7 13.0 %all_to_all.21.refs_0_ = f32[16,32,128]{2,1,0:T(8,128)S(1)} all-to-all(f32[16,32,128]{2,1,0:T(8,128)} %get-tuple-element.28), channel_id=1, replica_groups=mesh['space'=16,'period'=16] {'space'}, dimensions={0} | all-to-all | bytes 524288 | tf_op jit(solution)/shard_map/all_to_all | solution.py:580
  67.7 8.6 %all-to-all-start.3 = ((f32[16,4,128]{2,1,0:T(4,128)}), f32[16,4,128]{2,1,0:T(4,128)S(1)}, u32[]{:S(2)}, u32[]{:S(2)}) async-start(f32[16,4,128]{2,1,0:T(4,128)} %get-tuple-element.30), calls=%async_computation.3 | async-start | bytes 65536 | tf_op jit(solution)/shard_map/all_to_all | solution.py:582
  76.3 13.2 %adjoint_solve.1 = f32[2,16,128]{2,1,0:T(8,128)} custom-call(f32[16,32,128]{2,1,0:T(8,128)S(1)} %all_to_all.21.refs_0_, s32[16,128]{1,0:T(8,128)S(1)} %get-tuple-element.23.refs_5_.refs_1_, s32[1]{0:T(128)} %get-tuple-element.24.refs_6_.refs_2_, f32[16,32,128]{2,1,0:T(8,128)S(1)} %get-tuple-element.25.refs_7_.refs_3_, ...), custom_call_target="tpu_custom_call" | custom-call | flops 200000000 | bytes 3000000 | tf_op jit(solution)/shard_map/adjoint_solve/pallas_call | solution.py:534
  89.5 0.0 all-to-all-done.3
  89.5 0.6 reduce_sum.9
Async XLA Ops:
  0.6 23.3 %copy-start.1 = (s32[4,2048]{1,0:T(4,128)S(1)}, s32[4,2048]{1,0:T(4,128)}, u32[]{:S(2)}) copy-start(s32[4,2048]{1,0:T(4,128)} %refs_2_.2) | copy-start | bytes 98308
  0.6 23.3 %copy-start.2 = (f32[4,2048]{1,0:T(4,128)S(1)}, f32[4,2048]{1,0:T(4,128)}, u32[]{:S(2)}) copy-start(f32[4,2048]{1,0:T(4,128)} %refs_1_.3) | copy-start | bytes 98308
  4.4 31.3 %all-to-all-start.1 = ((f32[16,16,128]{2,1,0:T(8,128)}), f32[16,16,128]{2,1,0:T(8,128)S(1)}, u32[]{:S(2)}, u32[]{:S(2)}) async-start(f32[16,16,128]{2,1,0:T(8,128)} %get-tuple-element.27), calls=%async_computation.1 | async-start | bytes 262144 | tf_op jit(solution)/shard_map/all_to_all | solution.py:573
  14.4 16.3 %collective-permute-start = (f32[7,2,32,128]{3,2,1,0:T(8,128)}, f32[7,2,32,128]{3,2,1,0:T(8,128)S(1)}, u32[]{:S(2)}, u32[]{:S(2)}) collective-permute-start(f32[7,2,32,128]{3,2,1,0:T(8,128)} %get-tuple-element.19), channel_id=1, source_target_pairs={{0,16},{1,17},{2,18},{3,19},{4,20},{5,21},{6,22},{7,23},{8,24},{9,... | collective-permute-start | bytes 688136 | tf_op jit(solution)/shard_map/ppermute | solution.py:567
  15.7 15.0 %collective-permute-start.1 = (f32[7,2,32,128]{3,2,1,0:T(8,128)}, f32[7,2,32,128]{3,2,1,0:T(8,128)S(1)}, u32[]{:S(2)}, u32[]{:S(2)}) collective-permute-start(f32[7,2,32,128]{3,2,1,0:T(8,128)} %get-tuple-element.20), channel_id=1, source_target_pairs={{16,0},{17,1},{18,2},{19,3},{20,4},{21,5},{22,6},{23,7},{24,8},{25... | collective-permute-start | bytes 688136 | tf_op jit(solution)/shard_map/ppermute | solution.py:567
  17.0 8.8 %collective-permute-start.2 = (f32[6,32,128]{2,1,0:T(8,128)}, f32[6,32,128]{2,1,0:T(8,128)S(1)}, u32[]{:S(2)}, u32[]{:S(2)}) collective-permute-start(f32[6,32,128]{2,1,0:T(8,128)} %get-tuple-element.21), channel_id=1, source_target_pairs={{0,33},{1,32},{2,35},{3,34},{4,37},{5,36},{6,39},{7,38},{8,41},{9,... | collective-permute-start | bytes 294920 | tf_op jit(solution)/shard_map/ppermute | solution.py:567
  22.6 8.0 %collective-permute-start.3 = (f32[6,32,128]{2,1,0:T(8,128)}, f32[6,32,128]{2,1,0:T(8,128)S(1)}, u32[]{:S(2)}, u32[]{:S(2)}) collective-permute-start(f32[6,32,128]{2,1,0:T(8,128)} %get-tuple-element.22), channel_id=1, source_target_pairs={{32,1},{33,0},{34,3},{35,2},{36,5},{37,4},{38,7},{39,6},{40,9},{41... | collective-permute-start | bytes 294920 | tf_op jit(solution)/shard_map/ppermute | solution.py:567
  30.7 0.9 %copy-start = (f32[7,2,32,128]{3,2,1,0:T(8,128)S(1)}, f32[7,2,32,128]{3,2,1,0:T(8,128)}, u32[]{:S(2)}) copy-start(f32[7,2,32,128]{3,2,1,0:T(8,128)} %get-tuple-element.18.refs_0_) | copy-start | bytes 688132
  35.8 17.2 %copy-start.3 = (f32[16,16,128]{2,1,0:T(8,128)}, f32[16,16,128]{2,1,0:T(8,128)S(1)}, u32[]{:S(2)}) copy-start(f32[16,16,128]{2,1,0:T(8,128)S(1)} %all-to-all-done.1.refs_1_) | copy-start | bytes 393220
  67.7 21.8 %all-to-all-start.3 = ((f32[16,4,128]{2,1,0:T(4,128)}), f32[16,4,128]{2,1,0:T(4,128)S(1)}, u32[]{:S(2)}, u32[]{:S(2)}) async-start(f32[16,4,128]{2,1,0:T(4,128)} %get-tuple-element.30), calls=%async_computation.3 | async-start | bytes 65536 | tf_op jit(solution)/shard_map/all_to_all | solution.py:582

commit v3 on v2

--- a/solution.py
+++ b/solution.py
@@ -13,10 +13,12 @@
 HALO = SWEEPS - 1
 PLANES = 2 + 2 * HALO
 WINDOW = 32
+NARROW = 24
 DEGREE = SWEEPS
 MOMENTS = 2 * SWEEPS - 1
 LANES = 128
-VMEM_LIMIT = 48 * 1024 * 1024
+VMEM_SMALL = 6 * 1024 * 1024
+VMEM_LIMIT = 16 * 1024 * 1024
 
 
 def chebyshev_steps(sweep_count):
@@ -47,10 +49,12 @@
     return pl.multiple_of(jnp.clip(first, 0, grid_rows - WINDOW), 8)
 
 
-def place(grid_rows, own_rows):
-    member = lax.axis_index("period")
-    first_row = window_row(member, grid_rows, own_rows)
-    return lax.axis_index("space") * 2 - HALO, first_row, member * own_rows
+def narrow_row(member, grid_rows, own_rows):
+    return jnp.clip(member * own_rows - (NARROW - own_rows) // 2, 0, grid_rows - NARROW)
+
+
+def first_window_plane():
+    return lax.axis_index("space") * 2 - HALO
 
 
 def iota(shape, dim):
@@ -120,26 +124,21 @@
 
 def pack_kernel(
     grid_rows, own_rows, source, conductivity, shift, observed, weight,
-    slab, up, down, up2, down2, data, sems,
+    slab, beside, far_a, far_b, data, sems,
 ):
     member = lax.axis_index("period")
-    even = lax.axis_index("space") % 2 == 0
-    mine = window_row(member, grid_rows, own_rows)
-    beside = window_row(member + 1 - 2 * (member % 2), grid_rows, own_rows)
+    pair = (lax.axis_index("space") // 2) % 2
     copies = []
-    for target, row in (
-        (slab, mine),
-        (up, jnp.where(even, mine, beside)),
-        (down, jnp.where(even, beside, mine)),
-    ):
-        rows = pl.ds(pl.multiple_of(row, 8), WINDOW)
-        for pol in range(2):
-            copies.append((source.at[pol, :, :, rows, :], target.at[pl.ds(3 * pol, 3)]))
-        copies.append((conductivity.at[:, rows, :], target.at[6]))
-    rows = pl.ds(beside, WINDOW)
+    rows = pl.ds(window_row(member, grid_rows, own_rows), WINDOW)
     for pol in range(2):
-        copies.append((source.at[pol, :, 1, rows, :], up2.at[pl.ds(3 * pol, 3)]))
-        copies.append((source.at[pol, :, 0, rows, :], down2.at[pl.ds(3 * pol, 3)]))
+        copies.append((source.at[pol, :, :, rows, :], slab.at[pl.ds(3 * pol, 3)]))
+    copies.append((conductivity.at[:, rows, :], slab.at[6]))
+    rows = pl.ds(window_row(member + 1 - 2 * (member % 2), grid_rows, own_rows), WINDOW)
+    for pol in range(2):
+        copies.append((source.at[pol, :, :, rows, :], beside.at[pl.ds(3 * pol, 3)]))
+        copies.append((source.at[pol, :, 1 - pair, rows, :], far_a.at[pl.ds(3 * pol, 3)]))
+        copies.append((source.at[pol, :, pair, rows, :], far_b.at[pl.ds(3 * pol, 3)]))
+    copies.append((conductivity.at[:, rows, :], beside.at[6]))
     started = [pltpu.make_async_copy(a, b, sems.at[i]) for i, (a, b) in enumerate(copies)]
     for copy in started:
         copy.start()
@@ -159,33 +158,39 @@
     smem = pl.BlockSpec(memory_space=pltpu.SMEM)
     return pl.pallas_call(
         lambda *refs: pack_kernel(grid_rows, grid_rows // members, *refs),
-        out_shape=(shape((7, 2, WINDOW, LANES), jnp.float32),) * 3
+        out_shape=(shape((7, 2, WINDOW, LANES), jnp.float32),) * 2
         + (shape((6, WINDOW, LANES), jnp.float32),) * 2
         + (shape((members, 16, LANES), jnp.float32),),
         in_specs=[hbm, hbm, smem, vmem, vmem],
-        out_specs=(vmem,) * 6,
-        scratch_shapes=[pltpu.SemaphoreType.DMA((13,))],
+        out_specs=(vmem,) * 5,
+        scratch_shapes=[pltpu.SemaphoreType.DMA((10,))],
+        compiler_params=pltpu.CompilerParams(vmem_limit_bytes=VMEM_SMALL),
         name="pack",
     )(source, conductivity, shift, observed, weight)
 
 
 def stations_kernel(grid_rows, own_rows, cells, weights, places, count, features, marks, staged):
-    first_plane, first_row, first_own = place(grid_rows, own_rows)
+    member = lax.axis_index("period")
+    first_own = member * own_rows
+    first_row = window_row(member, grid_rows, own_rows)
+    first_narrow = narrow_row(member, grid_rows, own_rows)
     plane_size = grid_rows * LANES
     cell = cells[...]
-    x = cell // plane_size - first_plane
+    x = cell // plane_size - first_window_plane()
     y = (cell // LANES) % grid_rows
     reached = (
         (x >= 0) & (x < PLANES)
         & (y >= first_own - HALO - 1) & (y < first_own + own_rows + HALO + 1)
     )
     row = jnp.where(reached, x * WINDOW + y - first_row, 0).astype(jnp.float32)
+    narrow = jnp.where(reached, x * NARROW + y - first_narrow, 0).astype(jnp.float32)
     weight = jnp.where(reached, weights[...], 0.0)
     present = jnp.max(jnp.where(reached, 1.0, 0.0), axis=0, keepdims=True)
     blocks = cell.shape[1] // LANES
     staged[...] = jnp.zeros(staged.shape, jnp.float32)
     staged[0:4, :] = row
     staged[4:8, :] = (cell % LANES).astype(jnp.float32)
+    staged[20:24, :] = narrow
     for number, part in enumerate(parts_of(weight)):
         staged[8 + 4 * number : 12 + 4 * number, :] = part.astype(jnp.float32)
     for block in range(blocks):
@@ -241,12 +246,12 @@
     )(cells, weights)
 
 
-def row_weights(feature, first, count):
+def row_weights(feature, field, first, count):
     rows = (iota((count, LANES), 0) + first).astype(jnp.float32)
     total = jnp.zeros((count, LANES), jnp.float32)
     for q in range(4):
         weight = feature[8 + q : 9 + q] + feature[12 + q : 13 + q] + feature[16 + q : 17 + q]
-        total += jnp.where(rows == feature[q : q + 1], weight, 0.0)
+        total += jnp.where(rows == feature[field + q : field + q + 1], weight, 0.0)
     return total
 
 
@@ -256,24 +261,23 @@
 
 
 def forward_kernel(
-    grid_rows, own_rows, grid_planes, slab, below, above, below2, above2, places, count, features,
-    field, sent, mass, d1, d2,
+    grid_rows, own_rows, grid_planes, slab, mate, beside, far_a, far_b, places, count, features,
+    field, sent, mass, window, d1, d2,
 ):
-    first_plane, _, _ = place(grid_rows, own_rows)
+    first_plane = first_window_plane()
+    even = lax.axis_index("space") % 2 == 0
+    lower = (lax.axis_index("space") // 2) % 2 == 0
+    for plane in range(2):
+        here, there = mate[:, plane], beside[:, plane]
+        window[:, 1 + plane] = jnp.where(even, there, here)
+        window[:, 3 + plane] = slab[:, plane]
+        window[:, 5 + plane] = jnp.where(even, here, there)
+    window[0:6, 0] = jnp.where(lower, far_b[...], far_a[...])
+    window[0:6, PLANES - 1] = jnp.where(lower, far_a[...], far_b[...])
+    mass[...] = window[6, 1 : PLANES - 1]
 
     def part(number, plane):
-        if plane == 0:
-            return below2[number]
-        if plane <= 2:
-            return below[number, plane - 1]
-        if plane <= 4:
-            return slab[number, plane - 3]
-        if plane <= 6:
-            return above[number, plane - 5]
-        return above2[number]
-
-    for plane in range(1, PLANES - 1):
-        mass[plane - 1] = part(6, plane)
+        return window[number, plane]
 
     for pol in range(2):
         def b(plane, pol=pol):
@@ -332,7 +336,7 @@
 
     def one_chunk(chunk, carry):
         feature = features[chunk]
-        weight = row_weights(feature, HALO * WINDOW, 2 * WINDOW)
+        weight = row_weights(feature, 0, HALO * WINDOW, 2 * WINDOW)
         depth = depth_picks(feature)
         rows = []
         for j in range(DEGREE):
@@ -351,7 +355,7 @@
     lax.fori_loop(0, count[0], one_chunk, 0)
 
 
-def forward_solve(slab, below, above, below2, above2, station_parts, grid_rows, members, grid_planes):
+def forward_solve(windows, station_parts, grid_rows, members, grid_planes):
     shape = jax.ShapeDtypeStruct
     vmem = pl.BlockSpec(memory_space=pltpu.VMEM)
     smem = pl.BlockSpec(memory_space=pltpu.SMEM)
@@ -366,13 +370,14 @@
         in_specs=[vmem] * 6 + [smem, vmem],
         out_specs=(vmem, vmem, vmem),
         scratch_shapes=[
+            pltpu.VMEM((7, PLANES, WINDOW, LANES), jnp.float32),
             pltpu.VMEM((2, 2, 3, PLANES - 2, WINDOW, LANES), jnp.float32),
             pltpu.VMEM((3, 2, 3, PLANES - 4, WINDOW, LANES), jnp.float32),
         ],
         compiler_params=pltpu.CompilerParams(vmem_limit_bytes=VMEM_LIMIT),
         cost_estimate=pl.CostEstimate(flops=50_000_000, bytes_accessed=3_000_000, transcendentals=0),
         name="forward_solve",
-    )(slab, below, above, below2, above2, *station_parts)
+    )(*windows, *station_parts)
 
 
 def residual_kernel(grid_rows, own_rows, read, data, cells, moments, owned, staged):
@@ -419,6 +424,7 @@
         in_specs=[vmem, vmem, vmem],
         out_specs=(vmem, vmem),
         scratch_shapes=[pltpu.VMEM((32, LANES), jnp.float32)],
+        compiler_params=pltpu.CompilerParams(vmem_limit_bytes=VMEM_SMALL),
         name="residuals",
     )(read, data, cells)
 
@@ -427,13 +433,17 @@
     grid_rows, own_rows, grid_planes, periods, moments, places, count, features, mass, field,
     gradient, d0, d1, d2, picked, total,
 ):
-    first_plane, first_row, first_own = place(grid_rows, own_rows)
+    first_plane = first_window_plane()
+    member = lax.axis_index("period")
+    first_row = narrow_row(member, grid_rows, own_rows)
+    inner = pl.ds(first_row - window_row(member, grid_rows, own_rows), NARROW)
+    own = pl.ds(member * own_rows - first_row, own_rows)
     blocks = moments.shape[0]
-    window_rows = PLANES * WINDOW
+    window_rows = PLANES * NARROW
 
     def add_chunk(chunk, fresh):
         feature = features[chunk]
-        weight = row_weights(feature, 0, window_rows)
+        weight = row_weights(feature, 20, 0, window_rows)
         depth = depth_picks(feature)
         depth = jnp.concatenate([depth, depth], axis=1)
         gathered = jnp.zeros((96, LANES), jnp.float32)
@@ -453,7 +463,7 @@
                 d0[number] += placed
             return carry
 
-        lax.fori_loop(0, 4 * MOMENTS, one_field, 0)
+        lax.fori_loop(0, 4 * MOMENTS, one_field, 0, unroll=MOMENTS)
 
     add_chunk(0, True)
 
@@ -464,14 +474,14 @@
     lax.fori_loop(1, count[0], one_chunk, 0)
 
     def start(f, c, plane):
-        return d0[2 * f + c, plane * WINDOW : (plane + 1) * WINDOW, :]
+        return d0[2 * f + c, plane * NARROW : (plane + 1) * NARROW, :]
 
     def level_one(f, carry):
         def b(plane):
             return start(f, 0, plane), start(f, 1, plane), None
 
         for plane, here, curled in curl_curl(b, 1, 6, first_plane, grid_planes):
-            m = mass[plane - 1]
+            m = mass[plane - 1, inner, :]
             for c in range(2):
                 mixed = CENTER * here[c] + start(f + 2, c, plane)
                 d1[f, c, plane - 1] = (
@@ -487,7 +497,7 @@
             return tuple(d1[f, c, plane - 1] for c in range(3))
 
         for plane, here, curled in curl_curl(get, 2, 5, first_plane, grid_planes):
-            m = mass[plane - 1]
+            m = mass[plane - 1, inner, :]
             for c in range(3):
                 mixed = CENTER * here[c] + d1[f + 2, c, plane - 1]
                 value = (1.0 + MOMENTUM[2]) * here[c] - STEP[1] * (curled[c] + m * mixed)
@@ -505,7 +515,7 @@
             return tuple(d2[f, c, plane - 2] for c in range(3))
 
         for plane, here, curled in curl_curl(get, 3, 4, first_plane, grid_planes):
-            m = mass[plane - 1]
+            m = mass[plane - 1, inner, :]
             added = None
             for c in range(3):
                 mixed = CENTER * here[c] + d2[f + 2, c, plane - 2]
@@ -517,14 +527,13 @@
                 value = STEP[1] * first + STEP[2] * here[c] + STEP[3] * last
                 if c < 2:
                     value = value + STEP[0] * start(f, c, plane)
-                term = value * field[f, c, plane - 3]
+                term = value * field[f, c, plane - 3, inner, :]
                 added = term if added is None else added + term
             total[plane - 3] += added
         return carry
 
     lax.fori_loop(0, 2 * DEGREE, level_three, 0)
-    offset = pl.multiple_of(first_own - first_row, 8)
-    gradient[...] = total[:, pl.ds(offset, own_rows), :] * (-1.0 / periods)
+    gradient[...] = total[:, own, :] * (-1.0 / periods)
 
 
 def adjoint_solve(moments, station_parts, mass, field, grid_rows, members, grid_planes):
@@ -537,11 +546,11 @@
         in_specs=[vmem, vmem, smem, vmem, vmem, vmem],
         out_specs=vmem,
         scratch_shapes=[
-            pltpu.VMEM((4 * MOMENTS, PLANES * WINDOW, LANES), jnp.float32),
-            pltpu.VMEM((2 * (MOMENTS - 1), 3, PLANES - 2, WINDOW, LANES), jnp.float32),
-            pltpu.VMEM((2 * (MOMENTS - 2), 3, PLANES - 4, WINDOW, LANES), jnp.float32),
+            pltpu.VMEM((4 * MOMENTS, PLANES * NARROW, LANES), jnp.float32),
+            pltpu.VMEM((2 * (MOMENTS - 1), 3, PLANES - 2, NARROW, LANES), jnp.float32),
+            pltpu.VMEM((2 * (MOMENTS - 2), 3, PLANES - 4, NARROW, LANES), jnp.float32),
             pltpu.VMEM((32, LANES), jnp.float32),
-            pltpu.VMEM((2, WINDOW, LANES), jnp.float32),
+            pltpu.VMEM((2, NARROW, LANES), jnp.float32),
         ],
         compiler_params=pltpu.CompilerParams(vmem_limit_bytes=VMEM_LIMIT),
         cost_estimate=pl.CostEstimate(flops=200_000_000, bytes_accessed=3_000_000, transcendentals=0),
@@ -554,27 +563,29 @@
     count = lax.axis_size("space")
     members = lax.axis_size("period")
     grid_planes = conductivity.shape[0] * count
-    slab, up, down, up2, down2, data = pack(
+    slab, beside, far_a, far_b, data = pack(
         source, conductivity, period_shift, observed, data_weight, members
     )
 
-    def moved(values, by):
+    def swapped(values, partner):
         pairs = []
         for i in range(count):
-            if 0 <= i + by < count:
-                flip = 0 if (i + by) // 2 == i // 2 else 1
-                pairs += [(i * members + t, (i + by) * members + (t ^ flip)) for t in range(members)]
+            j = partner(i)
+            flip = 0 if i // 2 == j // 2 else 1
+            if 0 <= j < count:
+                pairs += [(i * members + t, j * members + (t ^ flip)) for t in range(members)]
         return lax.ppermute(values, ("space", "period"), pairs)
 
-    below = moved(up, 1)
-    above = moved(down, -1)
-    below2 = moved(up2, 2)
-    above2 = moved(down2, -2)
+    windows = (
+        slab,
+        swapped(slab, lambda i: i ^ 1),
+        swapped(beside, lambda i: i + 1 if i % 2 else i - 1),
+        swapped(far_a, lambda i: i ^ 2),
+        swapped(far_b, lambda i: i + 2 if i & 2 else i - 2),
+    )
     data = lax.all_to_all(data, "period", 0, 0, tiled=True)
     station_parts = stations(site_cells, site_weights, grid_rows, members)
-    field, sent, mass = forward_solve(
-        slab, below, above, below2, above2, station_parts, grid_rows, members, grid_planes
-    )
+    field, sent, mass = forward_solve(windows, station_parts, grid_rows, members, grid_planes)
     read = lax.all_to_all(sent, "space", 0, 0, tiled=True)
     moments, owned = residuals(read, data, site_cells, grid_rows, members)
     moments = lax.all_to_all(moments, "space", 0, 0, tiled=True)

time: 90.8 us -> 80.2 us (0.88)
  Pallas kernels: 23.5 us -> 15.7 us
  starting transfers between devices: 28 us -> 23.9 us
  waiting for transfers between devices: 5.45 us -> 2.61 us
  local copies, waits for them, and re-layouts: 0.95 us -> 3.72 us
  blocking collectives: 30.2 us -> 31.9 us
    pallas_call x1, Pallas kernels: 13.2 us -> 8.71 us  [adjoint_solve(): pl.pallas_call(lambda *refs: adjoint_kernel(grid_rows, own_rows, grid_pla...]
    ppermute x4, starting transfers between devices: 9.53 us -> 5.79 us  [swapped(): return lax.ppermute(values, ('space', 'period'), pairs)]
    ppermute x4, waiting for transfers between devices: 5.45 us -> 2.6 us  [swapped(): return lax.ppermute(values, ('space', 'period'), pairs)]
    unnamed x8 -> x12, local copies, waits for them, and re-layouts: 0.95 us -> 3.72 us
    all_to_all x1, blocking collectives: 17.1 us -> 19.7 us  [shards(): read = lax.all_to_all(sent, 'space', 0, 0, tiled=True)]
    pallas_call x1, Pallas kernels: 3.12 us -> 0.99 us  [pack(): pl.pallas_call(lambda *refs: pack_kernel(grid_rows, grid_rows // members,...]
    pallas_call x1, Pallas kernels: 1.78 us -> 0.67 us  [residuals(): pl.pallas_call(lambda *refs: residual_kernel(grid_rows, grid_rows // memb...]
  transfers between devices with their start and end apart: 6 -> 6, of which waited for: 2 -> 1; matrix products, arithmetic and copies ran while one was open for 0% -> 0% of each run, Pallas kernels for 21% -> 18%
where the time goes in v3:
time: 80.2 us; the launch traced here: 79.7 us
  blocking collectives  31.9 us (40%)
  starting transfers between devices  23.9 us (30%)
  Pallas kernels  15.7 us (20%)
  local copies, waits for them, and re-layouts  3.72 us (5%)
  waiting for transfers between devices  2.61 us (3%)
  between operations  1.36 us (2%)
    all_to_all x1, blocking collectives, shards(): read = lax.all_to_all(sent, 'space', 0, 0, tiled=True)  19.7 us
    all_to_all x1, blocking collectives, shards(): moments = lax.all_to_all(moments, 'space', 0, 0, tiled=True)  12.1 us
    all_to_all x1, starting transfers between devices, shards(): data = lax.all_to_all(data, 'period', 0, 0, tiled=True)  9.95 us
    pallas_call x1, Pallas kernels, adjoint_solve(): pl.pallas_call(lambda *refs: adjoint_kernel(grid_rows, own_rows, grid_pla...  8.71 us
    all_to_all x1, starting transfers between devices, shards(): owned = lax.all_to_all(owned, 'period', 0, 0, tiled=True)  8.12 us
    ppermute x4, starting transfers between devices, swapped(): return lax.ppermute(values, ('space', 'period'), pairs)  5.79 us
    pallas_call x1, Pallas kernels, forward_solve(): pl.pallas_call(lambda *refs: forward_kernel(grid_rows, grid_rows // membe...  4.04 us
    unnamed x12, local copies, waits for them, and re-layouts  3.72 us
  transfers between devices with their start and end apart: 6, of which 1 were waited for; matrix products, arithmetic and copies ran while one was open for 0% of the time, Pallas kernels for 18%

profile of v3, /device:TPU:2, one launch (start us, length us, event | category | flops | bytes accessed | tf_op | source)
XLA Modules:
  0.0 79.7 jit_solution(15164491492501465444)
XLA Ops:
  1.3 0.0 copy-start
  1.3 1.4 %copy-done = f32[2,3,2,256,128]{4,3,2,1,0:T(8,128)S(1)} copy-done((f32[2,3,2,256,128]{4,3,2,1,0:T(8,128)S(1)}, f32[2,3,2,256,128]{4,3,2,1,0:T(8,128)}, u32[]{:S(2)}) %copy-start) | copy-done | bytes 1572888
  2.7 0.0 copy-start.1
  2.7 0.9 %copy-done.1 = f32[2,256,128]{2,1,0:T(8,128)S(1)} copy-done((f32[2,256,128]{2,1,0:T(8,128)S(1)}, f32[2,256,128]{2,1,0:T(8,128)}, u32[]{:S(2)}) %copy-start.1) | copy-done | bytes 262168
  3.6 0.0 copy-start.4
  3.6 0.7 copy-done.4
  4.3 0.0 copy-start.5
  4.3 0.7 copy-done.5
  5.0 0.0 copy-start.2
  5.0 0.0 copy-start.3
  5.0 1.0 %pack.1 = (f32[7,2,32,128]{3,2,1,0:T(8,128)S(1)}, f32[7,2,32,128]{3,2,1,0:T(8,128)S(1)}, f32[6,32,128]{2,1,0:T(8,128)S(1)}, f32[6,32,128]{2,1,0:T(8,128)S(1)}, f32[16,16,128]{2,1,0:T(8,128)}) custom-call(f32[2,3,2,256,128]{4,3,2,1,0:T(8,128)S(1)} %copy-done, f32[2,256,128]{2,1,0:T(8,128)S(1)} %copy-done.1, f32[1]{0:T(128)S(6)} %copy.9.refs_2_, ...), custom_call_target="tpu_custom_call" | custom-call | tf_op jit(solution)/shard_map/pack/pallas_call | solution.py:159
  6.0 10.0 %all-to-all-start.1 = ((f32[16,16,128]{2,1,0:T(8,128)}), f32[16,16,128]{2,1,0:T(8,128)S(1)}, u32[]{:S(2)}, u32[]{:S(2)}) async-start(f32[16,16,128]{2,1,0:T(8,128)} %get-tuple-element.25), calls=%async_computation.1 | async-start | bytes 262144 | tf_op jit(solution)/shard_map/all_to_all | solution.py:586
  15.9 0.7 collective-permute-start.1
  16.6 2.2 %collective-permute-start = (f32[7,2,32,128]{3,2,1,0:T(8,128)S(1)}, f32[7,2,32,128]{3,2,1,0:T(8,128)S(1)}, u32[]{:S(2)}, u32[]{:S(2)}) collective-permute-start(f32[7,2,32,128]{3,2,1,0:T(8,128)S(1)} %get-tuple-element.17.refs_0_), channel_id=1, source_target_pairs={{0,16},{1,17},{2,18},{3,19},{4,20},{5,21},{6,22},{7,23},{8,24},{9,... | collective-permute-start | bytes 688136 | tf_op jit(solution)/shard_map/ppermute | solution.py:577
  18.8 2.3 %collective-permute-start.2 = (f32[6,32,128]{2,1,0:T(8,128)S(1)}, f32[6,32,128]{2,1,0:T(8,128)S(1)}, u32[]{:S(2)}, u32[]{:S(2)}) collective-permute-start(f32[6,32,128]{2,1,0:T(8,128)S(1)} %get-tuple-element.19), channel_id=1, source_target_pairs={{0,33},{1,32},{2,35},{3,34},{4,37},{5,36},{6,39},{7,38},{8,41},{9,... | collective-permute-start | bytes 294920 | tf_op jit(solution)/shard_map/ppermute | solution.py:577
  21.1 0.7 collective-permute-start.3
  21.8 0.0 copy-done.2
  21.8 0.0 copy-done.3
  21.8 1.3 %stations.1 = (s32[16,128]{1,0:T(8,128)S(1)}, s32[1]{0:T(128)}, f32[16,32,128]{2,1,0:T(8,128)S(1)}) custom-call(s32[4,2048]{1,0:T(4,128)S(1)} %copy-done.2, f32[4,2048]{1,0:T(4,128)S(1)} %copy-done.3), custom_call_target="tpu_custom_call" | custom-call | flops 10000000 | bytes 200000 | tf_op jit(solution)/shard_map/stations/pallas_call | solution.py:230
  23.1 2.6 %collective-permute-done.2.refs_3_ = f32[6,32,128]{2,1,0:T(8,128)S(1)} collective-permute-done((f32[6,32,128]{2,1,0:T(8,128)S(1)}, f32[6,32,128]{2,1,0:T(8,128)S(1)}, u32[]{:S(2)}, u32[]{:S(2)}) %collective-permute-start.2) | collective-permute-done | bytes 98336 | tf_op jit(solution)/shard_map/ppermute | solution.py:577
  25.7 0.0 collective-permute-done.3.refs_4_
  25.7 0.0 collective-permute-done.1.refs_2_
  25.7 0.0 collective-permute-done.refs_1_
  25.7 4.0 %forward_solve.1 = (f32[4,2,3,2,32,128]{5,4,3,2,1,0:T(8,128)S(1)}, f32[16,16,128]{2,1,0:T(8,128)S(1)}, f32[6,32,128]{2,1,0:T(8,128)S(1)}) custom-call(f32[7,2,32,128]{3,2,1,0:T(8,128)S(1)} %get-tuple-element.17.refs_0_, f32[7,2,32,128]{3,2,1,0:T(8,128)S(1)} %collective-permute-done.refs_1_, f32[7,2,32,128]{3,2,1,0:T(8,128)S(1)} %collective-permute-done.1.refs_2_, ...), custom_call_target="tpu_custom_call" | custom-call | flops 50000000 | bytes 3000000 | tf_op jit(solution)/shard_map/forward_solve/pallas_call | solution.py:363
  29.7 0.0 all-to-all-done.1.refs_1_
  29.7 19.7 %all_to_all.20.refs_0_ = f32[16,16,128]{2,1,0:T(8,128)S(1)} all-to-all(f32[16,16,128]{2,1,0:T(8,128)S(1)} %get-tuple-element.24), channel_id=1, replica_groups=mesh['space'=16,'period'=16] {'space'}, dimensions={0} | all-to-all | bytes 262144 | tf_op jit(solution)/shard_map/all_to_all | solution.py:589
  49.5 0.7 residuals.1
  50.1 12.1 %all_to_all.21.refs_0_ = f32[16,32,128]{2,1,0:T(8,128)S(1)} all-to-all(f32[16,32,128]{2,1,0:T(8,128)S(1)} %get-tuple-element.26), channel_id=1, replica_groups=mesh['space'=16,'period'=16] {'space'}, dimensions={0} | all-to-all | bytes 524288 | tf_op jit(solution)/shard_map/all_to_all | solution.py:591
  62.3 8.1 %all-to-all-start.3 = ((f32[16,4,128]{2,1,0:T(4,128)}), f32[16,4,128]{2,1,0:T(4,128)S(1)}, u32[]{:S(2)}, u32[]{:S(2)}) async-start(f32[16,4,128]{2,1,0:T(4,128)} %get-tuple-element.28), calls=%async_computation.3 | async-start | bytes 65536 | tf_op jit(solution)/shard_map/all_to_all | solution.py:593
  70.4 8.7 %adjoint_solve.1 = f32[2,16,128]{2,1,0:T(8,128)} custom-call(f32[16,32,128]{2,1,0:T(8,128)S(1)} %all_to_all.21.refs_0_, s32[16,128]{1,0:T(8,128)S(1)} %get-tuple-element.21.refs_5_.refs_1_, s32[1]{0:T(128)} %get-tuple-element.22.refs_6_.refs_2_, f32[16,32,128]{2,1,0:T(8,128)S(1)} %get-tuple-element.23.refs_7_.refs_3_, ...), custom_call_target="tpu_custom_call" | custom-call | flops 200000000 | bytes 3000000 | tf_op jit(solution)/shard_map/adjoint_solve/pallas_call | solution.py:543
  79.1 0.0 all-to-all-done.3
  79.1 0.6 reduce_sum.9
Async XLA Ops:
  1.3 1.4 %copy-start = (f32[2,3,2,256,128]{4,3,2,1,0:T(8,128)S(1)}, f32[2,3,2,256,128]{4,3,2,1,0:T(8,128)}, u32[]{:S(2)}) copy-start(f32[2,3,2,256,128]{4,3,2,1,0:T(8,128)} %refs_0_.2) | copy-start | bytes 4718596
  2.7 0.9 %copy-start.1 = (f32[2,256,128]{2,1,0:T(8,128)S(1)}, f32[2,256,128]{2,1,0:T(8,128)}, u32[]{:S(2)}) copy-start(f32[2,256,128]{2,1,0:T(8,128)} %refs_1_.2) | copy-start | bytes 786436
  3.6 0.7 copy-start.4
  4.3 0.7 copy-start.5
  5.0 16.8 %copy-start.2 = (s32[4,2048]{1,0:T(4,128)S(1)}, s32[4,2048]{1,0:T(4,128)}, u32[]{:S(2)}) copy-start(s32[4,2048]{1,0:T(4,128)} %refs_2_.2) | copy-start | bytes 98308
  5.0 16.8 %copy-start.3 = (f32[4,2048]{1,0:T(4,128)S(1)}, f32[4,2048]{1,0:T(4,128)}, u32[]{:S(2)}) copy-start(f32[4,2048]{1,0:T(4,128)} %refs_1_.3) | copy-start | bytes 98308
  6.0 23.7 %all-to-all-start.1 = ((f32[16,16,128]{2,1,0:T(8,128)}), f32[16,16,128]{2,1,0:T(8,128)S(1)}, u32[]{:S(2)}, u32[]{:S(2)}) async-start(f32[16,16,128]{2,1,0:T(8,128)} %get-tuple-element.25), calls=%async_computation.1 | async-start | bytes 262144 | tf_op jit(solution)/shard_map/all_to_all | solution.py:586
  15.9 9.7 %collective-permute-start.1 = (f32[7,2,32,128]{3,2,1,0:T(8,128)S(1)}, f32[7,2,32,128]{3,2,1,0:T(8,128)S(1)}, u32[]{:S(2)}, u32[]{:S(2)}) collective-permute-start(f32[7,2,32,128]{3,2,1,0:T(8,128)S(1)} %get-tuple-element.18), channel_id=1, source_target_pairs={{16,33},{17,32},{18,35},{19,34},{20,37},{21,36},{22,39},{23,38},{2... | collective-permute-start | bytes 688136 | tf_op jit(solution)/shard_map/ppermute | solution.py:577
  16.6 9.1 %collective-permute-start = (f32[7,2,32,128]{3,2,1,0:T(8,128)S(1)}, f32[7,2,32,128]{3,2,1,0:T(8,128)S(1)}, u32[]{:S(2)}, u32[]{:S(2)}) collective-permute-start(f32[7,2,32,128]{3,2,1,0:T(8,128)S(1)} %get-tuple-element.17.refs_0_), channel_id=1, source_target_pairs={{0,16},{1,17},{2,18},{3,19},{4,20},{5,21},{6,22},{7,23},{8,24},{9,... | collective-permute-start | bytes 688136 | tf_op jit(solution)/shard_map/ppermute | solution.py:577
  18.8 6.8 %collective-permute-start.2 = (f32[6,32,128]{2,1,0:T(8,128)S(1)}, f32[6,32,128]{2,1,0:T(8,128)S(1)}, u32[]{:S(2)}, u32[]{:S(2)}) collective-permute-start(f32[6,32,128]{2,1,0:T(8,128)S(1)} %get-tuple-element.19), channel_id=1, source_target_pairs={{0,33},{1,32},{2,35},{3,34},{4,37},{5,36},{6,39},{7,38},{8,41},{9,... | collective-permute-start | bytes 294920 | tf_op jit(solution)/shard_map/ppermute | solution.py:577
  21.1 4.6 %collective-permute-start.3 = (f32[6,32,128]{2,1,0:T(8,128)S(1)}, f32[6,32,128]{2,1,0:T(8,128)S(1)}, u32[]{:S(2)}, u32[]{:S(2)}) collective-permute-start(f32[6,32,128]{2,1,0:T(8,128)S(1)} %get-tuple-element.20), channel_id=1, source_target_pairs={{32,65},{33,64},{34,67},{35,66},{36,69},{37,68},{38,71},{39,70},{4... | collective-permute-start | bytes 294920 | tf_op jit(solution)/shard_map/ppermute | solution.py:577
  62.3 16.8 %all-to-all-start.3 = ((f32[16,4,128]{2,1,0:T(4,128)}), f32[16,4,128]{2,1,0:T(4,128)S(1)}, u32[]{:S(2)}, u32[]{:S(2)}) async-start(f32[16,4,128]{2,1,0:T(4,128)} %get-tuple-element.28), calls=%async_computation.3 | async-start | bytes 65536 | tf_op jit(solution)/shard_map/all_to_all | solution.py:593

commit v4 on v3

--- a/solution.py
+++ b/solution.py
@@ -124,11 +124,11 @@
 
 def pack_kernel(
     grid_rows, own_rows, source, conductivity, shift, observed, weight,
-    slab, beside, far_a, far_b, data, sems,
+    slab, beside, far_a, far_b, data, pairs, sems,
 ):
     member = lax.axis_index("period")
     pair = (lax.axis_index("space") // 2) % 2
-    copies = []
+    copies = [(observed.at[0], pairs.at[0]), (weight.at[0], pairs.at[1])]
     rows = pl.ds(window_row(member, grid_rows, own_rows), WINDOW)
     for pol in range(2):
         copies.append((source.at[pol, :, :, rows, :], slab.at[pl.ds(3 * pol, 3)]))
@@ -142,18 +142,18 @@
     started = [pltpu.make_async_copy(a, b, sems.at[i]) for i, (a, b) in enumerate(copies)]
     for copy in started:
         copy.start()
-    for member in range(data.shape[0]):
-        data[member, 0:4, :] = observed[0]
-        data[member, 4:8, :] = weight[0]
-        data[member, 8:16, :] = jnp.full((8, LANES), shift[0], jnp.float32)
     for copy in started:
         copy.wait()
+    for member in range(data.shape[0]):
+        data[member, 0:4, :] = pairs[0]
+        data[member, 4:8, :] = pairs[1]
+        data[member, 8:16, :] = jnp.full((8, LANES), shift[0], jnp.float32)
 
 
 def pack(source, conductivity, shift, observed, weight, members):
     grid_rows = source.shape[3]
     shape = jax.ShapeDtypeStruct
-    hbm = pl.BlockSpec(memory_space=pl.ANY)
+    hbm = pl.BlockSpec(memory_space=pltpu.HBM)
     vmem = pl.BlockSpec(memory_space=pltpu.VMEM)
     smem = pl.BlockSpec(memory_space=pltpu.SMEM)
     return pl.pallas_call(
@@ -161,10 +161,10 @@
         out_shape=(shape((7, 2, WINDOW, LANES), jnp.float32),) * 2
         + (shape((6, WINDOW, LANES), jnp.float32),) * 2
         + (shape((members, 16, LANES), jnp.float32),),
-        in_specs=[hbm, hbm, smem, vmem, vmem],
+        in_specs=[hbm, hbm, smem, hbm, hbm],
         out_specs=(vmem,) * 5,
-        scratch_shapes=[pltpu.SemaphoreType.DMA((10,))],
-        compiler_params=pltpu.CompilerParams(vmem_limit_bytes=VMEM_SMALL),
+        scratch_shapes=[pltpu.VMEM((2, 4, LANES), jnp.float32), pltpu.SemaphoreType.DMA((12,))],
+        compiler_params=pltpu.CompilerParams(vmem_limit_bytes=62 * 1024 * 1024),
         name="pack",
     )(source, conductivity, shift, observed, weight)
 
@@ -375,7 +375,7 @@
             pltpu.VMEM((3, 2, 3, PLANES - 4, WINDOW, LANES), jnp.float32),
         ],
         compiler_params=pltpu.CompilerParams(vmem_limit_bytes=VMEM_LIMIT),
-        cost_estimate=pl.CostEstimate(flops=50_000_000, bytes_accessed=3_000_000, transcendentals=0),
+        cost_estimate=pl.CostEstimate(flops=20_000_000_000, bytes_accessed=3_000_000, transcendentals=0),
         name="forward_solve",
     )(*windows, *station_parts)
 
@@ -583,9 +583,12 @@
         swapped(far_a, lambda i: i ^ 2),
         swapped(far_b, lambda i: i + 2 if i & 2 else i - 2),
     )
+    mate, data = lax.optimization_barrier((windows[1], data))
+    windows = (windows[0], mate, *windows[2:])
     data = lax.all_to_all(data, "period", 0, 0, tiled=True)
     station_parts = stations(site_cells, site_weights, grid_rows, members)
     field, sent, mass = forward_solve(windows, station_parts, grid_rows, members, grid_planes)
+    sent, data = lax.optimization_barrier((sent, data))
     read = lax.all_to_all(sent, "space", 0, 0, tiled=True)
     moments, owned = residuals(read, data, site_cells, grid_rows, members)
     moments = lax.all_to_all(moments, "space", 0, 0, tiled=True)

time: 80.2 us -> 73.9 us (0.921)
  starting transfers between devices: 23.9 us -> 20.3 us
  blocking collectives: 31.9 us -> 28.7 us
  local copies, waits for them, and re-layouts: 3.72 us -> 0.94 us
  waiting for transfers between devices: 2.61 us -> 4.3 us
  Pallas kernels: 15.7 us -> 17 us
    all_to_all x1, waiting for transfers between devices: 0.01 us -> 4.29 us  [shards(): data = lax.all_to_all(data, 'period', 0, 0, tiled=True)]
    all_to_all x1, blocking collectives: 19.7 us -> 16.6 us  [shards(): read = lax.all_to_all(sent, 'space', 0, 0, tiled=True)]
    all_to_all x1, starting transfers between devices: 8.12 us -> 5.15 us  [shards(): owned = lax.all_to_all(owned, 'period', 0, 0, tiled=True)]
    unnamed x12 -> x6, local copies, waits for them, and re-layouts: 3.72 us -> 0.94 us
    ppermute x4, waiting for transfers between devices: 2.6 us -> 0.01 us  [swapped(): return lax.ppermute(values, ('space', 'period'), pairs)]
    pallas_call x1, Pallas kernels: 0.99 us -> 2.18 us  [pack(): pl.pallas_call(lambda *refs: pack_kernel(grid_rows, grid_rows // members,...]
    ppermute x4, starting transfers between devices: 5.79 us -> 4.86 us  [swapped(): return lax.ppermute(values, ('space', 'period'), pairs)]
  transfers between devices with their start and end apart: 6 -> 6, of which waited for: 1 -> 1; matrix products, arithmetic and copies ran while one was open for 0% -> 0% of each run, Pallas kernels for 18% -> 19%
where the time goes in v4:
time: 73.9 us; the launch traced here: 73.3 us
  blocking collectives  28.7 us (39%)
  starting transfers between devices  20.3 us (27%)
  Pallas kernels  17 us (23%)
  waiting for transfers between devices  4.3 us (6%)
  between operations  1.4 us (2%)
  local copies, waits for them, and re-layouts  0.94 us (1%)
    all_to_all x1, blocking collectives, shards(): read = lax.all_to_all(sent, 'space', 0, 0, tiled=True)  16.6 us
    all_to_all x1, blocking collectives, shards(): moments = lax.all_to_all(moments, 'space', 0, 0, tiled=True)  12.1 us
    all_to_all x1, starting transfers between devices, shards(): data = lax.all_to_all(data, 'period', 0, 0, tiled=True)  10.3 us
    pallas_call x1, Pallas kernels, adjoint_solve(): pl.pallas_call(lambda *refs: adjoint_kernel(grid_rows, own_rows, grid_pla...  8.76 us
    all_to_all x1, starting transfers between devices, shards(): owned = lax.all_to_all(owned, 'period', 0, 0, tiled=True)  5.15 us
    ppermute x4, starting transfers between devices, swapped(): return lax.ppermute(values, ('space', 'period'), pairs)  4.86 us
    all_to_all x1, waiting for transfers between devices, shards(): data = lax.all_to_all(data, 'period', 0, 0, tiled=True)  4.29 us
    pallas_call x1, Pallas kernels, forward_solve(): pl.pallas_call(lambda *refs: forward_kernel(grid_rows, grid_rows // membe...  4.08 us
  transfers between devices with their start and end apart: 6, of which 1 were waited for; matrix products, arithmetic and copies ran while one was open for 0% of the time, Pallas kernels for 19%

profile of v4, /device:TPU:2, one launch (start us, length us, event | category | flops | bytes accessed | tf_op | source)
XLA Modules:
  0.0 73.3 jit_solution(9064693420603198724)
XLA Ops:
  0.6 0.0 copy-start
  0.6 0.0 copy-start.1
  1.3 2.2 %pack.1 = (f32[7,2,32,128]{3,2,1,0:T(8,128)}, f32[7,2,32,128]{3,2,1,0:T(8,128)}, f32[6,32,128]{2,1,0:T(8,128)}, f32[6,32,128]{2,1,0:T(8,128)}, f32[16,16,128]{2,1,0:T(8,128)}) custom-call(f32[2,3,2,256,128]{4,3,2,1,0:T(8,128)} %refs_0_.2, f32[2,256,128]{2,1,0:T(8,128)} %refs_1_.2, f32[1]{0:T(128)S(6)} %copy.9.refs_2_, f32[1,4,128]{2,1,0:T(4,128)} %refs_3_.1, ...), custom_call_target="tpu_custom_call" | custom-call | tf_op jit(solution)/shard_map/pack/pallas_call | solution.py:159
  3.5 0.1 collective-permute-start
  3.6 0.7 collective-permute-start.1
  4.3 3.4 %collective-permute-start.2 = (f32[6,32,128]{2,1,0:T(8,128)}, f32[6,32,128]{2,1,0:T(8,128)S(1)}, u32[]{:S(2)}, u32[]{:S(2)}) collective-permute-start(f32[6,32,128]{2,1,0:T(8,128)} %get-tuple-element.25), channel_id=1, source_target_pairs={{0,33},{1,32},{2,35},{3,34},{4,37},{5,36},{6,39},{7,38},{8,41},{9,... | collective-permute-start | bytes 294920 | tf_op jit(solution)/shard_map/ppermute | solution.py:577
  7.7 0.7 collective-permute-start.3
  8.4 0.0 copy-done
  8.4 0.0 copy-done.1
  8.4 1.3 %stations.1 = (s32[16,128]{1,0:T(8,128)S(1)}, s32[1]{0:T(128)}, f32[16,32,128]{2,1,0:T(8,128)S(1)}) custom-call(s32[4,2048]{1,0:T(4,128)S(1)} %copy-done, f32[4,2048]{1,0:T(4,128)S(1)} %copy-done.1), custom_call_target="tpu_custom_call" | custom-call | flops 10000000 | bytes 200000 | tf_op jit(solution)/shard_map/stations/pallas_call | solution.py:230
  9.7 0.0 collective-permute-done.refs_1_
  9.7 10.3 %all-to-all-start = ((f32[16,16,128]{2,1,0:T(8,128)}), f32[16,16,128]{2,1,0:T(8,128)S(1)}, u32[]{:S(2)}, u32[]{:S(2)}) async-start(f32[16,16,128]{2,1,0:T(8,128)} %get-tuple-element.31), calls=%async_computation | async-start | bytes 262144 | tf_op jit(solution)/shard_map/all_to_all | solution.py:588
  20.0 0.0 collective-permute-done.2.refs_3_
  20.0 0.0 collective-permute-done.3.refs_4_
  20.0 0.0 collective-permute-done.1.refs_2_
  20.0 0.0 copy-start.2
  20.0 0.9 %copy-done.2 = f32[7,2,32,128]{3,2,1,0:T(8,128)S(1)} copy-done((f32[7,2,32,128]{3,2,1,0:T(8,128)S(1)}, f32[7,2,32,128]{3,2,1,0:T(8,128)}, u32[]{:S(2)}) %copy-start.2) | copy-done | bytes 229400
  21.0 4.1 %forward_solve.1 = (f32[4,2,3,2,32,128]{5,4,3,2,1,0:T(8,128)S(1)}, f32[16,16,128]{2,1,0:T(8,128)S(1)}, f32[6,32,128]{2,1,0:T(8,128)S(1)}) custom-call(f32[7,2,32,128]{3,2,1,0:T(8,128)S(1)} %copy-done.2, f32[7,2,32,128]{3,2,1,0:T(8,128)S(1)} %collective-permute-done.refs_1_, f32[7,2,32,128]{3,2,1,0:T(8,128)S(1)} %collective-permute-done.1.refs_2_, ...), custom_call_target="tpu_custom_call" | custom-call | flops 20000000000 | bytes 3000000 | tf_op jit(solution)/shard_map/forward_solve/pallas_call | solution.py:363
  25.1 4.3 %all-to-all-done.refs_1_ = f32[16,16,128]{2,1,0:T(8,128)S(1)} async-done(((f32[16,16,128]{2,1,0:T(8,128)}), f32[16,16,128]{2,1,0:T(8,128)S(1)}, u32[]{:S(2)}, u32[]{:S(2)}) %all-to-all-start) | async-done | bytes 131104 | tf_op jit(solution)/shard_map/all_to_all | solution.py:588
  29.3 16.6 %all_to_all.20.refs_0_ = f32[16,16,128]{2,1,0:T(8,128)S(1)} all-to-all(f32[16,16,128]{2,1,0:T(8,128)S(1)} %get-tuple-element.32), channel_id=1, replica_groups=mesh['space'=16,'period'=16] {'space'}, dimensions={0} | all-to-all | bytes 262144 | tf_op jit(solution)/shard_map/all_to_all | solution.py:592
  45.9 0.7 residuals.1
  46.6 12.1 %all_to_all.21.refs_0_ = f32[16,32,128]{2,1,0:T(8,128)S(1)} all-to-all(f32[16,32,128]{2,1,0:T(8,128)S(1)} %get-tuple-element.34), channel_id=1, replica_groups=mesh['space'=16,'period'=16] {'space'}, dimensions={0} | all-to-all | bytes 524288 | tf_op jit(solution)/shard_map/all_to_all | solution.py:594
  58.7 5.1 %all-to-all-start.3 = ((f32[16,4,128]{2,1,0:T(4,128)}), f32[16,4,128]{2,1,0:T(4,128)S(1)}, u32[]{:S(2)}, u32[]{:S(2)}) async-start(f32[16,4,128]{2,1,0:T(4,128)} %get-tuple-element.36), calls=%async_computation.3 | async-start | bytes 65536 | tf_op jit(solution)/shard_map/all_to_all | solution.py:596
  63.9 8.8 %adjoint_solve.1 = f32[2,16,128]{2,1,0:T(8,128)} custom-call(f32[16,32,128]{2,1,0:T(8,128)S(1)} %all_to_all.21.refs_0_, s32[16,128]{1,0:T(8,128)S(1)} %get-tuple-element.27.refs_5_.refs_1_, s32[1]{0:T(128)} %get-tuple-element.28.refs_6_.refs_2_, f32[16,32,128]{2,1,0:T(8,128)S(1)} %get-tuple-element.29.refs_7_.refs_3_, ...), custom_call_target="tpu_custom_call" | custom-call | flops 200000000 | bytes 3000000 | tf_op jit(solution)/shard_map/adjoint_solve/pallas_call | solution.py:543
  72.7 0.0 all-to-all-done.3
  72.7 0.6 reduce_sum.9
Async XLA Ops:
  0.6 7.7 %copy-start = (s32[4,2048]{1,0:T(4,128)S(1)}, s32[4,2048]{1,0:T(4,128)}, u32[]{:S(2)}) copy-start(s32[4,2048]{1,0:T(4,128)} %refs_2_.2) | copy-start | bytes 98308
  0.6 7.7 %copy-start.1 = (f32[4,2048]{1,0:T(4,128)S(1)}, f32[4,2048]{1,0:T(4,128)}, u32[]{:S(2)}) copy-start(f32[4,2048]{1,0:T(4,128)} %refs_1_.3) | copy-start | bytes 98308
  3.5 6.2 %collective-permute-start = (f32[7,2,32,128]{3,2,1,0:T(8,128)}, f32[7,2,32,128]{3,2,1,0:T(8,128)S(1)}, u32[]{:S(2)}, u32[]{:S(2)}) collective-permute-start(f32[7,2,32,128]{3,2,1,0:T(8,128)} %get-tuple-element.21.refs_0_), channel_id=1, source_target_pairs={{0,16},{1,17},{2,18},{3,19},{4,20},{5,21},{6,22},{7,23},{8,24},{9,... | collective-permute-start | bytes 688136 | tf_op jit(solution)/shard_map/ppermute | solution.py:577
  3.6 16.4 %collective-permute-start.1 = (f32[7,2,32,128]{3,2,1,0:T(8,128)}, f32[7,2,32,128]{3,2,1,0:T(8,128)S(1)}, u32[]{:S(2)}, u32[]{:S(2)}) collective-permute-start(f32[7,2,32,128]{3,2,1,0:T(8,128)} %get-tuple-element.24), channel_id=1, source_target_pairs={{16,33},{17,32},{18,35},{19,34},{20,37},{21,36},{22,39},{23,38},{2... | collective-permute-start | bytes 688136 | tf_op jit(solution)/shard_map/ppermute | solution.py:577
  4.3 15.7 %collective-permute-start.2 = (f32[6,32,128]{2,1,0:T(8,128)}, f32[6,32,128]{2,1,0:T(8,128)S(1)}, u32[]{:S(2)}, u32[]{:S(2)}) collective-permute-start(f32[6,32,128]{2,1,0:T(8,128)} %get-tuple-element.25), channel_id=1, source_target_pairs={{0,33},{1,32},{2,35},{3,34},{4,37},{5,36},{6,39},{7,38},{8,41},{9,... | collective-permute-start | bytes 294920 | tf_op jit(solution)/shard_map/ppermute | solution.py:577
  7.7 12.3 %collective-permute-start.3 = (f32[6,32,128]{2,1,0:T(8,128)}, f32[6,32,128]{2,1,0:T(8,128)S(1)}, u32[]{:S(2)}, u32[]{:S(2)}) collective-permute-start(f32[6,32,128]{2,1,0:T(8,128)} %get-tuple-element.26), channel_id=1, source_target_pairs={{32,65},{33,64},{34,67},{35,66},{36,69},{37,68},{38,71},{39,70},{4... | collective-permute-start | bytes 294920 | tf_op jit(solution)/shard_map/ppermute | solution.py:577
  9.7 19.6 %all-to-all-start = ((f32[16,16,128]{2,1,0:T(8,128)}), f32[16,16,128]{2,1,0:T(8,128)S(1)}, u32[]{:S(2)}, u32[]{:S(2)}) async-start(f32[16,16,128]{2,1,0:T(8,128)} %get-tuple-element.31), calls=%async_computation | async-start | bytes 262144 | tf_op jit(solution)/shard_map/all_to_all | solution.py:588
  20.0 0.9 %copy-start.2 = (f32[7,2,32,128]{3,2,1,0:T(8,128)S(1)}, f32[7,2,32,128]{3,2,1,0:T(8,128)}, u32[]{:S(2)}) copy-start(f32[7,2,32,128]{3,2,1,0:T(8,128)} %get-tuple-element.21.refs_0_) | copy-start | bytes 688132
  58.7 13.9 %all-to-all-start.3 = ((f32[16,4,128]{2,1,0:T(4,128)}), f32[16,4,128]{2,1,0:T(4,128)S(1)}, u32[]{:S(2)}, u32[]{:S(2)}) async-start(f32[16,4,128]{2,1,0:T(4,128)} %get-tuple-element.36), calls=%async_computation.3 | async-start | bytes 65536 | tf_op jit(solution)/shard_map/all_to_all | solution.py:596

commit v5 on v4

--- a/solution.py
+++ b/solution.py
@@ -164,9 +164,13 @@
         in_specs=[hbm, hbm, smem, hbm, hbm],
         out_specs=(vmem,) * 5,
         scratch_shapes=[pltpu.VMEM((2, 4, LANES), jnp.float32), pltpu.SemaphoreType.DMA((12,))],
-        compiler_params=pltpu.CompilerParams(vmem_limit_bytes=62 * 1024 * 1024),
+        compiler_params=pltpu.CompilerParams(vmem_limit_bytes=VMEM_SMALL),
         name="pack",
-    )(source, conductivity, shift, observed, weight)
+    )(
+        *(pltpu.with_memory_space_constraint(v, pltpu.HBM) for v in (source, conductivity)),
+        shift,
+        *(pltpu.with_memory_space_constraint(v, pltpu.HBM) for v in (observed, weight)),
+    )
 
 
 def stations_kernel(grid_rows, own_rows, cells, weights, places, count, features, marks, staged):
@@ -583,10 +587,10 @@
         swapped(far_a, lambda i: i ^ 2),
         swapped(far_b, lambda i: i + 2 if i & 2 else i - 2),
     )
-    mate, data = lax.optimization_barrier((windows[1], data))
+    mate, data, late_cells = lax.optimization_barrier((windows[1], data, site_cells))
     windows = (windows[0], mate, *windows[2:])
     data = lax.all_to_all(data, "period", 0, 0, tiled=True)
-    station_parts = stations(site_cells, site_weights, grid_rows, members)
+    station_parts = stations(late_cells, site_weights, grid_rows, members)
     field, sent, mass = forward_solve(windows, station_parts, grid_rows, members, grid_planes)
     sent, data = lax.optimization_barrier((sent, data))
     read = lax.all_to_all(sent, "space", 0, 0, tiled=True)

time: 73.9 us -> 72.2 us (0.977)
  local copies, waits for them, and re-layouts: 0.94 us -> 0.01 us
    unnamed x6 -> x4, local copies, waits for them, and re-layouts: 0.94 us -> 0.01 us
  transfers between devices with their start and end apart: 6 -> 6, of which waited for: 1 -> 1; matrix products, arithmetic and copies ran while one was open for 0% -> 0% of each run, Pallas kernels for 19% -> 20%
where the time goes in v5:
time: 72.2 us; the launch traced here: 71.7 us
  blocking collectives  28.7 us (40%)
  starting transfers between devices  20.3 us (28%)
  Pallas kernels  16.7 us (23%)
  waiting for transfers between devices  3.95 us (5%)
  between operations  1.4 us (2%)
    all_to_all x1, blocking collectives, shards(): read = lax.all_to_all(sent, 'space', 0, 0, tiled=True)  16.6 us
    all_to_all x1, blocking collectives, shards(): moments = lax.all_to_all(moments, 'space', 0, 0, tiled=True)  12.1 us
    all_to_all x1, starting transfers between devices, shards(): data = lax.all_to_all(data, 'period', 0, 0, tiled=True)  10.3 us
    pallas_call x1, Pallas kernels, adjoint_solve(): pl.pallas_call(lambda *refs: adjoint_kernel(grid_rows, own_rows, grid_pla...  8.72 us
    all_to_all x1, starting transfers between devices, shards(): owned = lax.all_to_all(owned, 'period', 0, 0, tiled=True)  5.16 us
    ppermute x4, starting transfers between devices, swapped(): return lax.ppermute(values, ('space', 'period'), pairs)  4.86 us
    pallas_call x1, Pallas kernels, forward_solve(): pl.pallas_call(lambda *refs: forward_kernel(grid_rows, grid_rows // membe...  4.06 us
    all_to_all x1, waiting for transfers between devices, shards(): data = lax.all_to_all(data, 'period', 0, 0, tiled=True)  3.94 us
  transfers between devices with their start and end apart: 6, of which 1 were waited for; matrix products, arithmetic and copies ran while one was open for 0% of the time, Pallas kernels for 20%

profile of v5, /device:TPU:2, one launch (start us, length us, event | category | flops | bytes accessed | tf_op | source)
XLA Modules:
  0.0 71.7 jit_solution(9889766333775598579)
XLA Ops:
  0.6 0.0 copy-start
  0.6 0.0 copy-start.1
  1.3 1.9 %pack.1 = (f32[7,2,32,128]{3,2,1,0:T(8,128)S(1)}, f32[7,2,32,128]{3,2,1,0:T(8,128)S(1)}, f32[6,32,128]{2,1,0:T(8,128)S(1)}, f32[6,32,128]{2,1,0:T(8,128)S(1)}, f32[16,16,128]{2,1,0:T(8,128)}) custom-call(f32[2,3,2,256,128]{4,3,2,1,0:T(8,128)} %refs_0_.1, f32[2,256,128]{2,1,0:T(8,128)} %refs_1_.2, f32[1]{0:T(128)S(6)} %copy.9.refs_2_, f32[1,4,128]{2,1,0:T(4,128)} %refs_3_.1, ...), custom_call_target="tpu_custom_call" | custom-call | tf_op jit(solution)/shard_map/pack/pallas_call | solution.py:159
  3.2 0.1 collective-permute-start
  3.3 0.7 collective-permute-start.1
  4.0 3.4 %collective-permute-start.2 = (f32[6,32,128]{2,1,0:T(8,128)S(1)}, f32[6,32,128]{2,1,0:T(8,128)S(1)}, u32[]{:S(2)}, u32[]{:S(2)}) collective-permute-start(f32[6,32,128]{2,1,0:T(8,128)S(1)} %get-tuple-element.26), channel_id=1, source_target_pairs={{0,33},{1,32},{2,35},{3,34},{4,37},{5,36},{6,39},{7,38},{8,41},{9,... | collective-permute-start | bytes 294920 | tf_op jit(solution)/shard_map/ppermute | solution.py:581
  7.5 0.7 collective-permute-start.3
  8.1 0.0 collective-permute-done.refs_1_
  8.1 10.3 %all-to-all-start = ((f32[16,16,128]{2,1,0:T(8,128)}), f32[16,16,128]{2,1,0:T(8,128)S(1)}, u32[]{:S(2)}, u32[]{:S(2)}) async-start(f32[16,16,128]{2,1,0:T(8,128)} %get-tuple-element.33), calls=%async_computation | async-start | bytes 262144 | tf_op jit(solution)/shard_map/all_to_all | solution.py:592
  18.4 0.0 copy-done
  18.4 0.0 copy-done.1
  18.4 1.3 %stations.1 = (s32[16,128]{1,0:T(8,128)S(1)}, s32[1]{0:T(128)}, f32[16,32,128]{2,1,0:T(8,128)S(1)}) custom-call(s32[4,2048]{1,0:T(4,128)S(1)} %copy-done, f32[4,2048]{1,0:T(4,128)S(1)} %copy-done.1), custom_call_target="tpu_custom_call" | custom-call | flops 10000000 | bytes 200000 | tf_op jit(solution)/shard_map/stations/pallas_call | solution.py:234
  19.7 0.0 collective-permute-done.2.refs_3_
  19.7 0.0 collective-permute-done.3.refs_4_
  19.8 0.0 collective-permute-done.1.refs_2_
  19.8 4.1 %forward_solve.1 = (f32[4,2,3,2,32,128]{5,4,3,2,1,0:T(8,128)S(1)}, f32[16,16,128]{2,1,0:T(8,128)S(1)}, f32[6,32,128]{2,1,0:T(8,128)S(1)}) custom-call(f32[7,2,32,128]{3,2,1,0:T(8,128)S(1)} %get-tuple-element.22.refs_0_, f32[7,2,32,128]{3,2,1,0:T(8,128)S(1)} %collective-permute-done.refs_1_, f32[7,2,32,128]{3,2,1,0:T(8,128)S(1)} %collective-permute-done.1.refs_2_, ...), custom_call_target="tpu_custom_call" | custom-call | flops 20000000000 | bytes 3000000 | tf_op jit(solution)/shard_map/forward_solve/pallas_call | solution.py:367
  23.8 3.9 %all-to-all-done.refs_1_ = f32[16,16,128]{2,1,0:T(8,128)S(1)} async-done(((f32[16,16,128]{2,1,0:T(8,128)}), f32[16,16,128]{2,1,0:T(8,128)S(1)}, u32[]{:S(2)}, u32[]{:S(2)}) %all-to-all-start) | async-done | bytes 131104 | tf_op jit(solution)/shard_map/all_to_all | solution.py:592
  27.8 16.6 %all_to_all.20.refs_0_ = f32[16,16,128]{2,1,0:T(8,128)S(1)} all-to-all(f32[16,16,128]{2,1,0:T(8,128)S(1)} %get-tuple-element.34), channel_id=1, replica_groups=mesh['space'=16,'period'=16] {'space'}, dimensions={0} | all-to-all | bytes 262144 | tf_op jit(solution)/shard_map/all_to_all | solution.py:596
  44.4 0.7 residuals.1
  45.0 12.1 %all_to_all.21.refs_0_ = f32[16,32,128]{2,1,0:T(8,128)S(1)} all-to-all(f32[16,32,128]{2,1,0:T(8,128)S(1)} %get-tuple-element.36), channel_id=1, replica_groups=mesh['space'=16,'period'=16] {'space'}, dimensions={0} | all-to-all | bytes 524288 | tf_op jit(solution)/shard_map/all_to_all | solution.py:598
  57.2 5.2 %all-to-all-start.3 = ((f32[16,4,128]{2,1,0:T(4,128)}), f32[16,4,128]{2,1,0:T(4,128)S(1)}, u32[]{:S(2)}, u32[]{:S(2)}) async-start(f32[16,4,128]{2,1,0:T(4,128)} %get-tuple-element.38), calls=%async_computation.3 | async-start | bytes 65536 | tf_op jit(solution)/shard_map/all_to_all | solution.py:600
  62.3 8.7 %adjoint_solve.1 = f32[2,16,128]{2,1,0:T(8,128)} custom-call(f32[16,32,128]{2,1,0:T(8,128)S(1)} %all_to_all.21.refs_0_, s32[16,128]{1,0:T(8,128)S(1)} %get-tuple-element.29.refs_5_.refs_1_, s32[1]{0:T(128)} %get-tuple-element.30.refs_6_.refs_2_, f32[16,32,128]{2,1,0:T(8,128)S(1)} %get-tuple-element.31.refs_7_.refs_3_, ...), custom_call_target="tpu_custom_call" | custom-call | flops 200000000 | bytes 3000000 | tf_op jit(solution)/shard_map/adjoint_solve/pallas_call | solution.py:547
  71.1 0.0 all-to-all-done.3
  71.1 0.6 reduce_sum.9
Async XLA Ops:
  0.6 17.8 %copy-start = (s32[4,2048]{1,0:T(4,128)S(1)}, s32[4,2048]{1,0:T(4,128)}, u32[]{:S(2)}) copy-start(s32[4,2048]{1,0:T(4,128)} %refs_2_.2) | copy-start | bytes 98308
  0.6 17.8 %copy-start.1 = (f32[4,2048]{1,0:T(4,128)S(1)}, f32[4,2048]{1,0:T(4,128)}, u32[]{:S(2)}) copy-start(f32[4,2048]{1,0:T(4,128)} %refs_1_.3) | copy-start | bytes 98308
  3.2 4.9 %collective-permute-start = (f32[7,2,32,128]{3,2,1,0:T(8,128)S(1)}, f32[7,2,32,128]{3,2,1,0:T(8,128)S(1)}, u32[]{:S(2)}, u32[]{:S(2)}) collective-permute-start(f32[7,2,32,128]{3,2,1,0:T(8,128)S(1)} %get-tuple-element.22.refs_0_), channel_id=1, source_target_pairs={{0,16},{1,17},{2,18},{3,19},{4,20},{5,21},{6,22},{7,23},{8,24},{9,... | collective-permute-start | bytes 688136 | tf_op jit(solution)/shard_map/ppermute | solution.py:581
  3.3 16.4 %collective-permute-start.1 = (f32[7,2,32,128]{3,2,1,0:T(8,128)S(1)}, f32[7,2,32,128]{3,2,1,0:T(8,128)S(1)}, u32[]{:S(2)}, u32[]{:S(2)}) collective-permute-start(f32[7,2,32,128]{3,2,1,0:T(8,128)S(1)} %get-tuple-element.25), channel_id=1, source_target_pairs={{16,33},{17,32},{18,35},{19,34},{20,37},{21,36},{22,39},{23,38},{2... | collective-permute-start | bytes 688136 | tf_op jit(solution)/shard_map/ppermute | solution.py:581
  4.0 15.7 %collective-permute-start.2 = (f32[6,32,128]{2,1,0:T(8,128)S(1)}, f32[6,32,128]{2,1,0:T(8,128)S(1)}, u32[]{:S(2)}, u32[]{:S(2)}) collective-permute-start(f32[6,32,128]{2,1,0:T(8,128)S(1)} %get-tuple-element.26), channel_id=1, source_target_pairs={{0,33},{1,32},{2,35},{3,34},{4,37},{5,36},{6,39},{7,38},{8,41},{9,... | collective-permute-start | bytes 294920 | tf_op jit(solution)/shard_map/ppermute | solution.py:581
  7.5 12.3 %collective-permute-start.3 = (f32[6,32,128]{2,1,0:T(8,128)S(1)}, f32[6,32,128]{2,1,0:T(8,128)S(1)}, u32[]{:S(2)}, u32[]{:S(2)}) collective-permute-start(f32[6,32,128]{2,1,0:T(8,128)S(1)} %get-tuple-element.27), channel_id=1, source_target_pairs={{32,65},{33,64},{34,67},{35,66},{36,69},{37,68},{38,71},{39,70},{4... | collective-permute-start | bytes 294920 | tf_op jit(solution)/shard_map/ppermute | solution.py:581
  8.1 19.6 %all-to-all-start = ((f32[16,16,128]{2,1,0:T(8,128)}), f32[16,16,128]{2,1,0:T(8,128)S(1)}, u32[]{:S(2)}, u32[]{:S(2)}) async-start(f32[16,16,128]{2,1,0:T(8,128)} %get-tuple-element.33), calls=%async_computation | async-start | bytes 262144 | tf_op jit(solution)/shard_map/all_to_all | solution.py:592
  57.2 13.9 %all-to-all-start.3 = ((f32[16,4,128]{2,1,0:T(4,128)}), f32[16,4,128]{2,1,0:T(4,128)S(1)}, u32[]{:S(2)}, u32[]{:S(2)}) async-start(f32[16,4,128]{2,1,0:T(4,128)} %get-tuple-element.38), calls=%async_computation.3 | async-start | bytes 65536 | tf_op jit(solution)/shard_map/all_to_all | solution.py:600

commit v6 on v5

--- a/solution.py
+++ b/solution.py
@@ -93,13 +93,13 @@
     return jnp.where(iota(v.shape, 0) == 0, 0.0, pltpu.roll(v, 1, 0))
 
 
-def curl_curl(get, first, last, first_plane, planes_in_grid):
+def curl_curl(get, first, last, first_plane, planes_in_grid, along_z=None):
     before = None
     here = get(first - 1)
     for plane in range(first - 1, last + 1):
         after = get(plane + 1)
         east, north, down = here
-        c2 = next_z(east) - east
+        c2 = along_z(plane, 0) if along_z else next_z(east) - east
         if down is not None:
             c2 = c2 - (after[2] - down)
         c3 = (after[1] - north) - (next_y(east) - east)
@@ -108,7 +108,7 @@
             c2 = c2 * inside
             c3 = c3 * inside
         if plane >= first:
-            c1 = north - next_z(north)
+            c1 = -along_z(plane, 1) if along_z else north - next_z(north)
             if down is not None:
                 c1 = c1 + (next_y(down) - down)
             a1 = (c3 - last_y(c3)) - (c2 - last_z(c2))
@@ -264,6 +264,13 @@
     return jnp.where(depth == feature[4:5], 1.0, 0.0).astype(jnp.bfloat16)
 
 
+def depth_picks_and_differences(feature):
+    depth = iota((LANES, LANES), 0).astype(jnp.float32)
+    here = jnp.where(depth == feature[4:5], 1.0, 0.0)
+    change = jnp.where(depth + 1.0 == feature[4:5], 1.0, 0.0) - here
+    return jnp.concatenate([here, change], axis=0).astype(jnp.bfloat16)
+
+
 def forward_kernel(
     grid_rows, own_rows, grid_planes, slab, mate, beside, far_a, far_b, places, count, features,
     field, sent, mass, window, d1, d2,
@@ -435,7 +442,7 @@
 
 def adjoint_kernel(
     grid_rows, own_rows, grid_planes, periods, moments, places, count, features, mass, field,
-    gradient, d0, d1, d2, picked, total,
+    gradient, d0, slope, d1, d2, picked, total,
 ):
     first_plane = first_window_plane()
     member = lax.axis_index("period")
@@ -448,7 +455,7 @@
     def add_chunk(chunk, fresh):
         feature = features[chunk]
         weight = row_weights(feature, 20, 0, window_rows)
-        depth = depth_picks(feature)
+        depth = depth_picks_and_differences(feature)
         depth = jnp.concatenate([depth, depth], axis=1)
         gathered = jnp.zeros((96, LANES), jnp.float32)
         for block in range(blocks):
@@ -462,12 +469,14 @@
             low = (values - high.astype(jnp.float32)).astype(jnp.bfloat16)
             placed = dot_nt(jnp.concatenate([high, low], axis=1), depth)
             if fresh:
-                d0[number] = placed
+                d0[number] = placed[:, :LANES]
+                slope[number] = placed[:, LANES:]
             else:
-                d0[number] += placed
+                d0[number] += placed[:, :LANES]
+                slope[number] += placed[:, LANES:]
             return carry
 
-        lax.fori_loop(0, 4 * MOMENTS, one_field, 0, unroll=MOMENTS)
+        lax.fori_loop(0, 4 * MOMENTS, one_field, 0, unroll=2 * MOMENTS)
 
     add_chunk(0, True)
 
@@ -484,7 +493,10 @@
         def b(plane):
             return start(f, 0, plane), start(f, 1, plane), None
 
-        for plane, here, curled in curl_curl(b, 1, 6, first_plane, grid_planes):
+        def along_z(plane, c):
+            return slope[2 * f + c, plane * NARROW : (plane + 1) * NARROW, :]
+
+        for plane, here, curled in curl_curl(b, 1, 6, first_plane, grid_planes, along_z):
             m = mass[plane - 1, inner, :]
             for c in range(2):
                 mixed = CENTER * here[c] + start(f + 2, c, plane)
@@ -494,7 +506,7 @@
             d1[f, 2, plane - 1] = -STEP[0] * curled[2]
         return carry
 
-    lax.fori_loop(0, 2 * (MOMENTS - 1), level_one, 0)
+    lax.fori_loop(0, 2 * (MOMENTS - 1), level_one, 0, unroll=4)
 
     def level_two(f, carry):
         def get(plane):
@@ -510,7 +522,7 @@
                 d2[f, c, plane - 2] = value
         return carry
 
-    lax.fori_loop(0, 2 * (MOMENTS - 2), level_two, 0)
+    lax.fori_loop(0, 2 * (MOMENTS - 2), level_two, 0, unroll=2)
 
     total[...] = jnp.zeros(total.shape, jnp.float32)
 
@@ -536,7 +548,7 @@
             total[plane - 3] += added
         return carry
 
-    lax.fori_loop(0, 2 * DEGREE, level_three, 0)
+    lax.fori_loop(0, 2 * DEGREE, level_three, 0, unroll=8)
     gradient[...] = total[:, own, :] * (-1.0 / periods)
 
 
@@ -550,6 +562,7 @@
         in_specs=[vmem, vmem, smem, vmem, vmem, vmem],
         out_specs=vmem,
         scratch_shapes=[
+            pltpu.VMEM((4 * MOMENTS, PLANES * NARROW, LANES), jnp.float32),
             pltpu.VMEM((4 * MOMENTS, PLANES * NARROW, LANES), jnp.float32),
             pltpu.VMEM((2 * (MOMENTS - 1), 3, PLANES - 2, NARROW, LANES), jnp.float32),
             pltpu.VMEM((2 * (MOMENTS - 2), 3, PLANES - 4, NARROW, LANES), jnp.float32),

time: 72.2 us -> 71.2 us (0.986)
  Pallas kernels: 16.7 us -> 14.5 us
  waiting for transfers between devices: 3.95 us -> 4.93 us
    pallas_call x1, Pallas kernels: 8.72 us -> 6.51 us  [adjoint_solve(): pl.pallas_call(lambda *refs: adjoint_kernel(grid_rows, own_rows, grid_pla...]
    all_to_all x1, waiting for transfers between devices: 0.01 us -> 0.98 us  [shards(): owned = lax.all_to_all(owned, 'period', 0, 0, tiled=True)]
  transfers between devices with their start and end apart: 6 -> 6, of which waited for: 1 -> 2; matrix products, arithmetic and copies ran while one was open for 0% -> 0% of each run, Pallas kernels for 20% -> 17%
where the time goes in v6:
time: 71.2 us; the launch traced here: 70.4 us
  blocking collectives  28.7 us (40%)
  starting transfers between devices  20.3 us (29%)
  Pallas kernels  14.5 us (20%)
  waiting for transfers between devices  4.93 us (7%)
  between operations  1.4 us (2%)
    all_to_all x1, blocking collectives, shards(): read = lax.all_to_all(sent, 'space', 0, 0, tiled=True)  16.6 us
    all_to_all x1, blocking collectives, shards(): moments = lax.all_to_all(moments, 'space', 0, 0, tiled=True)  12.1 us
    all_to_all x1, starting transfers between devices, shards(): data = lax.all_to_all(data, 'period', 0, 0, tiled=True)  10.3 us
    pallas_call x1, Pallas kernels, adjoint_solve(): pl.pallas_call(lambda *refs: adjoint_kernel(grid_rows, own_rows, grid_pla...  6.51 us
    all_to_all x1, starting transfers between devices, shards(): owned = lax.all_to_all(owned, 'period', 0, 0, tiled=True)  5.16 us
    ppermute x4, starting transfers between devices, swapped(): return lax.ppermute(values, ('space', 'period'), pairs)  4.86 us
    pallas_call x1, Pallas kernels, forward_solve(): pl.pallas_call(lambda *refs: forward_kernel(grid_rows, grid_rows // membe...  4.06 us
    all_to_all x1, waiting for transfers between devices, shards(): data = lax.all_to_all(data, 'period', 0, 0, tiled=True)  3.94 us
  transfers between devices with their start and end apart: 6, of which 2 were waited for; matrix products, arithmetic and copies ran while one was open for 0% of the time, Pallas kernels for 17%

profile of v6, /device:TPU:2, one launch (start us, length us, event | category | flops | bytes accessed | tf_op | source)
XLA Modules:
  0.0 70.4 jit_solution(10196573544010243151)
XLA Ops:
  0.6 0.0 copy-start
  0.6 0.0 copy-start.1
  1.3 1.9 %pack.1 = (f32[7,2,32,128]{3,2,1,0:T(8,128)S(1)}, f32[7,2,32,128]{3,2,1,0:T(8,128)S(1)}, f32[6,32,128]{2,1,0:T(8,128)S(1)}, f32[6,32,128]{2,1,0:T(8,128)S(1)}, f32[16,16,128]{2,1,0:T(8,128)}) custom-call(f32[2,3,2,256,128]{4,3,2,1,0:T(8,128)} %refs_0_.1, f32[2,256,128]{2,1,0:T(8,128)} %refs_1_.2, f32[1]{0:T(128)S(6)} %copy.9.refs_2_, f32[1,4,128]{2,1,0:T(4,128)} %refs_3_.1, ...), custom_call_target="tpu_custom_call" | custom-call | tf_op jit(solution)/shard_map/pack/pallas_call | solution.py:159
  3.2 0.1 collective-permute-start
  3.3 0.7 collective-permute-start.1
  4.0 3.4 %collective-permute-start.2 = (f32[6,32,128]{2,1,0:T(8,128)S(1)}, f32[6,32,128]{2,1,0:T(8,128)S(1)}, u32[]{:S(2)}, u32[]{:S(2)}) collective-permute-start(f32[6,32,128]{2,1,0:T(8,128)S(1)} %get-tuple-element.26), channel_id=1, source_target_pairs={{0,33},{1,32},{2,35},{3,34},{4,37},{5,36},{6,39},{7,38},{8,41},{9,... | collective-permute-start | bytes 294920 | tf_op jit(solution)/shard_map/ppermute | solution.py:594
  7.5 0.7 collective-permute-start.3
  8.1 0.0 collective-permute-done.refs_1_
  8.1 10.3 %all-to-all-start = ((f32[16,16,128]{2,1,0:T(8,128)}), f32[16,16,128]{2,1,0:T(8,128)S(1)}, u32[]{:S(2)}, u32[]{:S(2)}) async-start(f32[16,16,128]{2,1,0:T(8,128)} %get-tuple-element.33), calls=%async_computation | async-start | bytes 262144 | tf_op jit(solution)/shard_map/all_to_all | solution.py:605
  18.4 0.0 copy-done
  18.4 0.0 copy-done.1
  18.4 1.3 %stations.1 = (s32[16,128]{1,0:T(8,128)S(1)}, s32[1]{0:T(128)}, f32[16,32,128]{2,1,0:T(8,128)S(1)}) custom-call(s32[4,2048]{1,0:T(4,128)S(1)} %copy-done, f32[4,2048]{1,0:T(4,128)S(1)} %copy-done.1), custom_call_target="tpu_custom_call" | custom-call | flops 10000000 | bytes 200000 | tf_op jit(solution)/shard_map/stations/pallas_call | solution.py:234
  19.7 0.0 collective-permute-done.2.refs_3_
  19.7 0.0 collective-permute-done.3.refs_4_
  19.8 0.0 collective-permute-done.1.refs_2_
  19.8 4.1 %forward_solve.1 = (f32[4,2,3,2,32,128]{5,4,3,2,1,0:T(8,128)S(1)}, f32[16,16,128]{2,1,0:T(8,128)S(1)}, f32[6,32,128]{2,1,0:T(8,128)S(1)}) custom-call(f32[7,2,32,128]{3,2,1,0:T(8,128)S(1)} %get-tuple-element.22.refs_0_, f32[7,2,32,128]{3,2,1,0:T(8,128)S(1)} %collective-permute-done.refs_1_, f32[7,2,32,128]{3,2,1,0:T(8,128)S(1)} %collective-permute-done.1.refs_2_, ...), custom_call_target="tpu_custom_call" | custom-call | flops 20000000000 | bytes 3000000 | tf_op jit(solution)/shard_map/forward_solve/pallas_call | solution.py:374
  23.8 3.9 %all-to-all-done.refs_1_ = f32[16,16,128]{2,1,0:T(8,128)S(1)} async-done(((f32[16,16,128]{2,1,0:T(8,128)}), f32[16,16,128]{2,1,0:T(8,128)S(1)}, u32[]{:S(2)}, u32[]{:S(2)}) %all-to-all-start) | async-done | bytes 131104 | tf_op jit(solution)/shard_map/all_to_all | solution.py:605
  27.8 16.6 %all_to_all.20.refs_0_ = f32[16,16,128]{2,1,0:T(8,128)S(1)} all-to-all(f32[16,16,128]{2,1,0:T(8,128)S(1)} %get-tuple-element.34), channel_id=1, replica_groups=mesh['space'=16,'period'=16] {'space'}, dimensions={0} | all-to-all | bytes 262144 | tf_op jit(solution)/shard_map/all_to_all | solution.py:609
  44.4 0.7 residuals.1
  45.0 12.1 %all_to_all.21.refs_0_ = f32[16,32,128]{2,1,0:T(8,128)S(1)} all-to-all(f32[16,32,128]{2,1,0:T(8,128)S(1)} %get-tuple-element.36), channel_id=1, replica_groups=mesh['space'=16,'period'=16] {'space'}, dimensions={0} | all-to-all | bytes 524288 | tf_op jit(solution)/shard_map/all_to_all | solution.py:611
  57.2 5.2 %all-to-all-start.3 = ((f32[16,4,128]{2,1,0:T(4,128)}), f32[16,4,128]{2,1,0:T(4,128)S(1)}, u32[]{:S(2)}, u32[]{:S(2)}) async-start(f32[16,4,128]{2,1,0:T(4,128)} %get-tuple-element.38), calls=%async_computation.3 | async-start | bytes 65536 | tf_op jit(solution)/shard_map/all_to_all | solution.py:613
  62.3 6.5 %adjoint_solve.1 = f32[2,16,128]{2,1,0:T(8,128)} custom-call(f32[16,32,128]{2,1,0:T(8,128)S(1)} %all_to_all.21.refs_0_, s32[16,128]{1,0:T(8,128)S(1)} %get-tuple-element.29.refs_5_.refs_1_, s32[1]{0:T(128)} %get-tuple-element.30.refs_6_.refs_2_, f32[16,32,128]{2,1,0:T(8,128)S(1)} %get-tuple-element.31.refs_7_.refs_3_, ...), custom_call_target="tpu_custom_call" | custom-call | flops 200000000 | bytes 3000000 | tf_op jit(solution)/shard_map/adjoint_solve/pallas_call | solution.py:559
  68.8 1.0 %all-to-all-done.3 = f32[16,4,128]{2,1,0:T(4,128)S(1)} async-done(((f32[16,4,128]{2,1,0:T(4,128)}), f32[16,4,128]{2,1,0:T(4,128)S(1)}, u32[]{:S(2)}, u32[]{:S(2)}) %all-to-all-start.3) | async-done | bytes 32800 | tf_op jit(solution)/shard_map/all_to_all | solution.py:613
  69.8 0.6 reduce_sum.9
Async XLA Ops:
  0.6 17.8 %copy-start = (s32[4,2048]{1,0:T(4,128)S(1)}, s32[4,2048]{1,0:T(4,128)}, u32[]{:S(2)}) copy-start(s32[4,2048]{1,0:T(4,128)} %refs_2_.2) | copy-start | bytes 98308
  0.6 17.8 %copy-start.1 = (f32[4,2048]{1,0:T(4,128)S(1)}, f32[4,2048]{1,0:T(4,128)}, u32[]{:S(2)}) copy-start(f32[4,2048]{1,0:T(4,128)} %refs_1_.3) | copy-start | bytes 98308
  3.2 4.9 %collective-permute-start = (f32[7,2,32,128]{3,2,1,0:T(8,128)S(1)}, f32[7,2,32,128]{3,2,1,0:T(8,128)S(1)}, u32[]{:S(2)}, u32[]{:S(2)}) collective-permute-start(f32[7,2,32,128]{3,2,1,0:T(8,128)S(1)} %get-tuple-element.22.refs_0_), channel_id=1, source_target_pairs={{0,16},{1,17},{2,18},{3,19},{4,20},{5,21},{6,22},{7,23},{8,24},{9,... | collective-permute-start | bytes 688136 | tf_op jit(solution)/shard_map/ppermute | solution.py:594
  3.3 16.4 %collective-permute-start.1 = (f32[7,2,32,128]{3,2,1,0:T(8,128)S(1)}, f32[7,2,32,128]{3,2,1,0:T(8,128)S(1)}, u32[]{:S(2)}, u32[]{:S(2)}) collective-permute-start(f32[7,2,32,128]{3,2,1,0:T(8,128)S(1)} %get-tuple-element.25), channel_id=1, source_target_pairs={{16,33},{17,32},{18,35},{19,34},{20,37},{21,36},{22,39},{23,38},{2... | collective-permute-start | bytes 688136 | tf_op jit(solution)/shard_map/ppermute | solution.py:594
  4.0 15.7 %collective-permute-start.2 = (f32[6,32,128]{2,1,0:T(8,128)S(1)}, f32[6,32,128]{2,1,0:T(8,128)S(1)}, u32[]{:S(2)}, u32[]{:S(2)}) collective-permute-start(f32[6,32,128]{2,1,0:T(8,128)S(1)} %get-tuple-element.26), channel_id=1, source_target_pairs={{0,33},{1,32},{2,35},{3,34},{4,37},{5,36},{6,39},{7,38},{8,41},{9,... | collective-permute-start | bytes 294920 | tf_op jit(solution)/shard_map/ppermute | solution.py:594
  7.5 12.3 %collective-permute-start.3 = (f32[6,32,128]{2,1,0:T(8,128)S(1)}, f32[6,32,128]{2,1,0:T(8,128)S(1)}, u32[]{:S(2)}, u32[]{:S(2)}) collective-permute-start(f32[6,32,128]{2,1,0:T(8,128)S(1)} %get-tuple-element.27), channel_id=1, source_target_pairs={{32,65},{33,64},{34,67},{35,66},{36,69},{37,68},{38,71},{39,70},{4... | collective-permute-start | bytes 294920 | tf_op jit(solution)/shard_map/ppermute | solution.py:594
  8.1 19.6 %all-to-all-start = ((f32[16,16,128]{2,1,0:T(8,128)}), f32[16,16,128]{2,1,0:T(8,128)S(1)}, u32[]{:S(2)}, u32[]{:S(2)}) async-start(f32[16,16,128]{2,1,0:T(8,128)} %get-tuple-element.33), calls=%async_computation | async-start | bytes 262144 | tf_op jit(solution)/shard_map/all_to_all | solution.py:605
  57.2 12.6 %all-to-all-start.3 = ((f32[16,4,128]{2,1,0:T(4,128)}), f32[16,4,128]{2,1,0:T(4,128)S(1)}, u32[]{:S(2)}, u32[]{:S(2)}) async-start(f32[16,4,128]{2,1,0:T(4,128)} %get-tuple-element.38), calls=%async_computation.3 | async-start | bytes 65536 | tf_op jit(solution)/shard_map/all_to_all | solution.py:613

commit v7 on v6

--- a/solution.py
+++ b/solution.py
@@ -124,10 +124,10 @@
 
 def pack_kernel(
     grid_rows, own_rows, source, conductivity, shift, observed, weight,
-    slab, beside, far_a, far_b, data, pairs, sems,
+    slab, beside, far, data, pairs, sems,
 ):
     member = lax.axis_index("period")
-    pair = (lax.axis_index("space") // 2) % 2
+    odd = lax.axis_index("space") % 2
     copies = [(observed.at[0], pairs.at[0]), (weight.at[0], pairs.at[1])]
     rows = pl.ds(window_row(member, grid_rows, own_rows), WINDOW)
     for pol in range(2):
@@ -136,8 +136,7 @@
     rows = pl.ds(window_row(member + 1 - 2 * (member % 2), grid_rows, own_rows), WINDOW)
     for pol in range(2):
         copies.append((source.at[pol, :, :, rows, :], beside.at[pl.ds(3 * pol, 3)]))
-        copies.append((source.at[pol, :, 1 - pair, rows, :], far_a.at[pl.ds(3 * pol, 3)]))
-        copies.append((source.at[pol, :, pair, rows, :], far_b.at[pl.ds(3 * pol, 3)]))
+        copies.append((source.at[pol, :, 1 - odd, rows, :], far.at[pl.ds(3 * pol, 3)]))
     copies.append((conductivity.at[:, rows, :], beside.at[6]))
     started = [pltpu.make_async_copy(a, b, sems.at[i]) for i, (a, b) in enumerate(copies)]
     for copy in started:
@@ -159,11 +158,11 @@
     return pl.pallas_call(
         lambda *refs: pack_kernel(grid_rows, grid_rows // members, *refs),
         out_shape=(shape((7, 2, WINDOW, LANES), jnp.float32),) * 2
-        + (shape((6, WINDOW, LANES), jnp.float32),) * 2
+        + (shape((6, WINDOW, LANES), jnp.float32),)
         + (shape((members, 16, LANES), jnp.float32),),
         in_specs=[hbm, hbm, smem, hbm, hbm],
-        out_specs=(vmem,) * 5,
-        scratch_shapes=[pltpu.VMEM((2, 4, LANES), jnp.float32), pltpu.SemaphoreType.DMA((12,))],
+        out_specs=(vmem,) * 4,
+        scratch_shapes=[pltpu.VMEM((2, 4, LANES), jnp.float32), pltpu.SemaphoreType.DMA((10,))],
         compiler_params=pltpu.CompilerParams(vmem_limit_bytes=VMEM_SMALL),
         name="pack",
     )(
@@ -272,19 +271,18 @@
 
 
 def forward_kernel(
-    grid_rows, own_rows, grid_planes, slab, mate, beside, far_a, far_b, places, count, features,
+    grid_rows, own_rows, grid_planes, slab, mate, beside, far, relay, places, count, features,
     field, sent, mass, window, d1, d2,
 ):
     first_plane = first_window_plane()
     even = lax.axis_index("space") % 2 == 0
-    lower = (lax.axis_index("space") // 2) % 2 == 0
     for plane in range(2):
         here, there = mate[:, plane], beside[:, plane]
         window[:, 1 + plane] = jnp.where(even, there, here)
         window[:, 3 + plane] = slab[:, plane]
         window[:, 5 + plane] = jnp.where(even, here, there)
-    window[0:6, 0] = jnp.where(lower, far_b[...], far_a[...])
-    window[0:6, PLANES - 1] = jnp.where(lower, far_a[...], far_b[...])
+    window[0:6, 0] = jnp.where(even, far[...], relay[0:6, 1])
+    window[0:6, PLANES - 1] = jnp.where(even, relay[0:6, 0], far[...])
     mass[...] = window[6, 1 : PLANES - 1]
 
     def part(number, plane):
@@ -580,7 +578,7 @@
     count = lax.axis_size("space")
     members = lax.axis_size("period")
     grid_planes = conductivity.shape[0] * count
-    slab, beside, far_a, far_b, data = pack(
+    slab, beside, far, data = pack(
         source, conductivity, period_shift, observed, data_weight, members
     )
 
@@ -593,17 +591,15 @@
                 pairs += [(i * members + t, j * members + (t ^ flip)) for t in range(members)]
         return lax.ppermute(values, ("space", "period"), pairs)
 
-    windows = (
-        slab,
-        swapped(slab, lambda i: i ^ 1),
-        swapped(beside, lambda i: i + 1 if i % 2 else i - 1),
-        swapped(far_a, lambda i: i ^ 2),
-        swapped(far_b, lambda i: i + 2 if i & 2 else i - 2),
-    )
-    mate, data, late_cells = lax.optimization_barrier((windows[1], data, site_cells))
-    windows = (windows[0], mate, *windows[2:])
+    mate = swapped(slab, lambda i: i ^ 1)
+    beside = swapped(beside, lambda i: i + 1 if i % 2 else i - 1)
+    far = swapped(far, lambda i: i - 2 if i % 2 else i + 2)
+    mate, data, late_cells = lax.optimization_barrier((mate, data, site_cells))
     data = lax.all_to_all(data, "period", 0, 0, tiled=True)
-    station_parts = stations(late_cells, site_weights, grid_rows, members)
+    places, *lists = stations(late_cells, site_weights, grid_rows, members)
+    beside, far, places = lax.optimization_barrier((beside, far, places))
+    station_parts = (places, *lists)
+    windows = (slab, mate, beside, far, swapped(beside, lambda i: i ^ 1))
     field, sent, mass = forward_solve(windows, station_parts, grid_rows, members, grid_planes)
     sent, data = lax.optimization_barrier((sent, data))
     read = lax.all_to_all(sent, "space", 0, 0, tiled=True)

time: 71.2 us -> 76.3 us (1.072)
  starting transfers between devices: 20.3 us -> 25.4 us
  waiting for transfers between devices: 4.93 us -> 6.38 us
  blocking collectives: 28.7 us -> 27.5 us
    ppermute x4, starting transfers between devices: 4.86 us -> 10.3 us  [swapped(): return lax.ppermute(values, ('space', 'period'), pairs)]
    all_to_all x1, blocking collectives: 16.6 us -> 15.3 us  [shards(): read = lax.all_to_all(sent, 'space', 0, 0, tiled=True)]
    ppermute x4, waiting for transfers between devices: 0.01 us -> 0.88 us  [swapped(): return lax.ppermute(values, ('space', 'period'), pairs)]
  transfers between devices with their start and end apart: 6 -> 6, of which waited for: 2 -> 3; matrix products, arithmetic and copies ran while one was open for 0% -> 0% of each run, Pallas kernels for 17% -> 16%
where the time goes in v7:
time: 76.3 us; the launch traced here: 75.6 us
  blocking collectives  27.5 us (36%)
  starting transfers between devices  25.4 us (33%)
  Pallas kernels  14.4 us (19%)
  waiting for transfers between devices  6.38 us (8%)
  between operations  1.38 us (2%)
    all_to_all x1, blocking collectives, shards(): read = lax.all_to_all(sent, 'space', 0, 0, tiled=True)  15.3 us
    all_to_all x1, blocking collectives, shards(): moments = lax.all_to_all(moments, 'space', 0, 0, tiled=True)  12.1 us
    ppermute x4, starting transfers between devices, swapped(): return lax.ppermute(values, ('space', 'period'), pairs)  10.3 us
    all_to_all x1, starting transfers between devices, shards(): data = lax.all_to_all(data, 'period', 0, 0, tiled=True)  9.96 us
    pallas_call x1, Pallas kernels, adjoint_solve(): pl.pallas_call(lambda *refs: adjoint_kernel(grid_rows, own_rows, grid_pla...  6.51 us
    all_to_all x1, starting transfers between devices, shards(): owned = lax.all_to_all(owned, 'period', 0, 0, tiled=True)  5.11 us
    all_to_all x1, waiting for transfers between devices, shards(): data = lax.all_to_all(data, 'period', 0, 0, tiled=True)  4.53 us
    pallas_call x1, Pallas kernels, forward_solve(): pl.pallas_call(lambda *refs: forward_kernel(grid_rows, grid_rows // membe...  4.06 us
  transfers between devices with their start and end apart: 6, of which 3 were waited for; matrix products, arithmetic and copies ran while one was open for 0% of the time, Pallas kernels for 16%

profile of v7, /device:TPU:2, one launch (start us, length us, event | category | flops | bytes accessed | tf_op | source)
XLA Modules:
  0.0 75.6 jit_solution(49880465750816474)
XLA Ops:
  0.6 0.0 copy-start
  0.6 0.0 copy-start.1
  1.3 1.9 %pack.1 = (f32[7,2,32,128]{3,2,1,0:T(8,128)S(1)}, f32[7,2,32,128]{3,2,1,0:T(8,128)S(1)}, f32[6,32,128]{2,1,0:T(8,128)S(1)}, f32[16,16,128]{2,1,0:T(8,128)}) custom-call(f32[2,3,2,256,128]{4,3,2,1,0:T(8,128)} %refs_0_.1, f32[2,256,128]{2,1,0:T(8,128)} %refs_1_.2, f32[1]{0:T(128)S(6)} %copy.9.refs_2_, f32[1,4,128]{2,1,0:T(4,128)} %refs_3_.1, f32[1,4,128]{2,1,0:T(4,128)} %refs_4_.1), custom_call_target="tpu_custom_call" | custom-call | tf_op jit(solution)/shard_map/pack/pallas_call | solution.py:158
  3.2 0.1 collective-permute-start
  3.3 0.7 collective-permute-start.1
  4.0 5.3 %collective-permute-start.2 = (f32[6,32,128]{2,1,0:T(8,128)S(1)}, f32[6,32,128]{2,1,0:T(8,128)S(1)}, u32[]{:S(2)}, u32[]{:S(2)}) collective-permute-start(f32[6,32,128]{2,1,0:T(8,128)S(1)} %get-tuple-element.28), channel_id=1, source_target_pairs={{0,33},{1,32},{2,35},{3,34},{4,37},{5,36},{6,39},{7,38},{8,41},{9,... | collective-permute-start | bytes 294920 | tf_op jit(solution)/shard_map/ppermute | solution.py:592
  9.2 0.0 collective-permute-done.refs_1_
  9.2 0.0 copy-done
  9.3 0.0 copy-done.1
  9.3 1.3 %stations.1 = (s32[16,128]{1,0:T(8,128)S(1)}, s32[1]{0:T(128)}, f32[16,32,128]{2,1,0:T(8,128)S(1)}) custom-call(s32[4,2048]{1,0:T(4,128)S(1)} %copy-done, f32[4,2048]{1,0:T(4,128)S(1)} %copy-done.1), custom_call_target="tpu_custom_call" | custom-call | flops 10000000 | bytes 200000 | tf_op jit(solution)/shard_map/stations/pallas_call | solution.py:233
  10.6 0.9 %collective-permute-done.2.refs_3_ = f32[6,32,128]{2,1,0:T(8,128)S(1)} collective-permute-done((f32[6,32,128]{2,1,0:T(8,128)S(1)}, f32[6,32,128]{2,1,0:T(8,128)S(1)}, u32[]{:S(2)}, u32[]{:S(2)}) %collective-permute-start.2) | collective-permute-done | bytes 98336 | tf_op jit(solution)/shard_map/ppermute | solution.py:592
  11.4 0.0 collective-permute-done.1.refs_2_
  11.4 4.3 %collective-permute-start.3 = (f32[7,2,32,128]{3,2,1,0:T(8,128)S(1)}, f32[7,2,32,128]{3,2,1,0:T(8,128)S(1)}, u32[]{:S(2)}, u32[]{:S(2)}) collective-permute-start(f32[7,2,32,128]{3,2,1,0:T(8,128)S(1)} %collective-permute-done.1.refs_2_), channel_id=1, source_target_pairs={{0,16},{1,17},{2,18},{3,19},{4,20},{5,21},{6,22},{7,23},{8,24},{9,... | collective-permute-start | bytes 688136 | tf_op jit(solution)/shard_map/ppermute | solution.py:592
  15.7 10.0 %all-to-all-start = ((f32[16,16,128]{2,1,0:T(8,128)}), f32[16,16,128]{2,1,0:T(8,128)S(1)}, u32[]{:S(2)}, u32[]{:S(2)}) async-start(f32[16,16,128]{2,1,0:T(8,128)} %get-tuple-element.37), calls=%async_computation | async-start | bytes 262144 | tf_op jit(solution)/shard_map/all_to_all | solution.py:598
  25.6 0.0 collective-permute-done.3.refs_4_
  25.6 4.1 %forward_solve.1 = (f32[4,2,3,2,32,128]{5,4,3,2,1,0:T(8,128)S(1)}, f32[16,16,128]{2,1,0:T(8,128)S(1)}, f32[6,32,128]{2,1,0:T(8,128)S(1)}) custom-call(f32[7,2,32,128]{3,2,1,0:T(8,128)S(1)} %get-tuple-element.24.refs_0_, f32[7,2,32,128]{3,2,1,0:T(8,128)S(1)} %collective-permute-done.refs_1_, f32[7,2,32,128]{3,2,1,0:T(8,128)S(1)} %collective-permute-done.1.refs_2_, ...), custom_call_target="tpu_custom_call" | custom-call | flops 20000000000 | bytes 3000000 | tf_op jit(solution)/shard_map/forward_solve/pallas_call | solution.py:372
  29.7 4.5 %all-to-all-done.refs_1_ = f32[16,16,128]{2,1,0:T(8,128)S(1)} async-done(((f32[16,16,128]{2,1,0:T(8,128)}), f32[16,16,128]{2,1,0:T(8,128)S(1)}, u32[]{:S(2)}, u32[]{:S(2)}) %all-to-all-start) | async-done | bytes 131104 | tf_op jit(solution)/shard_map/all_to_all | solution.py:598
  34.2 15.3 %all_to_all.20.refs_0_ = f32[16,16,128]{2,1,0:T(8,128)S(1)} all-to-all(f32[16,16,128]{2,1,0:T(8,128)S(1)} %get-tuple-element.38), channel_id=1, replica_groups=mesh['space'=16,'period'=16] {'space'}, dimensions={0} | all-to-all | bytes 262144 | tf_op jit(solution)/shard_map/all_to_all | solution.py:605
  49.6 0.7 residuals.1
  50.3 12.1 %all_to_all.21.refs_0_ = f32[16,32,128]{2,1,0:T(8,128)S(1)} all-to-all(f32[16,32,128]{2,1,0:T(8,128)S(1)} %get-tuple-element.40), channel_id=1, replica_groups=mesh['space'=16,'period'=16] {'space'}, dimensions={0} | all-to-all | bytes 524288 | tf_op jit(solution)/shard_map/all_to_all | solution.py:607
  62.4 5.1 %all-to-all-start.3 = ((f32[16,4,128]{2,1,0:T(4,128)}), f32[16,4,128]{2,1,0:T(4,128)S(1)}, u32[]{:S(2)}, u32[]{:S(2)}) async-start(f32[16,4,128]{2,1,0:T(4,128)} %get-tuple-element.42), calls=%async_computation.3 | async-start | bytes 65536 | tf_op jit(solution)/shard_map/all_to_all | solution.py:609
  67.5 6.5 %adjoint_solve.1 = f32[2,16,128]{2,1,0:T(8,128)} custom-call(f32[16,32,128]{2,1,0:T(8,128)S(1)} %all_to_all.21.refs_0_, s32[16,128]{1,0:T(8,128)S(1)} %get-tuple-element.33.refs_5_.refs_1_, s32[1]{0:T(128)} %get-tuple-element.34.refs_6_.refs_2_, f32[16,32,128]{2,1,0:T(8,128)S(1)} %get-tuple-element.35.refs_7_.refs_3_, ...), custom_call_target="tpu_custom_call" | custom-call | flops 200000000 | bytes 3000000 | tf_op jit(solution)/shard_map/adjoint_solve/pallas_call | solution.py:557
  74.0 1.0 %all-to-all-done.3 = f32[16,4,128]{2,1,0:T(4,128)S(1)} async-done(((f32[16,4,128]{2,1,0:T(4,128)}), f32[16,4,128]{2,1,0:T(4,128)S(1)}, u32[]{:S(2)}, u32[]{:S(2)}) %all-to-all-start.3) | async-done | bytes 32800 | tf_op jit(solution)/shard_map/all_to_all | solution.py:609
  75.0 0.6 reduce_sum.9
Async XLA Ops:
  0.6 8.6 %copy-start = (s32[4,2048]{1,0:T(4,128)S(1)}, s32[4,2048]{1,0:T(4,128)}, u32[]{:S(2)}) copy-start(s32[4,2048]{1,0:T(4,128)} %refs_2_.2) | copy-start | bytes 98308
  0.6 8.6 %copy-start.1 = (f32[4,2048]{1,0:T(4,128)S(1)}, f32[4,2048]{1,0:T(4,128)}, u32[]{:S(2)}) copy-start(f32[4,2048]{1,0:T(4,128)} %refs_1_.3) | copy-start | bytes 98308
  3.2 6.1 %collective-permute-start = (f32[7,2,32,128]{3,2,1,0:T(8,128)S(1)}, f32[7,2,32,128]{3,2,1,0:T(8,128)S(1)}, u32[]{:S(2)}, u32[]{:S(2)}) collective-permute-start(f32[7,2,32,128]{3,2,1,0:T(8,128)S(1)} %get-tuple-element.24.refs_0_), channel_id=1, source_target_pairs={{0,16},{1,17},{2,18},{3,19},{4,20},{5,21},{6,22},{7,23},{8,24},{9,... | collective-permute-start | bytes 688136 | tf_op jit(solution)/shard_map/ppermute | solution.py:592
  3.3 8.1 %collective-permute-start.1 = (f32[7,2,32,128]{3,2,1,0:T(8,128)S(1)}, f32[7,2,32,128]{3,2,1,0:T(8,128)S(1)}, u32[]{:S(2)}, u32[]{:S(2)}) collective-permute-start(f32[7,2,32,128]{3,2,1,0:T(8,128)S(1)} %get-tuple-element.27), channel_id=1, source_target_pairs={{16,33},{17,32},{18,35},{19,34},{20,37},{21,36},{22,39},{23,38},{2... | collective-permute-start | bytes 688136 | tf_op jit(solution)/shard_map/ppermute | solution.py:592
  4.0 7.5 %collective-permute-start.2 = (f32[6,32,128]{2,1,0:T(8,128)S(1)}, f32[6,32,128]{2,1,0:T(8,128)S(1)}, u32[]{:S(2)}, u32[]{:S(2)}) collective-permute-start(f32[6,32,128]{2,1,0:T(8,128)S(1)} %get-tuple-element.28), channel_id=1, source_target_pairs={{0,33},{1,32},{2,35},{3,34},{4,37},{5,36},{6,39},{7,38},{8,41},{9,... | collective-permute-start | bytes 294920 | tf_op jit(solution)/shard_map/ppermute | solution.py:592
  11.4 14.2 %collective-permute-start.3 = (f32[7,2,32,128]{3,2,1,0:T(8,128)S(1)}, f32[7,2,32,128]{3,2,1,0:T(8,128)S(1)}, u32[]{:S(2)}, u32[]{:S(2)}) collective-permute-start(f32[7,2,32,128]{3,2,1,0:T(8,128)S(1)} %collective-permute-done.1.refs_2_), channel_id=1, source_target_pairs={{0,16},{1,17},{2,18},{3,19},{4,20},{5,21},{6,22},{7,23},{8,24},{9,... | collective-permute-start | bytes 688136 | tf_op jit(solution)/shard_map/ppermute | solution.py:592
  15.7 18.6 %all-to-all-start = ((f32[16,16,128]{2,1,0:T(8,128)}), f32[16,16,128]{2,1,0:T(8,128)S(1)}, u32[]{:S(2)}, u32[]{:S(2)}) async-start(f32[16,16,128]{2,1,0:T(8,128)} %get-tuple-element.37), calls=%async_computation | async-start | bytes 262144 | tf_op jit(solution)/shard_map/all_to_all | solution.py:598
  62.4 12.6 %all-to-all-start.3 = ((f32[16,4,128]{2,1,0:T(4,128)}), f32[16,4,128]{2,1,0:T(4,128)S(1)}, u32[]{:S(2)}, u32[]{:S(2)}) async-start(f32[16,4,128]{2,1,0:T(4,128)} %get-tuple-element.42), calls=%async_computation.3 | async-start | bytes 65536 | tf_op jit(solution)/shard_map/all_to_all | solution.py:609

commit v8 on v7

--- a/solution.py
+++ b/solution.py
@@ -124,7 +124,7 @@
 
 def pack_kernel(
     grid_rows, own_rows, source, conductivity, shift, observed, weight,
-    slab, beside, far, data, pairs, sems,
+    slab, beside, data, pairs, sems,
 ):
     member = lax.axis_index("period")
     odd = lax.axis_index("space") % 2
@@ -136,7 +136,9 @@
     rows = pl.ds(window_row(member + 1 - 2 * (member % 2), grid_rows, own_rows), WINDOW)
     for pol in range(2):
         copies.append((source.at[pol, :, :, rows, :], beside.at[pl.ds(3 * pol, 3)]))
-        copies.append((source.at[pol, :, 1 - odd, rows, :], far.at[pl.ds(3 * pol, 3)]))
+        for c in range(3):
+            number = 3 * pol + c
+            copies.append((source.at[pol, c, 1 - odd, rows, :], slab.at[7 + number // 2, number % 2]))
     copies.append((conductivity.at[:, rows, :], beside.at[6]))
     started = [pltpu.make_async_copy(a, b, sems.at[i]) for i, (a, b) in enumerate(copies)]
     for copy in started:
@@ -157,12 +159,14 @@
     smem = pl.BlockSpec(memory_space=pltpu.SMEM)
     return pl.pallas_call(
         lambda *refs: pack_kernel(grid_rows, grid_rows // members, *refs),
-        out_shape=(shape((7, 2, WINDOW, LANES), jnp.float32),) * 2
-        + (shape((6, WINDOW, LANES), jnp.float32),)
+        out_shape=(
+            shape((10, 2, WINDOW, LANES), jnp.float32),
+            shape((7, 2, WINDOW, LANES), jnp.float32),
+        )
         + (shape((members, 16, LANES), jnp.float32),),
         in_specs=[hbm, hbm, smem, hbm, hbm],
-        out_specs=(vmem,) * 4,
-        scratch_shapes=[pltpu.VMEM((2, 4, LANES), jnp.float32), pltpu.SemaphoreType.DMA((10,))],
+        out_specs=(vmem,) * 3,
+        scratch_shapes=[pltpu.VMEM((2, 4, LANES), jnp.float32), pltpu.SemaphoreType.DMA((14,))],
         compiler_params=pltpu.CompilerParams(vmem_limit_bytes=VMEM_SMALL),
         name="pack",
     )(
@@ -170,6 +174,23 @@
         shift,
         *(pltpu.with_memory_space_constraint(v, pltpu.HBM) for v in (observed, weight)),
     )
+
+
+def extend_kernel(beside, mate, payload):
+    payload[0:7] = beside[...]
+    payload[7:10] = mate[7:10]
+
+
+def extend(beside, mate):
+    vmem = pl.BlockSpec(memory_space=pltpu.VMEM)
+    return pl.pallas_call(
+        extend_kernel,
+        out_shape=jax.ShapeDtypeStruct((10, 2, WINDOW, LANES), jnp.float32),
+        in_specs=[vmem, vmem],
+        out_specs=vmem,
+        compiler_params=pltpu.CompilerParams(vmem_limit_bytes=VMEM_SMALL),
+        name="extend",
+    )(beside, mate)
 
 
 def stations_kernel(grid_rows, own_rows, cells, weights, places, count, features, marks, staged):
@@ -271,18 +292,19 @@
 
 
 def forward_kernel(
-    grid_rows, own_rows, grid_planes, slab, mate, beside, far, relay, places, count, features,
+    grid_rows, own_rows, grid_planes, slab, mate, beside, relay, places, count, features,
     field, sent, mass, window, d1, d2,
 ):
     first_plane = first_window_plane()
     even = lax.axis_index("space") % 2 == 0
     for plane in range(2):
-        here, there = mate[:, plane], beside[:, plane]
+        here, there = mate[0:7, plane], beside[0:7, plane]
         window[:, 1 + plane] = jnp.where(even, there, here)
-        window[:, 3 + plane] = slab[:, plane]
+        window[:, 3 + plane] = slab[0:7, plane]
         window[:, 5 + plane] = jnp.where(even, here, there)
-    window[0:6, 0] = jnp.where(even, far[...], relay[0:6, 1])
-    window[0:6, PLANES - 1] = jnp.where(even, relay[0:6, 0], far[...])
+    far = beside[7:10].reshape(6, WINDOW, LANES)
+    window[0:6, 0] = jnp.where(even, far, relay[0:6, 1])
+    window[0:6, PLANES - 1] = jnp.where(even, relay[0:6, 0], far)
     mass[...] = window[6, 1 : PLANES - 1]
 
     def part(number, plane):
@@ -348,12 +370,13 @@
         weight = row_weights(feature, 0, HALO * WINDOW, 2 * WINDOW)
         depth = depth_picks(feature)
         rows = []
+        stacked = jnp.concatenate([depth] * 3, axis=0)
         for j in range(DEGREE):
-            for pol in range(2):
-                for c in range(2):
-                    values = field[j, pol, c].reshape(2 * WINDOW, LANES)
-                    at_depth = sum(dot_nn(piece, depth) for piece in parts_of(values))
-                    rows.append(jnp.sum(at_depth * weight, axis=0, keepdims=True))
+            values = field[j, :, 0:2].reshape(8 * WINDOW, LANES)
+            at_depth = dot_nn(jnp.concatenate(parts_of(values), axis=1), stacked)
+            for number in range(4):
+                part = at_depth[2 * WINDOW * number : 2 * WINDOW * (number + 1)]
+                rows.append(jnp.sum(part * weight, axis=0, keepdims=True))
         read = jnp.concatenate(rows, axis=0)
         pieces = jnp.concatenate(parts_of(read), axis=0)
         for block in range(members):
@@ -376,7 +399,7 @@
             shape((blocks, 4 * DEGREE, LANES), jnp.float32),
             shape((PLANES - 2, WINDOW, LANES), jnp.float32),
         ),
-        in_specs=[vmem] * 6 + [smem, vmem],
+        in_specs=[vmem] * 5 + [smem, vmem],
         out_specs=(vmem, vmem, vmem),
         scratch_shapes=[
             pltpu.VMEM((7, PLANES, WINDOW, LANES), jnp.float32),
@@ -578,7 +601,7 @@
     count = lax.axis_size("space")
     members = lax.axis_size("period")
     grid_planes = conductivity.shape[0] * count
-    slab, beside, far, data = pack(
+    slab, beside, data = pack(
         source, conductivity, period_shift, observed, data_weight, members
     )
 
@@ -592,14 +615,13 @@
         return lax.ppermute(values, ("space", "period"), pairs)
 
     mate = swapped(slab, lambda i: i ^ 1)
-    beside = swapped(beside, lambda i: i + 1 if i % 2 else i - 1)
-    far = swapped(far, lambda i: i - 2 if i % 2 else i + 2)
-    mate, data, late_cells = lax.optimization_barrier((mate, data, site_cells))
+    payload, data, late_cells = lax.optimization_barrier((extend(beside, mate), data, site_cells))
+    beside = swapped(payload, lambda i: i + 1 if i % 2 else i - 1)
+    places, *lists = stations(late_cells, site_weights, grid_rows, members)
     data = lax.all_to_all(data, "period", 0, 0, tiled=True)
-    places, *lists = stations(late_cells, site_weights, grid_rows, members)
-    beside, far, places = lax.optimization_barrier((beside, far, places))
+    beside, data, places = lax.optimization_barrier((beside, data, places))
     station_parts = (places, *lists)
-    windows = (slab, mate, beside, far, swapped(beside, lambda i: i ^ 1))
+    windows = (slab, mate, beside, swapped(beside, lambda i: i ^ 1))
     field, sent, mass = forward_solve(windows, station_parts, grid_rows, members, grid_planes)
     sent, data = lax.optimization_barrier((sent, data))
     read = lax.all_to_all(sent, "space", 0, 0, tiled=True)

time: 76.3 us -> 73.3 us (0.961)
  starting transfers between devices: 25.4 us -> 17.7 us
  waiting for transfers between devices: 6.38 us -> 11.1 us
    ppermute x4 -> x3, starting transfers between devices: 10.3 us -> 2.42 us  [swapped(): return lax.ppermute(values, ('space', 'period'), pairs)]
    all_to_all x1, waiting for transfers between devices: 4.53 us -> 7.22 us  [shards(): data = lax.all_to_all(data, 'period', 0, 0, tiled=True)]
    ppermute x4 -> x3, waiting for transfers between devices: 0.88 us -> 2.87 us  [swapped(): return lax.ppermute(values, ('space', 'period'), pairs)]
  transfers between devices with their start and end apart: 6 -> 5, of which waited for: 3 -> 4; matrix products, arithmetic and copies ran while one was open for 0% -> 0% of each run, Pallas kernels for 16% -> 11%
where the time goes in v8:
time: 73.3 us; the launch traced here: 72.6 us
  blocking collectives  27.5 us (38%)
  starting transfers between devices  17.7 us (24%)
  Pallas kernels  14.3 us (20%)
  waiting for transfers between devices  11.1 us (15%)
  between operations  1.36 us (2%)
    all_to_all x1, blocking collectives, shards(): read = lax.all_to_all(sent, 'space', 0, 0, tiled=True)  15.4 us
    all_to_all x1, blocking collectives, shards(): moments = lax.all_to_all(moments, 'space', 0, 0, tiled=True)  12.1 us
    all_to_all x1, starting transfers between devices, shards(): data = lax.all_to_all(data, 'period', 0, 0, tiled=True)  9.97 us
    all_to_all x1, waiting for transfers between devices, shards(): data = lax.all_to_all(data, 'period', 0, 0, tiled=True)  7.22 us
    pallas_call x1, Pallas kernels, adjoint_solve(): pl.pallas_call(lambda *refs: adjoint_kernel(grid_rows, own_rows, grid_pla...  6.51 us
    all_to_all x1, starting transfers between devices, shards(): owned = lax.all_to_all(owned, 'period', 0, 0, tiled=True)  5.35 us
    pallas_call x1, Pallas kernels, forward_solve(): pl.pallas_call(lambda *refs: forward_kernel(grid_rows, grid_rows // membe...  3.88 us
    ppermute x3, waiting for transfers between devices, swapped(): return lax.ppermute(values, ('space', 'period'), pairs)  2.87 us
  transfers between devices with their start and end apart: 5, of which 4 were waited for; matrix products, arithmetic and copies ran while one was open for 0% of the time, Pallas kernels for 11%

profile of v8, /device:TPU:2, one launch (start us, length us, event | category | flops | bytes accessed | tf_op | source)
XLA Modules:
  0.0 72.6 jit_solution(9410568623868914187)
XLA Ops:
  0.6 0.0 copy-start
  0.6 0.0 copy-start.1
  1.3 1.9 %pack.1 = (f32[10,2,32,128]{3,2,1,0:T(8,128)S(1)}, f32[7,2,32,128]{3,2,1,0:T(8,128)S(1)}, f32[16,16,128]{2,1,0:T(8,128)}) custom-call(f32[2,3,2,256,128]{4,3,2,1,0:T(8,128)} %refs_0_.1, f32[2,256,128]{2,1,0:T(8,128)} %refs_1_.2, f32[1]{0:T(128)S(6)} %copy.9.refs_2_, f32[1,4,128]{2,1,0:T(4,128)} %refs_3_.1, f32[1,4,128]{2,1,0:T(4,128)} %refs_4_.1), custom_call_target="tpu_custom_call" | custom-call | tf_op jit(solution)/shard_map/pack/pallas_call | solution.py:160
  3.2 0.1 collective-permute-start
  3.3 1.6 %collective-permute-done.mate.refs_1_ = f32[10,2,32,128]{3,2,1,0:T(8,128)S(1)} collective-permute-done((f32[10,2,32,128]{3,2,1,0:T(8,128)S(1)}, f32[10,2,32,128]{3,2,1,0:T(8,128)S(1)}, u32[]{:S(2)}, u32[]{:S(2)}) %collective-permute-start) | collective-permute-done | bytes 327712 | tf_op jit(solution)/shard_map/ppermute | solution.py:615
  5.0 0.7 collective-permute-start.1
  5.7 10.0 %all-to-all-start = ((f32[16,16,128]{2,1,0:T(8,128)}), f32[16,16,128]{2,1,0:T(8,128)S(1)}, u32[]{:S(2)}, u32[]{:S(2)}) async-start(f32[16,16,128]{2,1,0:T(8,128)} %get-tuple-element.27), calls=%async_computation | async-start | bytes 262144 | tf_op jit(solution)/shard_map/all_to_all | solution.py:621
  15.6 0.0 copy-done
  15.6 0.0 copy-done.1
  15.7 1.3 %stations.1 = (s32[16,128]{1,0:T(8,128)S(1)}, s32[1]{0:T(128)}, f32[16,32,128]{2,1,0:T(8,128)S(1)}) custom-call(s32[4,2048]{1,0:T(4,128)S(1)} %copy-done, f32[4,2048]{1,0:T(4,128)S(1)} %copy-done.1), custom_call_target="tpu_custom_call" | custom-call | flops 10000000 | bytes 200000 | tf_op jit(solution)/shard_map/stations/pallas_call | solution.py:254
  16.9 7.2 %all-to-all-done.refs_1_ = f32[16,16,128]{2,1,0:T(8,128)S(1)} async-done(((f32[16,16,128]{2,1,0:T(8,128)}), f32[16,16,128]{2,1,0:T(8,128)S(1)}, u32[]{:S(2)}, u32[]{:S(2)}) %all-to-all-start) | async-done | bytes 131104 | tf_op jit(solution)/shard_map/all_to_all | solution.py:621
  24.2 0.0 collective-permute-done.1.refs_2_
  24.2 1.6 %collective-permute-start.2 = (f32[10,2,32,128]{3,2,1,0:T(8,128)S(1)}, f32[10,2,32,128]{3,2,1,0:T(8,128)S(1)}, u32[]{:S(2)}, u32[]{:S(2)}) collective-permute-start(f32[10,2,32,128]{3,2,1,0:T(8,128)S(1)} %collective-permute-done.1.refs_2_), channel_id=1, source_target_pairs={{0,16},{1,17},{2,18},{3,19},{4,20},{5,21},{6,22},{7,23},{8,24},{9,... | collective-permute-start | bytes 983048 | tf_op jit(solution)/shard_map/ppermute | solution.py:615
  25.8 1.3 %collective-permute-done.2.refs_3_ = f32[10,2,32,128]{3,2,1,0:T(8,128)S(1)} collective-permute-done((f32[10,2,32,128]{3,2,1,0:T(8,128)S(1)}, f32[10,2,32,128]{3,2,1,0:T(8,128)S(1)}, u32[]{:S(2)}, u32[]{:S(2)}) %collective-permute-start.2) | collective-permute-done | bytes 327712 | tf_op jit(solution)/shard_map/ppermute | solution.py:615
  27.1 3.9 %forward_solve.1 = (f32[4,2,3,2,32,128]{5,4,3,2,1,0:T(8,128)S(1)}, f32[16,16,128]{2,1,0:T(8,128)S(1)}, f32[6,32,128]{2,1,0:T(8,128)S(1)}) custom-call(f32[10,2,32,128]{3,2,1,0:T(8,128)S(1)} %get-tuple-element.23.refs_0_, f32[10,2,32,128]{3,2,1,0:T(8,128)S(1)} %collective-permute-done.mate.refs_1_, f32[10,2,32,128]{3,2,1,0:T(8,128)S(1)} %collective-permute-done.1.refs_2_, ...), custom_call_target="tpu_custom_call" | custom-call | flops 20000000000 | bytes 3000000 | tf_op jit(solution)/shard_map/forward_solve/pallas_call | solution.py:395
  31.0 15.4 %all_to_all.20.refs_0_ = f32[16,16,128]{2,1,0:T(8,128)S(1)} all-to-all(f32[16,16,128]{2,1,0:T(8,128)S(1)} %get-tuple-element.36), channel_id=1, replica_groups=mesh['space'=16,'period'=16] {'space'}, dimensions={0} | all-to-all | bytes 262144 | tf_op jit(solution)/shard_map/all_to_all | solution.py:627
  46.4 0.7 residuals.1
  47.1 12.1 %all_to_all.21.refs_0_ = f32[16,32,128]{2,1,0:T(8,128)S(1)} all-to-all(f32[16,32,128]{2,1,0:T(8,128)S(1)} %get-tuple-element.38), channel_id=1, replica_groups=mesh['space'=16,'period'=16] {'space'}, dimensions={0} | all-to-all | bytes 524288 | tf_op jit(solution)/shard_map/all_to_all | solution.py:629
  59.2 5.3 %all-to-all-start.3 = ((f32[16,4,128]{2,1,0:T(4,128)}), f32[16,4,128]{2,1,0:T(4,128)S(1)}, u32[]{:S(2)}, u32[]{:S(2)}) async-start(f32[16,4,128]{2,1,0:T(4,128)} %get-tuple-element.40), calls=%async_computation.3 | async-start | bytes 65536 | tf_op jit(solution)/shard_map/all_to_all | solution.py:631
  64.5 6.5 %adjoint_solve.1 = f32[2,16,128]{2,1,0:T(8,128)} custom-call(f32[16,32,128]{2,1,0:T(8,128)S(1)} %all_to_all.21.refs_0_, s32[16,128]{1,0:T(8,128)S(1)} %get-tuple-element.31.refs_4_.refs_1_, s32[1]{0:T(128)} %get-tuple-element.32.refs_5_.refs_2_, f32[16,32,128]{2,1,0:T(8,128)S(1)} %get-tuple-element.33.refs_6_.refs_3_, ...), custom_call_target="tpu_custom_call" | custom-call | flops 200000000 | bytes 3000000 | tf_op jit(solution)/shard_map/adjoint_solve/pallas_call | solution.py:580
  71.1 1.0 %all-to-all-done.3 = f32[16,4,128]{2,1,0:T(4,128)S(1)} async-done(((f32[16,4,128]{2,1,0:T(4,128)}), f32[16,4,128]{2,1,0:T(4,128)S(1)}, u32[]{:S(2)}, u32[]{:S(2)}) %all-to-all-start.3) | async-done | bytes 32800 | tf_op jit(solution)/shard_map/all_to_all | solution.py:631
  72.0 0.6 reduce_sum.9
  (1 shorter events, 0.0 us)
Async XLA Ops:
  0.6 15.0 %copy-start = (s32[4,2048]{1,0:T(4,128)S(1)}, s32[4,2048]{1,0:T(4,128)}, u32[]{:S(2)}) copy-start(s32[4,2048]{1,0:T(4,128)} %refs_2_.2) | copy-start | bytes 98308
  0.6 15.0 %copy-start.1 = (f32[4,2048]{1,0:T(4,128)S(1)}, f32[4,2048]{1,0:T(4,128)}, u32[]{:S(2)}) copy-start(f32[4,2048]{1,0:T(4,128)} %refs_1_.3) | copy-start | bytes 98308
  3.2 1.7 %collective-permute-start = (f32[10,2,32,128]{3,2,1,0:T(8,128)S(1)}, f32[10,2,32,128]{3,2,1,0:T(8,128)S(1)}, u32[]{:S(2)}, u32[]{:S(2)}) collective-permute-start(f32[10,2,32,128]{3,2,1,0:T(8,128)S(1)} %get-tuple-element.23.refs_0_), channel_id=1, source_target_pairs={{0,16},{1,17},{2,18},{3,19},{4,20},{5,21},{6,22},{7,23},{8,24},{9,... | collective-permute-start | bytes 983048 | tf_op jit(solution)/shard_map/ppermute | solution.py:615
  5.0 19.2 %collective-permute-start.1 = (f32[10,2,32,128]{3,2,1,0:T(8,128)S(1)}, f32[10,2,32,128]{3,2,1,0:T(8,128)S(1)}, u32[]{:S(2)}, u32[]{:S(2)}) collective-permute-start(f32[10,2,32,128]{3,2,1,0:T(8,128)S(1)} %extend.1), channel_id=1, source_target_pairs={{16,33},{17,32},{18,35},{19,34},{20,37},{21,36},{22,39},{23,38},{2... | collective-permute-start | bytes 983048 | tf_op jit(solution)/shard_map/ppermute | solution.py:615
  5.7 18.5 %all-to-all-start = ((f32[16,16,128]{2,1,0:T(8,128)}), f32[16,16,128]{2,1,0:T(8,128)S(1)}, u32[]{:S(2)}, u32[]{:S(2)}) async-start(f32[16,16,128]{2,1,0:T(8,128)} %get-tuple-element.27), calls=%async_computation | async-start | bytes 262144 | tf_op jit(solution)/shard_map/all_to_all | solution.py:621
  24.2 2.9 %collective-permute-start.2 = (f32[10,2,32,128]{3,2,1,0:T(8,128)S(1)}, f32[10,2,32,128]{3,2,1,0:T(8,128)S(1)}, u32[]{:S(2)}, u32[]{:S(2)}) collective-permute-start(f32[10,2,32,128]{3,2,1,0:T(8,128)S(1)} %collective-permute-done.1.refs_2_), channel_id=1, source_target_pairs={{0,16},{1,17},{2,18},{3,19},{4,20},{5,21},{6,22},{7,23},{8,24},{9,... | collective-permute-start | bytes 983048 | tf_op jit(solution)/shard_map/ppermute | solution.py:615
  59.2 12.8 %all-to-all-start.3 = ((f32[16,4,128]{2,1,0:T(4,128)}), f32[16,4,128]{2,1,0:T(4,128)S(1)}, u32[]{:S(2)}, u32[]{:S(2)}) async-start(f32[16,4,128]{2,1,0:T(4,128)} %get-tuple-element.40), calls=%async_computation.3 | async-start | bytes 65536 | tf_op jit(solution)/shard_map/all_to_all | solution.py:631

commit v9 on v6

--- a/solution.py
+++ b/solution.py
@@ -142,12 +142,14 @@
     started = [pltpu.make_async_copy(a, b, sems.at[i]) for i, (a, b) in enumerate(copies)]
     for copy in started:
         copy.start()
-    for copy in started:
+    for copy in started[:2]:
         copy.wait()
     for member in range(data.shape[0]):
         data[member, 0:4, :] = pairs[0]
         data[member, 4:8, :] = pairs[1]
         data[member, 8:16, :] = jnp.full((8, LANES), shift[0], jnp.float32)
+    for copy in started[2:]:
+        copy.wait()
 
 
 def pack(source, conductivity, shift, observed, weight, members):
@@ -350,12 +352,13 @@
         weight = row_weights(feature, 0, HALO * WINDOW, 2 * WINDOW)
         depth = depth_picks(feature)
         rows = []
+        stacked = jnp.concatenate([depth] * 3, axis=0)
         for j in range(DEGREE):
-            for pol in range(2):
-                for c in range(2):
-                    values = field[j, pol, c].reshape(2 * WINDOW, LANES)
-                    at_depth = sum(dot_nn(piece, depth) for piece in parts_of(values))
-                    rows.append(jnp.sum(at_depth * weight, axis=0, keepdims=True))
+            values = field[j, :, 0:2].reshape(8 * WINDOW, LANES)
+            at_depth = dot_nn(jnp.concatenate(parts_of(values), axis=1), stacked)
+            for number in range(4):
+                part = at_depth[2 * WINDOW * number : 2 * WINDOW * (number + 1)]
+                rows.append(jnp.sum(part * weight, axis=0, keepdims=True))
         read = jnp.concatenate(rows, axis=0)
         pieces = jnp.concatenate(parts_of(read), axis=0)
         for block in range(members):

time: 71.2 us -> 71.2 us (level)
  no operation moved by 1% of the time
where the time goes in v9:
time: 71.2 us; the launch traced here: 70.4 us
  blocking collectives  28.7 us (40%)
  starting transfers between devices  20.3 us (29%)
  Pallas kernels  14.3 us (20%)
  waiting for transfers between devices  5.11 us (7%)
  between operations  1.4 us (2%)
    all_to_all x1, blocking collectives, shards(): read = lax.all_to_all(sent, 'space', 0, 0, tiled=True)  16.6 us
    all_to_all x1, blocking collectives, shards(): moments = lax.all_to_all(moments, 'space', 0, 0, tiled=True)  12.1 us
    all_to_all x1, starting transfers between devices, shards(): data = lax.all_to_all(data, 'period', 0, 0, tiled=True)  10.3 us
    pallas_call x1, Pallas kernels, adjoint_solve(): pl.pallas_call(lambda *refs: adjoint_kernel(grid_rows, own_rows, grid_pla...  6.52 us
    all_to_all x1, starting transfers between devices, shards(): owned = lax.all_to_all(owned, 'period', 0, 0, tiled=True)  5.16 us
    ppermute x4, starting transfers between devices, swapped(): return lax.ppermute(values, ('space', 'period'), pairs)  4.86 us
    all_to_all x1, waiting for transfers between devices, shards(): data = lax.all_to_all(data, 'period', 0, 0, tiled=True)  4.13 us
    pallas_call x1, Pallas kernels, forward_solve(): pl.pallas_call(lambda *refs: forward_kernel(grid_rows, grid_rows // membe...  3.87 us
  transfers between devices with their start and end apart: 6, of which 2 were waited for; matrix products, arithmetic and copies ran while one was open for 0% of the time, Pallas kernels for 17%

profile of v9, /device:TPU:2, one launch (start us, length us, event | category | flops | bytes accessed | tf_op | source)
XLA Modules:
  0.0 70.4 jit_solution(15621208585238872155)
XLA Ops:
  0.6 0.0 copy-start
  0.6 0.0 copy-start.1
  1.3 1.9 %pack.1 = (f32[7,2,32,128]{3,2,1,0:T(8,128)S(1)}, f32[7,2,32,128]{3,2,1,0:T(8,128)S(1)}, f32[6,32,128]{2,1,0:T(8,128)S(1)}, f32[6,32,128]{2,1,0:T(8,128)S(1)}, f32[16,16,128]{2,1,0:T(8,128)}) custom-call(f32[2,3,2,256,128]{4,3,2,1,0:T(8,128)} %refs_0_.1, f32[2,256,128]{2,1,0:T(8,128)} %refs_1_.2, f32[1]{0:T(128)S(6)} %copy.9.refs_2_, f32[1,4,128]{2,1,0:T(4,128)} %refs_3_.1, ...), custom_call_target="tpu_custom_call" | custom-call | tf_op jit(solution)/shard_map/pack/pallas_call | solution.py:161
  3.2 0.1 collective-permute-start
  3.3 0.7 collective-permute-start.1
  4.0 3.4 %collective-permute-start.2 = (f32[6,32,128]{2,1,0:T(8,128)S(1)}, f32[6,32,128]{2,1,0:T(8,128)S(1)}, u32[]{:S(2)}, u32[]{:S(2)}) collective-permute-start(f32[6,32,128]{2,1,0:T(8,128)S(1)} %get-tuple-element.26), channel_id=1, source_target_pairs={{0,33},{1,32},{2,35},{3,34},{4,37},{5,36},{6,39},{7,38},{8,41},{9,... | collective-permute-start | bytes 294920 | tf_op jit(solution)/shard_map/ppermute | solution.py:597
  7.4 0.7 collective-permute-start.3
  8.1 0.0 collective-permute-done.refs_1_
  8.1 10.3 %all-to-all-start = ((f32[16,16,128]{2,1,0:T(8,128)}), f32[16,16,128]{2,1,0:T(8,128)S(1)}, u32[]{:S(2)}, u32[]{:S(2)}) async-start(f32[16,16,128]{2,1,0:T(8,128)} %get-tuple-element.33), calls=%async_computation | async-start | bytes 262144 | tf_op jit(solution)/shard_map/all_to_all | solution.py:608
  18.4 0.0 copy-done
  18.4 0.0 copy-done.1
  18.4 1.3 %stations.1 = (s32[16,128]{1,0:T(8,128)S(1)}, s32[1]{0:T(128)}, f32[16,32,128]{2,1,0:T(8,128)S(1)}) custom-call(s32[4,2048]{1,0:T(4,128)S(1)} %copy-done, f32[4,2048]{1,0:T(4,128)S(1)} %copy-done.1), custom_call_target="tpu_custom_call" | custom-call | flops 10000000 | bytes 200000 | tf_op jit(solution)/shard_map/stations/pallas_call | solution.py:236
  19.7 0.0 collective-permute-done.2.refs_3_
  19.7 0.0 collective-permute-done.3.refs_4_
  19.7 0.0 collective-permute-done.1.refs_2_
  19.8 3.9 %forward_solve.1 = (f32[4,2,3,2,32,128]{5,4,3,2,1,0:T(8,128)S(1)}, f32[16,16,128]{2,1,0:T(8,128)S(1)}, f32[6,32,128]{2,1,0:T(8,128)S(1)}) custom-call(f32[7,2,32,128]{3,2,1,0:T(8,128)S(1)} %get-tuple-element.22.refs_0_, f32[7,2,32,128]{3,2,1,0:T(8,128)S(1)} %collective-permute-done.refs_1_, f32[7,2,32,128]{3,2,1,0:T(8,128)S(1)} %collective-permute-done.1.refs_2_, ...), custom_call_target="tpu_custom_call" | custom-call | flops 20000000000 | bytes 3000000 | tf_op jit(solution)/shard_map/forward_solve/pallas_call | solution.py:377
  23.6 4.1 %all-to-all-done.refs_1_ = f32[16,16,128]{2,1,0:T(8,128)S(1)} async-done(((f32[16,16,128]{2,1,0:T(8,128)}), f32[16,16,128]{2,1,0:T(8,128)S(1)}, u32[]{:S(2)}, u32[]{:S(2)}) %all-to-all-start) | async-done | bytes 131104 | tf_op jit(solution)/shard_map/all_to_all | solution.py:608
  27.8 16.6 %all_to_all.20.refs_0_ = f32[16,16,128]{2,1,0:T(8,128)S(1)} all-to-all(f32[16,16,128]{2,1,0:T(8,128)S(1)} %get-tuple-element.34), channel_id=1, replica_groups=mesh['space'=16,'period'=16] {'space'}, dimensions={0} | all-to-all | bytes 262144 | tf_op jit(solution)/shard_map/all_to_all | solution.py:612
  44.3 0.7 residuals.1
  45.0 12.1 %all_to_all.21.refs_0_ = f32[16,32,128]{2,1,0:T(8,128)S(1)} all-to-all(f32[16,32,128]{2,1,0:T(8,128)S(1)} %get-tuple-element.36), channel_id=1, replica_groups=mesh['space'=16,'period'=16] {'space'}, dimensions={0} | all-to-all | bytes 524288 | tf_op jit(solution)/shard_map/all_to_all | solution.py:614
  57.2 5.2 %all-to-all-start.3 = ((f32[16,4,128]{2,1,0:T(4,128)}), f32[16,4,128]{2,1,0:T(4,128)S(1)}, u32[]{:S(2)}, u32[]{:S(2)}) async-start(f32[16,4,128]{2,1,0:T(4,128)} %get-tuple-element.38), calls=%async_computation.3 | async-start | bytes 65536 | tf_op jit(solution)/shard_map/all_to_all | solution.py:616
  62.3 6.5 %adjoint_solve.1 = f32[2,16,128]{2,1,0:T(8,128)} custom-call(f32[16,32,128]{2,1,0:T(8,128)S(1)} %all_to_all.21.refs_0_, s32[16,128]{1,0:T(8,128)S(1)} %get-tuple-element.29.refs_5_.refs_1_, s32[1]{0:T(128)} %get-tuple-element.30.refs_6_.refs_2_, f32[16,32,128]{2,1,0:T(8,128)S(1)} %get-tuple-element.31.refs_7_.refs_3_, ...), custom_call_target="tpu_custom_call" | custom-call | flops 200000000 | bytes 3000000 | tf_op jit(solution)/shard_map/adjoint_solve/pallas_call | solution.py:562
  68.8 1.0 %all-to-all-done.3 = f32[16,4,128]{2,1,0:T(4,128)S(1)} async-done(((f32[16,4,128]{2,1,0:T(4,128)}), f32[16,4,128]{2,1,0:T(4,128)S(1)}, u32[]{:S(2)}, u32[]{:S(2)}) %all-to-all-start.3) | async-done | bytes 32800 | tf_op jit(solution)/shard_map/all_to_all | solution.py:616
  69.8 0.6 reduce_sum.9
Async XLA Ops:
  0.6 17.8 %copy-start = (s32[4,2048]{1,0:T(4,128)S(1)}, s32[4,2048]{1,0:T(4,128)}, u32[]{:S(2)}) copy-start(s32[4,2048]{1,0:T(4,128)} %refs_2_.2) | copy-start | bytes 98308
  0.6 17.8 %copy-start.1 = (f32[4,2048]{1,0:T(4,128)S(1)}, f32[4,2048]{1,0:T(4,128)}, u32[]{:S(2)}) copy-start(f32[4,2048]{1,0:T(4,128)} %refs_1_.3) | copy-start | bytes 98308
  3.2 4.9 %collective-permute-start = (f32[7,2,32,128]{3,2,1,0:T(8,128)S(1)}, f32[7,2,32,128]{3,2,1,0:T(8,128)S(1)}, u32[]{:S(2)}, u32[]{:S(2)}) collective-permute-start(f32[7,2,32,128]{3,2,1,0:T(8,128)S(1)} %get-tuple-element.22.refs_0_), channel_id=1, source_target_pairs={{0,16},{1,17},{2,18},{3,19},{4,20},{5,21},{6,22},{7,23},{8,24},{9,... | collective-permute-start | bytes 688136 | tf_op jit(solution)/shard_map/ppermute | solution.py:597
  3.3 16.4 %collective-permute-start.1 = (f32[7,2,32,128]{3,2,1,0:T(8,128)S(1)}, f32[7,2,32,128]{3,2,1,0:T(8,128)S(1)}, u32[]{:S(2)}, u32[]{:S(2)}) collective-permute-start(f32[7,2,32,128]{3,2,1,0:T(8,128)S(1)} %get-tuple-element.25), channel_id=1, source_target_pairs={{16,33},{17,32},{18,35},{19,34},{20,37},{21,36},{22,39},{23,38},{2... | collective-permute-start | bytes 688136 | tf_op jit(solution)/shard_map/ppermute | solution.py:597
  4.0 15.7 %collective-permute-start.2 = (f32[6,32,128]{2,1,0:T(8,128)S(1)}, f32[6,32,128]{2,1,0:T(8,128)S(1)}, u32[]{:S(2)}, u32[]{:S(2)}) collective-permute-start(f32[6,32,128]{2,1,0:T(8,128)S(1)} %get-tuple-element.26), channel_id=1, source_target_pairs={{0,33},{1,32},{2,35},{3,34},{4,37},{5,36},{6,39},{7,38},{8,41},{9,... | collective-permute-start | bytes 294920 | tf_op jit(solution)/shard_map/ppermute | solution.py:597
  7.4 12.3 %collective-permute-start.3 = (f32[6,32,128]{2,1,0:T(8,128)S(1)}, f32[6,32,128]{2,1,0:T(8,128)S(1)}, u32[]{:S(2)}, u32[]{:S(2)}) collective-permute-start(f32[6,32,128]{2,1,0:T(8,128)S(1)} %get-tuple-element.27), channel_id=1, source_target_pairs={{32,65},{33,64},{34,67},{35,66},{36,69},{37,68},{38,71},{39,70},{4... | collective-permute-start | bytes 294920 | tf_op jit(solution)/shard_map/ppermute | solution.py:597
  8.1 19.6 %all-to-all-start = ((f32[16,16,128]{2,1,0:T(8,128)}), f32[16,16,128]{2,1,0:T(8,128)S(1)}, u32[]{:S(2)}, u32[]{:S(2)}) async-start(f32[16,16,128]{2,1,0:T(8,128)} %get-tuple-element.33), calls=%async_computation | async-start | bytes 262144 | tf_op jit(solution)/shard_map/all_to_all | solution.py:608
  57.2 12.6 %all-to-all-start.3 = ((f32[16,4,128]{2,1,0:T(4,128)}), f32[16,4,128]{2,1,0:T(4,128)S(1)}, u32[]{:S(2)}, u32[]{:S(2)}) async-start(f32[16,4,128]{2,1,0:T(4,128)} %get-tuple-element.38), calls=%async_computation.3 | async-start | bytes 65536 | tf_op jit(solution)/shard_map/all_to_all | solution.py:616

commit v10 on v8

--- a/solution.py
+++ b/solution.py
@@ -617,9 +617,9 @@
     mate = swapped(slab, lambda i: i ^ 1)
     payload, data, late_cells = lax.optimization_barrier((extend(beside, mate), data, site_cells))
     beside = swapped(payload, lambda i: i + 1 if i % 2 else i - 1)
+    data = lax.all_to_all(data, "period", 0, 0, tiled=True)
     places, *lists = stations(late_cells, site_weights, grid_rows, members)
-    data = lax.all_to_all(data, "period", 0, 0, tiled=True)
-    beside, data, places = lax.optimization_barrier((beside, data, places))
+    beside, places = lax.optimization_barrier((beside, places))
     station_parts = (places, *lists)
     windows = (slab, mate, beside, swapped(beside, lambda i: i ^ 1))
     field, sent, mass = forward_solve(windows, station_parts, grid_rows, members, grid_planes)

time: 73.3 us -> 78.1 us (1.065)
  starting transfers between devices: 17.7 us -> 25.5 us
  waiting for transfers between devices: 11.1 us -> 7.31 us
  blocking collectives: 27.5 us -> 28.3 us
    ppermute x3, starting transfers between devices: 2.42 us -> 10.1 us  [swapped(): return lax.ppermute(values, ('space', 'period'), pairs)]
    all_to_all x1, waiting for transfers between devices: 7.22 us -> 4.71 us  [shards(): data = lax.all_to_all(data, 'period', 0, 0, tiled=True)]
    ppermute x3, waiting for transfers between devices: 2.87 us -> 1.62 us  [swapped(): return lax.ppermute(values, ('space', 'period'), pairs)]
  transfers between devices with their start and end apart: 5 -> 5, of which waited for: 4 -> 3; matrix products, arithmetic and copies ran while one was open for 0% -> 0% of each run, Pallas kernels for 11% -> 15%
where the time goes in v10:
time: 78.1 us; the launch traced here: 77.4 us
  blocking collectives  28.3 us (36%)
  starting transfers between devices  25.5 us (33%)
  Pallas kernels  14.3 us (18%)
  waiting for transfers between devices  7.31 us (9%)
  between operations  1.38 us (2%)
    all_to_all x1, blocking collectives, shards(): read = lax.all_to_all(sent, 'space', 0, 0, tiled=True)  16.1 us
    all_to_all x1, blocking collectives, shards(): moments = lax.all_to_all(moments, 'space', 0, 0, tiled=True)  12.1 us
    all_to_all x1, starting transfers between devices, shards(): data = lax.all_to_all(data, 'period', 0, 0, tiled=True)  10.2 us
    ppermute x3, starting transfers between devices, swapped(): return lax.ppermute(values, ('space', 'period'), pairs)  10.1 us
    pallas_call x1, Pallas kernels, adjoint_solve(): pl.pallas_call(lambda *refs: adjoint_kernel(grid_rows, own_rows, grid_pla...  6.51 us
    all_to_all x1, starting transfers between devices, shards(): owned = lax.all_to_all(owned, 'period', 0, 0, tiled=True)  5.14 us
    all_to_all x1, waiting for transfers between devices, shards(): data = lax.all_to_all(data, 'period', 0, 0, tiled=True)  4.71 us
    pallas_call x1, Pallas kernels, forward_solve(): pl.pallas_call(lambda *refs: forward_kernel(grid_rows, grid_rows // membe...  3.88 us
  transfers between devices with their start and end apart: 5, of which 3 were waited for; matrix products, arithmetic and copies ran while one was open for 0% of the time, Pallas kernels for 15%

profile of v10, /device:TPU:2, one launch (start us, length us, event | category | flops | bytes accessed | tf_op | source)
XLA Modules:
  0.0 77.4 jit_solution(15252198853874775381)
XLA Ops:
  0.6 0.0 copy-start
  0.6 0.0 copy-start.1
  1.3 1.9 %pack.1 = (f32[10,2,32,128]{3,2,1,0:T(8,128)S(1)}, f32[7,2,32,128]{3,2,1,0:T(8,128)S(1)}, f32[16,16,128]{2,1,0:T(8,128)}) custom-call(f32[2,3,2,256,128]{4,3,2,1,0:T(8,128)} %refs_0_.1, f32[2,256,128]{2,1,0:T(8,128)} %refs_1_.2, f32[1]{0:T(128)S(6)} %copy.9.refs_2_, f32[1,4,128]{2,1,0:T(4,128)} %refs_3_.1, f32[1,4,128]{2,1,0:T(4,128)} %refs_4_.1), custom_call_target="tpu_custom_call" | custom-call | tf_op jit(solution)/shard_map/pack/pallas_call | solution.py:160
  3.2 0.1 collective-permute-start
  3.3 1.6 %collective-permute-done.mate.refs_1_ = f32[10,2,32,128]{3,2,1,0:T(8,128)S(1)} collective-permute-done((f32[10,2,32,128]{3,2,1,0:T(8,128)S(1)}, f32[10,2,32,128]{3,2,1,0:T(8,128)S(1)}, u32[]{:S(2)}, u32[]{:S(2)}) %collective-permute-start) | collective-permute-done | bytes 327712 | tf_op jit(solution)/shard_map/ppermute | solution.py:615
  5.0 0.7 collective-permute-start.1
  5.7 0.0 copy-done
  5.7 0.0 copy-done.1
  5.7 1.3 %stations.1 = (s32[16,128]{1,0:T(8,128)S(1)}, s32[1]{0:T(128)}, f32[16,32,128]{2,1,0:T(8,128)S(1)}) custom-call(s32[4,2048]{1,0:T(4,128)S(1)} %copy-done, f32[4,2048]{1,0:T(4,128)S(1)} %copy-done.1), custom_call_target="tpu_custom_call" | custom-call | flops 10000000 | bytes 200000 | tf_op jit(solution)/shard_map/stations/pallas_call | solution.py:254
  7.0 0.0 collective-permute-done.1.refs_2_
  7.0 9.4 %collective-permute-start.2 = (f32[10,2,32,128]{3,2,1,0:T(8,128)S(1)}, f32[10,2,32,128]{3,2,1,0:T(8,128)S(1)}, u32[]{:S(2)}, u32[]{:S(2)}) collective-permute-start(f32[10,2,32,128]{3,2,1,0:T(8,128)S(1)} %collective-permute-done.1.refs_2_), channel_id=1, source_target_pairs={{0,16},{1,17},{2,18},{3,19},{4,20},{5,21},{6,22},{7,23},{8,24},{9,... | collective-permute-start | bytes 983048 | tf_op jit(solution)/shard_map/ppermute | solution.py:615
  16.4 10.2 %all-to-all-start = ((f32[16,16,128]{2,1,0:T(8,128)}), f32[16,16,128]{2,1,0:T(8,128)S(1)}, u32[]{:S(2)}, u32[]{:S(2)}) async-start(f32[16,16,128]{2,1,0:T(8,128)} %get-tuple-element.33), calls=%async_computation | async-start | bytes 262144 | tf_op jit(solution)/shard_map/all_to_all | solution.py:620
  26.6 0.0 collective-permute-done.2.refs_3_
  26.6 3.9 %forward_solve.1 = (f32[4,2,3,2,32,128]{5,4,3,2,1,0:T(8,128)S(1)}, f32[16,16,128]{2,1,0:T(8,128)S(1)}, f32[6,32,128]{2,1,0:T(8,128)S(1)}) custom-call(f32[10,2,32,128]{3,2,1,0:T(8,128)S(1)} %get-tuple-element.22.refs_0_, f32[10,2,32,128]{3,2,1,0:T(8,128)S(1)} %collective-permute-done.mate.refs_1_, f32[10,2,32,128]{3,2,1,0:T(8,128)S(1)} %collective-permute-done.1.refs_2_, ...), custom_call_target="tpu_custom_call" | custom-call | flops 20000000000 | bytes 3000000 | tf_op jit(solution)/shard_map/forward_solve/pallas_call | solution.py:395
  30.5 4.7 %all-to-all-done.refs_1_ = f32[16,16,128]{2,1,0:T(8,128)S(1)} async-done(((f32[16,16,128]{2,1,0:T(8,128)}), f32[16,16,128]{2,1,0:T(8,128)S(1)}, u32[]{:S(2)}, u32[]{:S(2)}) %all-to-all-start) | async-done | bytes 131104 | tf_op jit(solution)/shard_map/all_to_all | solution.py:620
  35.2 16.1 %all_to_all.20.refs_0_ = f32[16,16,128]{2,1,0:T(8,128)S(1)} all-to-all(f32[16,16,128]{2,1,0:T(8,128)S(1)} %get-tuple-element.34), channel_id=1, replica_groups=mesh['space'=16,'period'=16] {'space'}, dimensions={0} | all-to-all | bytes 262144 | tf_op jit(solution)/shard_map/all_to_all | solution.py:627
  51.3 0.7 residuals.1
  52.0 12.1 %all_to_all.21.refs_0_ = f32[16,32,128]{2,1,0:T(8,128)S(1)} all-to-all(f32[16,32,128]{2,1,0:T(8,128)S(1)} %get-tuple-element.36), channel_id=1, replica_groups=mesh['space'=16,'period'=16] {'space'}, dimensions={0} | all-to-all | bytes 524288 | tf_op jit(solution)/shard_map/all_to_all | solution.py:629
  64.2 5.1 %all-to-all-start.3 = ((f32[16,4,128]{2,1,0:T(4,128)}), f32[16,4,128]{2,1,0:T(4,128)S(1)}, u32[]{:S(2)}, u32[]{:S(2)}) async-start(f32[16,4,128]{2,1,0:T(4,128)} %get-tuple-element.38), calls=%async_computation.3 | async-start | bytes 65536 | tf_op jit(solution)/shard_map/all_to_all | solution.py:631
  69.3 6.5 %adjoint_solve.1 = f32[2,16,128]{2,1,0:T(8,128)} custom-call(f32[16,32,128]{2,1,0:T(8,128)S(1)} %all_to_all.21.refs_0_, s32[16,128]{1,0:T(8,128)S(1)} %get-tuple-element.29.refs_4_.refs_1_, s32[1]{0:T(128)} %get-tuple-element.30.refs_5_.refs_2_, f32[16,32,128]{2,1,0:T(8,128)S(1)} %get-tuple-element.31.refs_6_.refs_3_, ...), custom_call_target="tpu_custom_call" | custom-call | flops 200000000 | bytes 3000000 | tf_op jit(solution)/shard_map/adjoint_solve/pallas_call | solution.py:580
  75.8 1.0 %all-to-all-done.3 = f32[16,4,128]{2,1,0:T(4,128)S(1)} async-done(((f32[16,4,128]{2,1,0:T(4,128)}), f32[16,4,128]{2,1,0:T(4,128)S(1)}, u32[]{:S(2)}, u32[]{:S(2)}) %all-to-all-start.3) | async-done | bytes 32800 | tf_op jit(solution)/shard_map/all_to_all | solution.py:631
  76.8 0.6 reduce_sum.9
  (1 shorter events, 0.0 us)
Async XLA Ops:
  0.6 5.0 %copy-start = (s32[4,2048]{1,0:T(4,128)S(1)}, s32[4,2048]{1,0:T(4,128)}, u32[]{:S(2)}) copy-start(s32[4,2048]{1,0:T(4,128)} %refs_2_.2) | copy-start | bytes 98308
  0.6 5.0 %copy-start.1 = (f32[4,2048]{1,0:T(4,128)S(1)}, f32[4,2048]{1,0:T(4,128)}, u32[]{:S(2)}) copy-start(f32[4,2048]{1,0:T(4,128)} %refs_1_.3) | copy-start | bytes 98308
  3.2 1.7 %collective-permute-start = (f32[10,2,32,128]{3,2,1,0:T(8,128)S(1)}, f32[10,2,32,128]{3,2,1,0:T(8,128)S(1)}, u32[]{:S(2)}, u32[]{:S(2)}) collective-permute-start(f32[10,2,32,128]{3,2,1,0:T(8,128)S(1)} %get-tuple-element.22.refs_0_), channel_id=1, source_target_pairs={{0,16},{1,17},{2,18},{3,19},{4,20},{5,21},{6,22},{7,23},{8,24},{9,... | collective-permute-start | bytes 983048 | tf_op jit(solution)/shard_map/ppermute | solution.py:615
  5.0 2.0 %collective-permute-start.1 = (f32[10,2,32,128]{3,2,1,0:T(8,128)S(1)}, f32[10,2,32,128]{3,2,1,0:T(8,128)S(1)}, u32[]{:S(2)}, u32[]{:S(2)}) collective-permute-start(f32[10,2,32,128]{3,2,1,0:T(8,128)S(1)} %extend.1), channel_id=1, source_target_pairs={{16,33},{17,32},{18,35},{19,34},{20,37},{21,36},{22,39},{23,38},{2... | collective-permute-start | bytes 983048 | tf_op jit(solution)/shard_map/ppermute | solution.py:615
  7.0 19.6 %collective-permute-start.2 = (f32[10,2,32,128]{3,2,1,0:T(8,128)S(1)}, f32[10,2,32,128]{3,2,1,0:T(8,128)S(1)}, u32[]{:S(2)}, u32[]{:S(2)}) collective-permute-start(f32[10,2,32,128]{3,2,1,0:T(8,128)S(1)} %collective-permute-done.1.refs_2_), channel_id=1, source_target_pairs={{0,16},{1,17},{2,18},{3,19},{4,20},{5,21},{6,22},{7,23},{8,24},{9,... | collective-permute-start | bytes 983048 | tf_op jit(solution)/shard_map/ppermute | solution.py:615
  16.4 18.8 %all-to-all-start = ((f32[16,16,128]{2,1,0:T(8,128)}), f32[16,16,128]{2,1,0:T(8,128)S(1)}, u32[]{:S(2)}, u32[]{:S(2)}) async-start(f32[16,16,128]{2,1,0:T(8,128)} %get-tuple-element.33), calls=%async_computation | async-start | bytes 262144 | tf_op jit(solution)/shard_map/all_to_all | solution.py:620
  64.2 12.6 %all-to-all-start.3 = ((f32[16,4,128]{2,1,0:T(4,128)}), f32[16,4,128]{2,1,0:T(4,128)S(1)}, u32[]{:S(2)}, u32[]{:S(2)}) async-start(f32[16,4,128]{2,1,0:T(4,128)} %get-tuple-element.38), calls=%async_computation.3 | async-start | bytes 65536 | tf_op jit(solution)/shard_map/all_to_all | solution.py:631
